TPU v7x, 256 devices: a whole 4x4x8 slice. The times are simulated.
256 devices in a mesh: seq: 64 (over y, z, x_hi), head: 4 (over x_lo, core).
Axes of the slice: x: 4 (x_hi: 2, x_lo: 2; x = x_hi * 2 + x_lo), y: 4, z: 8, core: 2. Of those that a mesh axis runs over, the one named last changes fastest.
Arguments:
- text_rows: bfloat16 [32768, 8192], P('seq', 'head'), may hold values from -12 to 12
- text_gain: bfloat16 [8192], P('head'), may hold values from 0.5 to 4
- query_weight: bfloat16 [8192, 4096], P('seq', 'head'), may hold values from -0.0625 to 0.0625
- key_weight: bfloat16 [1280, 4096], P('seq', 'head'), may hold values from -0.15625 to 0.15625
- value_weight: bfloat16 [1280, 4096], P('seq', 'head'), may hold values from -0.15625 to 0.15625
- images: bfloat16 [128, 256, 1280], P('seq'), may hold values from -6 to 6
- patch_counts: int32 [128], P('seq'), may hold values from 64 to 256, as said below
- image_counts: int32 [64], P('seq'), may hold values from 0 to 2, as said below
- image_spans: int32 [2, 128], P(None, 'seq'), may hold values from 0 to 32768, as said below
- latents: bfloat16 [64, 1280], replicated, may hold values from -6 to 6
- latent_gain: bfloat16 [1280], replicated, may hold values from 0.5 to 4
- context_gain: bfloat16 [1280], replicated, may hold values from 0.5 to 4
- final_gain: bfloat16 [1280], replicated, may hold values from 0.5 to 4
- res_query: bfloat16 [1280, 1536], P(None, 'head'), may hold values from -0.15625 to 0.15625
- res_key: bfloat16 [1280, 1536], P(None, 'head'), may hold values from -0.15625 to 0.15625
- res_value: bfloat16 [1280, 1536], P(None, 'head'), may hold values from -0.15625 to 0.15625
- res_output: bfloat16 [1536, 1280], P('head'), may hold values from -0.15625 to 0.15625
Outputs:
- attended: bfloat16 [32768, 4096], P('seq', 'head')
Inputs may be any that keep to these rules, and one draw needn't show every extreme that they name: `image_spans`: row 0 holds span starts, row 1 span ends. For live slots (see image_counts) a span starts inside its owner shard's 512 tokens, is nonempty, ends no later than 1024 tokens after its start, and live spans are disjoint; some span reaches tokens of the shard 2 after its owner. Bounds of slots that are not live carry no meaning. `image_counts`: images owned by each seq shard, its live slots being the first ones; some shard owns 2. `patch_counts`: patches past the count are padding; every shard has a slot with 256 and a slot with 64 live patches.
All inputs are finite; a program needn't handle non-finite values.
Results may differ from a plain program's by a relative error of at most 0.024.
The roundings to bfloat16 on the way count: a program that leaves them out, or rounds other values in their place, can miss the bound.
Values may be sent and summed in bfloat16 or wider, within the bound.
No kernel may reach another device: no remote copies, remote signals or barrier semaphores. Data moves between devices by JAX's collectives and lax.ppermute only.
A program may use at most 128 MiB of HBM per device.

v0:
```python
import jax
import jax.numpy as jnp
from jax import lax
from jax.sharding import PartitionSpec as P

D = 8192
HD = 128
RHD = 96
LAT = 64
PATCH = 256
REACH = 2


EPS_TEXT = 1e-06
EPS_VISION = 1e-05
FILL = -1e30


def shifted(x, axis, by):
    count = lax.axis_size(axis)
    pairs = [(i, i + by) for i in range(count) if 0 <= i + by < count]
    return lax.ppermute(x, axis, pairs)


def layer_norm(values, gain):
    middle = jnp.mean(values, axis=-1, keepdims=True)
    centred = values - middle
    spread = jnp.mean(centred * centred, axis=-1, keepdims=True)
    return centred * lax.rsqrt(spread + EPS_VISION) * gain


def masked_softmax(scores, allowed):
    highest = jnp.max(jnp.where(allowed, scores, FILL), axis=-1, keepdims=True)
    weights = jnp.where(allowed, jnp.exp(scores - highest), 0.0)
    summed = jnp.sum(weights, axis=-1, keepdims=True)
    anything = jnp.any(allowed, axis=-1, keepdims=True)
    return (weights / jnp.where(anything, summed, 1.0)).astype(jnp.bfloat16)


def local(
    text_rows,
    text_gain,
    query_weight,
    key_weight,
    value_weight,
    images,
    patch_counts,
    image_counts,
    image_spans,
    latents,
    latent_gain,
    context_gain,
    final_gain,
    res_query,
    res_key,
    res_value,
    res_output,
):
    tokens_here = text_rows.shape[0]
    source = text_rows.astype(jnp.float32)
    power = lax.psum(jnp.sum(source * source, axis=-1), "head")
    scaled = source * lax.rsqrt(power / D + EPS_TEXT)[:, None] * text_gain.astype(jnp.float32)
    normed_text = lax.all_gather(scaled.astype(jnp.bfloat16), "head", axis=1, tiled=True)
    queries = jnp.dot(
        normed_text,
        lax.all_gather(query_weight, "seq", axis=0, tiled=True),
        preferred_element_type=jnp.float32,
    ).astype(jnp.bfloat16)
    slot_count = images.shape[0]
    res_local = res_query.shape[1] // RHD
    latent_base = latents.astype(jnp.float32)
    latent_normed = layer_norm(latent_base, latent_gain.astype(jnp.float32)).astype(jnp.bfloat16)
    latent_queries = (
        jnp.dot(latent_normed, res_query, preferred_element_type=jnp.float32)
        .astype(jnp.bfloat16)
        .reshape(LAT, res_local, RHD)
    )
    context_normed = layer_norm(
        images.astype(jnp.float32), context_gain.astype(jnp.float32)
    ).astype(jnp.bfloat16)
    patch_keys = jnp.einsum(
        "cpf,fe->cpe", context_normed, res_key, preferred_element_type=jnp.float32
    ).astype(jnp.bfloat16)
    patch_values = jnp.einsum(
        "cpf,fe->cpe", context_normed, res_value, preferred_element_type=jnp.float32
    ).astype(jnp.bfloat16)
    latent_keys = jnp.dot(latent_normed, res_key, preferred_element_type=jnp.float32).astype(
        jnp.bfloat16
    )
    latent_values = jnp.dot(latent_normed, res_value, preferred_element_type=jnp.float32).astype(
        jnp.bfloat16
    )
    res_keys = jnp.concatenate(
        [patch_keys, jnp.broadcast_to(latent_keys[None], (slot_count, LAT, latent_keys.shape[1]))],
        axis=1,
    ).reshape(slot_count, PATCH + LAT, res_local, RHD)
    res_values = jnp.concatenate(
        [
            patch_values,
            jnp.broadcast_to(latent_values[None], (slot_count, LAT, latent_values.shape[1])),
        ],
        axis=1,
    ).reshape(slot_count, PATCH + LAT, res_local, RHD)
    res_scores = jnp.einsum(
        "qhd,ckhd->chqk", latent_queries, res_keys, preferred_element_type=jnp.float32
    ) * RHD ** (-0.5)
    key_rows = jnp.arange(PATCH + LAT, dtype=jnp.int32)
    patch_allowed = (key_rows[None, :] < patch_counts[:, None]) | (key_rows[None, :] >= PATCH)
    res_probs = masked_softmax(res_scores, patch_allowed[:, None, None, :])
    res_heads = (
        jnp.einsum("chqk,ckhd->cqhd", res_probs, res_values, preferred_element_type=jnp.float32)
        .astype(jnp.bfloat16)
        .reshape(slot_count, LAT, res_local * RHD)
    )
    partial_mix = jnp.einsum(
        "cqe,ef->cqf", res_heads, res_output, preferred_element_type=jnp.float32
    )
    mixed = lax.psum(partial_mix, "head")
    resampled = layer_norm(latent_base[None] + mixed, final_gain.astype(jnp.float32)).astype(
        jnp.bfloat16
    )
    live_slot = jnp.arange(slot_count, dtype=jnp.int32) < image_counts[0]
    span_bounds = jnp.where(live_slot[None, :], image_spans, 0)
    own_keys = jnp.einsum(
        "slf,fe->sle",
        resampled,
        lax.all_gather(key_weight, "seq", axis=0, tiled=True),
        preferred_element_type=jnp.float32,
    ).astype(jnp.bfloat16)
    own_values = jnp.einsum(
        "slf,fe->sle",
        resampled,
        lax.all_gather(value_weight, "seq", axis=0, tiled=True),
        preferred_element_type=jnp.float32,
    ).astype(jnp.bfloat16)
    key_list = [own_keys]
    value_list = [own_values]
    bound_list = [span_bounds]
    for distance in range(1, REACH + 1):
        far_keys, far_values, far_bounds = shifted(
            (own_keys, own_values, span_bounds), "seq", distance
        )
        key_list.insert(0, far_keys)
        value_list.insert(0, far_values)
        bound_list.insert(0, far_bounds)
    near_keys = jnp.concatenate(key_list, axis=0)
    near_values = jnp.concatenate(value_list, axis=0)
    near_bounds = jnp.concatenate(bound_list, axis=1)
    window = near_keys.shape[0]
    cross_local = queries.shape[1] // HD
    flat_keys = near_keys.reshape(window * LAT, cross_local, HD)
    flat_values = near_values.reshape(window * LAT, cross_local, HD)
    position = lax.axis_index("seq") * tokens_here + jnp.arange(tokens_here, dtype=jnp.int32)
    seen = (position[:, None] >= near_bounds[0][None, :]) & (
        position[:, None] < near_bounds[1][None, :]
    )
    seen = jnp.broadcast_to(seen[:, :, None], (tokens_here, window, LAT)).reshape(
        tokens_here, window * LAT
    )
    cross_scores = jnp.einsum(
        "thd,khd->htk",
        queries.reshape(tokens_here, cross_local, HD),
        flat_keys,
        preferred_element_type=jnp.float32,
    ) * HD ** (-0.5)
    cross_probs = masked_softmax(cross_scores, seen[None])
    attended = jnp.einsum(
        "htk,khd->thd", cross_probs, flat_values, preferred_element_type=jnp.float32
    ).astype(jnp.bfloat16)
    return attended.reshape(tokens_here, cross_local * HD)


def solution(mesh):
    return jax.shard_map(
        local,
        mesh=mesh,
        in_specs=(
            P("seq", "head"),
            P("head"),
            P("seq", "head"),
            P("seq", "head"),
            P("seq", "head"),
            P("seq", None, None),
            P("seq"),
            P("seq"),
            P(None, "seq"),
            P(),
            P(),
            P(),
            P(),
            P(None, "head"),
            P(None, "head"),
            P(None, "head"),
            P("head", None),
        ),
        out_specs=P("seq", "head"),
        check_vma=False,
    )
```

profile of v0, /device:TPU:24, one launch (start us, length us, event | category | flops | bytes accessed | tf_op | source)
XLA Modules:
  0.0 602.2 jit_solution(17090359084221551399)
XLA Ops:
  7.4 0.8 convert_element_type.80
  8.2 1.0 convert_reduce_fusion.1
  9.3 1.2 multiply_reduce_fusion.1
  10.5 0.7 convert_element_type.77
  11.2 1.6 convert_reduce_fusion
  12.8 1.8 fusion.15
  14.6 0.3 convolution_convert_fusion.8
  15.0 0.3 convolution_convert_fusion.7
  15.3 0.9 convolution_convert_fusion.2
  16.2 0.9 convolution_convert_fusion.1
  17.5 1.1 copy.49
  19.0 0.3 convolution_convert_fusion.6
  19.7 0.5 fusion.45
  20.2 1.6 fusion.24
  22.1 1.2 fusion.29
  23.4 0.5 all-gather.13.cloned.1.call-update
  24.0 0.5 all-gather.11.cloned.1.call-update
  24.6 0.5 fusion.6
  25.1 6.9 %psum.15 = f32[512]{0:T(512)S(1)} all-reduce(f32[512]{0:T(512)S(1)} %fusion.6), channel_id=1, replica_groups=mesh['seq'=64,'head'=4] {'head'}, use_global_device_ids=true, to_apply=%region_11.12 | all-reduce | flops 512 | bytes 4096 | tf_op jit(solution)/shard_map/psum | solution.py:61
  32.0 1.9 fusion.8
  33.9 0.7 all-gather.9.cloned.1.call-update
  35.3 4.6 collective-permute-start.3
  39.9 3.8 collective-permute-start.2
  43.9 3.1 collective-permute-done.3
  47.0 2.5 collective-permute-done.2
  49.5 20.6 %all-reduce.2.cloned.1.call-done = f32[2,64,1280]{2,1,0:T(8,128)} async-done(((f32[2,64,1280]{2,1,0:T(8,128)}), f32[2,64,1280]{2,1,0:T(8,128)}) %all-reduce.2.cloned.1.call-update) | async-done | bytes 655376 | tf_op jit(solution)/shard_map/psum | solution.py:118
  70.2 1.2 add_reduce_fusion
  71.4 1.3 multiply_reduce_fusion
  72.7 1.2 multiply_convert_fusion
  74.0 79.9 %all-gather.13.cloned.1.call-done = bf16[64,20,1024]{2,1,0:T(8,128)(2,1)} async-done(((bf16[1,20,1024]{2,1,0:T(8,128)(2,1)}), bf16[64,20,1024]{2,1,0:T(8,128)(2,1)}) %all-gather.13.cloned.1.call-update) | async-done | bytes 2621456 | tf_op jit(solution)/shard_map/all_gather | solution.py:127
  153.9 3.6 reshape.241
  157.5 0.5 convolution_convert_fusion.3
  158.0 2.5 collective-permute-start.5
  160.5 3.1 collective-permute-start.4
  163.6 114.0 %all-gather.11.cloned.1.call-done = bf16[64,20,1024]{2,1,0:T(8,128)(2,1)} async-done(((bf16[1,20,1024]{2,1,0:T(8,128)(2,1)}), bf16[64,20,1024]{2,1,0:T(8,128)(2,1)}) %all-gather.11.cloned.1.call-update) | async-done | bytes 2621456 | tf_op jit(solution)/shard_map/all_gather | solution.py:133
  277.5 3.6 reshape.240
  281.2 0.5 convolution_convert_fusion.4
  281.7 2.5 collective-permute-start.1
  284.1 3.2 collective-permute-start
  287.6 1.1 pad_maximum_fusion.1
  288.8 9.2 %collective-permute-done.1 = bf16[2,64,1024]{2,1,0:T(8,128)(2,1)S(1)} collective-permute-done((bf16[2,64,1024]{2,1,0:T(8,128)(2,1)S(1)}, bf16[2,64,1024]{2,1,0:T(8,128)(2,1)S(1)}, u32[]{:S(2)}, u32[]{:S(2)}) %collective-permute-start.1) | collective-permute-done | bytes 262176 | tf_op jit(solution)/shard_map/ppermute | solution.py:22
  298.3 60.1 %all-gather.7.cloned.1.call-done = bf16[512,8192]{1,0:T(8,128)(2,1)} async-done(((bf16[512,2048]{1,0:T(8,128)(2,1)}), bf16[512,8192]{1,0:T(8,128)(2,1)}) %all-gather.7.cloned.1.call-update) | async-done | bytes 8388624 | tf_op jit(solution)/shard_map/all_gather | solution.py:63
  358.4 215.2 %all-gather.9.cloned.1.call-done = bf16[8192,1024]{1,0:T(8,128)(2,1)} async-done(((bf16[128,1024]{1,0:T(8,128)(2,1)}), bf16[8192,1024]{1,0:T(8,128)(2,1)}) %all-gather.9.cloned.1.call-update) | async-done | bytes 16777232 | tf_op jit(solution)/shard_map/all_gather | solution.py:66
  573.6 14.8 %fusion.19 = bf16[64,8,8,128]{3,2,1,0:T(8,128)(2,1)S(1)} fusion(bf16[512,8192]{1,0:T(8,128)(2,1)} %all-gather.7.cloned.1.call-done, bf16[8192,1024]{1,0:T(8,128)(2,1)} %all-gather.9.cloned.1.call-done), kind=kOutput, calls=%fused_computation.25 | convolution fusion | flops 8590458880 | bytes 26214400 | tf_op jit(solution)/shard_map/dot_general | solution.py:64
  588.4 1.0 fusion.26
  589.5 3.0 fusion.46
  592.5 0.8 fusion.18
  593.2 1.3 copy.59
  (69 shorter events, 2.4 us)
Async XLA Ops:
  7.4 7.2 %copy-start = (bf16[1280,384]{1,0:T(8,128)(2,1)S(1)}, bf16[1280,384]{1,0:T(8,128)(2,1)}, u32[]{:S(2)}) copy-start(bf16[1280,384]{1,0:T(8,128)(2,1)} %param.32) | copy-start | bytes 2949124
  7.4 7.3 %copy-start.3 = (bf16[64,1280]{1,0:T(8,128)(2,1)S(1)}, bf16[64,1280]{1,0:T(8,128)(2,1)}, u32[]{:S(2)}) copy-start(bf16[64,1280]{1,0:T(8,128)(2,1)} %param.26) | copy-start | bytes 491524
  7.4 7.6 %copy-start.5 = (bf16[1280,384]{1,0:T(8,128)(2,1)S(1)}, bf16[1280,384]{1,0:T(8,128)(2,1)}, u32[]{:S(2)}) copy-start(bf16[1280,384]{1,0:T(8,128)(2,1)} %param.31) | copy-start | bytes 2949124
  7.4 62.8 %all-reduce.2.cloned.1.call-start = ((), (), s32[]{:S(2)}) async-start(), calls=%async_computation | async-start | bytes 1310720 | tf_op jit(solution)/shard_map/psum | solution.py:118
  9.3 6.0 %copy-start.4 = (bf16[2,256,1280]{2,1,0:T(8,128)(2,1)S(1)}, bf16[2,256,1280]{2,1,0:T(8,128)(2,1)}, u32[]{:S(2)}) copy-start(bf16[2,256,1280]{2,1,0:T(8,128)(2,1)} %param.22) | copy-start | bytes 3932164
  16.2 0.9 copy-start.11
  17.1 1.8 copy-start.6
  19.7 2.5 copy-start.7
  20.2 4.3 copy-start.8
  20.2 4.3 copy-start.2
  23.3 130.5 %all-gather.13.cloned.1.call-start = ((), (), s32[]{:S(2)}) async-start(), calls=%async_computation.4 | async-start | bytes 3194880 | tf_op jit(solution)/shard_map/all_gather | solution.py:127
  23.9 253.6 %all-gather.11.cloned.1.call-start = ((), (), s32[]{:S(2)}) async-start(), calls=%async_computation.3 | async-start | bytes 3194880 | tf_op jit(solution)/shard_map/all_gather | solution.py:133
  24.5 333.9 %all-gather.7.cloned.1.call-start = ((), (), s32[]{:S(2)}) async-start(), calls=%async_computation.1 | async-start | bytes 10485760 | tf_op jit(solution)/shard_map/all_gather | solution.py:63
  32.0 3.3 copy-start.10
  32.0 11.8 %copy-start.9 = (bf16[1280]{0:T(1024)(128)(2,1)S(1)}, bf16[1280]{0:T(1024)(128)(2,1)}, u32[]{:S(2)}) copy-start(bf16[1280]{0:T(1024)(128)(2,1)} %param.29) | copy-start | bytes 7684
  33.9 539.7 %all-gather.9.cloned.1.call-start = ((), (), s32[]{:S(2)}) async-start(), calls=%async_computation.2 | async-start | bytes 17039360 | tf_op jit(solution)/shard_map/all_gather | solution.py:66
  35.3 11.7 %collective-permute-start.3 = (s32[2,2]{1,0:T(2,128)S(1)}, s32[2,2]{1,0:T(2,128)S(1)}, u32[]{:S(2)}, u32[]{:S(2)}) collective-permute-start(s32[2,2]{1,0:T(2,128)S(1)} %broadcast_select_fusion.2), channel_id=1, source_target_pairs={{0,4},{4,8},{8,12},{12,16},{16,20},{20,24},{24,28},{28,32},{32,36}... | collective-permute-start | bytes 56 | tf_op jit(solution)/shard_map/ppermute | solution.py:22
  39.9 9.5 %collective-permute-start.2 = (s32[2,2]{1,0:T(2,128)S(1)}, s32[2,2]{1,0:T(2,128)S(1)}, u32[]{:S(2)}, u32[]{:S(2)}) collective-permute-start(s32[2,2]{1,0:T(2,128)S(1)} %broadcast_select_fusion.2), channel_id=1, source_target_pairs={{0,8},{4,12},{8,16},{12,20},{16,24},{20,28},{24,32},{28,36},{32,40... | collective-permute-start | bytes 56 | tf_op jit(solution)/shard_map/ppermute | solution.py:22
  158.0 129.5 %collective-permute-start.5 = (bf16[2,64,1024]{2,1,0:T(8,128)(2,1)S(1)}, bf16[2,64,1024]{2,1,0:T(8,128)(2,1)S(1)}, u32[]{:S(2)}, u32[]{:S(2)}) collective-permute-start(bf16[2,64,1024]{2,1,0:T(8,128)(2,1)S(1)} %convolution_convert_fusion.3), channel_id=1, source_target_pairs={{0,4},{4,8},{8,12},{12,16},{16,20},{20,24},{24,28},{28,32},{32,36}... | collective-permute-start | bytes 786440 | tf_op jit(solution)/shard_map/ppermute | solution.py:22
  160.5 127.1 %collective-permute-start.4 = (bf16[2,64,1024]{2,1,0:T(8,128)(2,1)S(1)}, bf16[2,64,1024]{2,1,0:T(8,128)(2,1)}, u32[]{:S(2)}, u32[]{:S(2)}) collective-permute-start(bf16[2,64,1024]{2,1,0:T(8,128)(2,1)S(1)} %convolution_convert_fusion.3), channel_id=1, source_target_pairs={{0,8},{4,12},{8,16},{12,20},{16,24},{20,28},{24,32},{28,36},{32,40... | collective-permute-start | bytes 786440 | tf_op jit(solution)/shard_map/ppermute | solution.py:22
  281.7 16.3 %collective-permute-start.1 = (bf16[2,64,1024]{2,1,0:T(8,128)(2,1)S(1)}, bf16[2,64,1024]{2,1,0:T(8,128)(2,1)S(1)}, u32[]{:S(2)}, u32[]{:S(2)}) collective-permute-start(bf16[2,64,1024]{2,1,0:T(8,128)(2,1)S(1)} %convolution_convert_fusion.4), channel_id=1, source_target_pairs={{0,4},{4,8},{8,12},{12,16},{16,20},{20,24},{24,28},{28,32},{32,36}... | collective-permute-start | bytes 786440 | tf_op jit(solution)/shard_map/ppermute | solution.py:22
  284.1 13.8 %collective-permute-start = (bf16[2,64,1024]{2,1,0:T(8,128)(2,1)S(1)}, bf16[2,64,1024]{2,1,0:T(8,128)(2,1)S(1)}, u32[]{:S(2)}, u32[]{:S(2)}) collective-permute-start(bf16[2,64,1024]{2,1,0:T(8,128)(2,1)S(1)} %convolution_convert_fusion.4), channel_id=1, source_target_pairs={{0,8},{4,12},{8,16},{12,20},{16,24},{20,28},{24,32},{28,36},{32,40... | collective-permute-start | bytes 786440 | tf_op jit(solution)/shard_map/ppermute | solution.py:22
  592.4 2.1 copy-start.1
Sparse Core Ops, SparseCore 0:
  23.5 46.6 all-reduce.1
Sparse Core Ops, SparseCore 1:
  27.5 126.3 all-gather.12
  157.4 120.0 all-gather.10
  279.2 79.1 all-gather.6
  362.1 211.4 all-gather.8
where the time goes:
time: 603 us; the launch traced here: 602 us
  waiting for transfers between devices  506 us (84%)
  matrix products  23.4 us (4%)
  starting transfers between devices  19.9 us (3%)
  other arithmetic  18.6 us (3%)
  between operations  16.2 us (3%)
  local copies, waits for them, and re-layouts  10.8 us (2%)
  blocking collectives  6.9 us (1%)
    all_gather x1, waiting for transfers between devices, local(): lax.all_gather(query_weight, 'seq', axis=0, tiled=True)  215 us
    all_gather x1, waiting for transfers between devices, local(): lax.all_gather(value_weight, 'seq', axis=0, tiled=True)  114 us
    all_gather x1, waiting for transfers between devices, local(): lax.all_gather(key_weight, 'seq', axis=0, tiled=True)  79.9 us
    all_gather x1, waiting for transfers between devices, local(): lax.all_gather(scaled.astype(jnp.bfloat16), 'head', axis=1, tiled=True)  60.1 us
    psum x1, waiting for transfers between devices, local(): mixed = lax.psum(partial_mix, 'head')  20.6 us
    ppermute x6, starting transfers between devices, shifted(): return lax.ppermute(x, axis, pairs)  19.7 us
    dot_general x1, matrix products, local(): jnp.dot(normed_text, lax.all_gather(query_weight, 'seq', axis=0, tiled=Tr...  14.8 us
    ppermute x6, waiting for transfers between devices, shifted(): return lax.ppermute(x, axis, pairs)  14.8 us
  transfers between devices with their start and end apart: 11, of which 8 were waited for; matrix products, arithmetic and copies ran while one was open for 3% of the time, Pallas kernels for 0%

commit v1 on v0

v1 whole, which is shorter than its diff:
```python
import functools

import jax
import jax.numpy as jnp
from jax import lax
from jax.experimental import pallas as pl
from jax.experimental.pallas import tpu as pltpu
from jax.sharding import Mesh, PartitionSpec as P

D = 8192
HD = 128
RHD = 96
LAT = 64
PATCH = 256
VW = 1280

EPS_TEXT = 1e-06
EPS_VISION = 1e-05
FILL = -1e30

NY, NZ, NX = 4, 8, 4
TOK = 512
COLS = 512
KEYS = 512
ROWS = 128


def layer_norm(values, gain):
    middle = jnp.mean(values, axis=-1, keepdims=True)
    centred = values - middle
    spread = jnp.mean(centred * centred, axis=-1, keepdims=True)
    return centred * lax.rsqrt(spread + EPS_VISION) * gain


def masked_softmax(scores, allowed):
    highest = jnp.max(jnp.where(allowed, scores, FILL), axis=-1, keepdims=True)
    weights = jnp.where(allowed, jnp.exp(scores - highest), 0.0)
    summed = jnp.sum(weights, axis=-1, keepdims=True)
    anything = jnp.any(allowed, axis=-1, keepdims=True)
    return (weights / jnp.where(anything, summed, 1.0)).astype(jnp.bfloat16)


def turned(x, axis, by, count):
    return lax.ppermute(x, axis, [(i, (i + by) % count) for i in range(count)])


def next_pair(x):
    return lax.ppermute(x, ("y", "z"), [(i, i + 1) for i in range(NY * NZ - 1)])


def absolute(blocks, axis, place, count):
    twice = jnp.concatenate([blocks, blocks], axis=axis)
    return lax.dynamic_slice_in_dim(twice, (count - place) % count, count, axis)


def relative(blocks, axis, place, count):
    twice = jnp.concatenate([blocks, blocks], axis=axis)
    return lax.dynamic_slice_in_dim(twice, place, count, axis)


def gather_rows(early, late):
    e1 = turned(early, "y", -1, NY)
    e3 = turned(early, "y", 1, NY)
    e2 = turned(early, "y", 2, NY)
    plus = [late]
    minus = [late]
    plus.append(turned(plus[-1], "z", -1, NZ))
    minus.append(turned(minus[-1], "z", 1, NZ))
    column = jnp.stack([early, e1, e2, e3])
    for _ in range(2):
        plus.append(turned(plus[-1], "z", -1, NZ))
        minus.append(turned(minus[-1], "z", 1, NZ))
    cut = late.shape[0] // 2
    far = jnp.concatenate(
        [turned(plus[3][:cut], "z", -1, NZ), turned(minus[3][cut:], "z", 1, NZ)], axis=0
    )
    row = jnp.stack([plus[0], plus[1], plus[2], plus[3], far, minus[3], minus[2], minus[1]])
    cplus = [column]
    cminus = [column]
    for _ in range(3):
        cplus.append(turned(cplus[-1], "z", -1, NZ))
        cminus.append(turned(cminus[-1], "z", 1, NZ))
    cfar = jnp.concatenate(
        [turned(cplus[3][:2], "z", -1, NZ), turned(cminus[3][2:], "z", 1, NZ)], axis=0
    )
    r1 = turned(row, "y", -1, NY)
    r3 = turned(row, "y", 1, NY)
    r2 = turned(row, "y", 2, NY)
    early_all = jnp.stack(
        [cplus[0], cplus[1], cplus[2], cplus[3], cfar, cminus[3], cminus[2], cminus[1]], axis=1
    )
    late_all = jnp.stack([row, r1, r2, r3])
    return early_all, late_all


def attend_kernel(where_ref, text_ref, weight_ref, scale_ref, key_ref, value_ref, bound_ref, out_ref, acc_ref):
    step = pl.program_id(0)
    part = jnp.dot(text_ref[0], weight_ref[...], preferred_element_type=jnp.float32)

    @pl.when(step == 0)
    def _():
        acc_ref[...] = part

    @pl.when(step > 0)
    def _():
        acc_ref[...] += part

    @pl.when(step == NY - 1)
    def _():
        position = where_ref[1] + lax.broadcasted_iota(jnp.int32, (TOK, KEYS), 0)
        seen = (position >= bound_ref[0:1, :]) & (position < bound_ref[1:2, :])
        anything = jnp.any(seen, axis=-1, keepdims=True)
        for head in range(COLS // HD):
            cols = pl.ds(head * HD, HD)
            queries = (acc_ref[:, cols] * scale_ref[...]).astype(jnp.bfloat16)
            scores = lax.dot_general(
                queries, key_ref[:, cols], (((1,), (1,)), ((), ())), preferred_element_type=jnp.float32
            ) * HD ** (-0.5)
            scores = jnp.where(seen, scores, FILL)
            highest = jnp.max(scores, axis=-1, keepdims=True)
            weights = jnp.where(seen, jnp.exp(scores - highest), 0.0)
            summed = jnp.sum(weights, axis=-1, keepdims=True)
            probs = (weights * (1.0 / jnp.where(anything, summed, 1.0))).astype(jnp.bfloat16)
            out_ref[:, cols] = jnp.dot(
                probs, value_ref[:, cols], preferred_element_type=jnp.float32
            ).astype(jnp.bfloat16)


def attend(half, pair, text, weight, scale, keys, values, bounds):
    where = jnp.stack([half, pair * (2 * TOK) + half * TOK]).astype(jnp.int32)
    return pl.pallas_call(
        attend_kernel,
        out_shape=jax.ShapeDtypeStruct((TOK, COLS), jnp.bfloat16),
        grid_spec=pltpu.PrefetchScalarGridSpec(
            num_scalar_prefetch=1,
            grid=(NY,),
            in_specs=[
                pl.BlockSpec((1, TOK, D // NY), lambda k, w: (w[0] * NY + k, 0, 0)),
                pl.BlockSpec((D // NY, COLS), lambda k, w: (k, 0)),
                pl.BlockSpec((TOK, 1), lambda k, w: (w[0], 0)),
                pl.BlockSpec((KEYS, COLS), lambda k, w: (0, 0)),
                pl.BlockSpec((KEYS, COLS), lambda k, w: (0, 0)),
                pl.BlockSpec((2, KEYS), lambda k, w: (0, 0)),
            ],
            out_specs=pl.BlockSpec((TOK, COLS), lambda k, w: (0, 0)),
            scratch_shapes=[pltpu.VMEM((TOK, COLS), jnp.float32)],
        ),
        compiler_params=pltpu.CompilerParams(vmem_limit_bytes=32 * 1024 * 1024),
        cost_estimate=pl.CostEstimate(
            flops=2 * TOK * COLS * (D + 2 * KEYS), bytes_accessed=18 << 20, transcendentals=TOK * KEYS * 4
        ),
    )(where, text, weight, scale, keys, values, bounds)


def resample(images, patch_counts, latents, latent_gain, context_gain, res_query, res_key, res_value, res_output):
    slot_count = images.shape[0]
    res_local = res_query.shape[1] // RHD
    latent_base = latents.astype(jnp.float32)
    latent_normed = layer_norm(latent_base, latent_gain.astype(jnp.float32)).astype(jnp.bfloat16)
    latent_queries = (
        jnp.dot(latent_normed, res_query, preferred_element_type=jnp.float32)
        .astype(jnp.bfloat16)
        .reshape(LAT, res_local, RHD)
    )
    context_normed = layer_norm(
        images.astype(jnp.float32), context_gain.astype(jnp.float32)
    ).astype(jnp.bfloat16)
    patch_keys = jnp.einsum(
        "cpf,fe->cpe", context_normed, res_key, preferred_element_type=jnp.float32
    ).astype(jnp.bfloat16)
    patch_values = jnp.einsum(
        "cpf,fe->cpe", context_normed, res_value, preferred_element_type=jnp.float32
    ).astype(jnp.bfloat16)
    latent_keys = jnp.dot(latent_normed, res_key, preferred_element_type=jnp.float32).astype(
        jnp.bfloat16
    )
    latent_values = jnp.dot(latent_normed, res_value, preferred_element_type=jnp.float32).astype(
        jnp.bfloat16
    )
    res_keys = jnp.concatenate(
        [patch_keys, jnp.broadcast_to(latent_keys[None], (slot_count, LAT, latent_keys.shape[1]))],
        axis=1,
    ).reshape(slot_count, PATCH + LAT, res_local, RHD)
    res_values = jnp.concatenate(
        [
            patch_values,
            jnp.broadcast_to(latent_values[None], (slot_count, LAT, latent_values.shape[1])),
        ],
        axis=1,
    ).reshape(slot_count, PATCH + LAT, res_local, RHD)
    res_scores = jnp.einsum(
        "qhd,ckhd->chqk", latent_queries, res_keys, preferred_element_type=jnp.float32
    ) * RHD ** (-0.5)
    key_rows = jnp.arange(PATCH + LAT, dtype=jnp.int32)
    patch_allowed = (key_rows[None, :] < patch_counts[:, None]) | (key_rows[None, :] >= PATCH)
    res_probs = masked_softmax(res_scores, patch_allowed[:, None, None, :])
    res_heads = (
        jnp.einsum("chqk,ckhd->cqhd", res_probs, res_values, preferred_element_type=jnp.float32)
        .astype(jnp.bfloat16)
        .reshape(slot_count, LAT, res_local * RHD)
    )
    return jnp.einsum("cqe,ef->cqf", res_heads, res_output, preferred_element_type=jnp.float32)


def local(
    text_rows,
    text_gain,
    query_weight,
    key_weight,
    value_weight,
    images,
    patch_counts,
    image_counts,
    image_spans,
    latents,
    latent_gain,
    context_gain,
    final_gain,
    res_query,
    res_key,
    res_value,
    res_output,
):
    y, z = lax.axis_index("y"), lax.axis_index("z")
    xh, xl, core = lax.axis_index("xh"), lax.axis_index("xl"), lax.axis_index("core")
    pair = y * NZ + z
    x = xh * 2 + xl

    block = jnp.concatenate([query_weight, key_weight, value_weight], axis=0)
    mine = lax.dynamic_slice_in_dim(block, xh * COLS, COLS, 1)
    other = turned(lax.dynamic_slice_in_dim(block, (1 - xh) * COLS, COLS, 1), "xh", 1, 2)
    low = jnp.where(xh == 0, mine, other)
    high = jnp.where(xh == 0, other, mine)
    part = key_weight.shape[0]
    early = low[:ROWS]
    late = jnp.concatenate(
        [
            high[:ROWS],
            low[ROWS : ROWS + part],
            high[ROWS : ROWS + part],
            low[ROWS + part :],
            high[ROWS + part :],
        ],
        axis=0,
    )
    early_all, late_all = gather_rows(early, late)

    source = text_rows.astype(jnp.float32)
    power = jnp.sum(source * source, axis=-1)
    scaled = (source * text_gain.astype(jnp.float32)).astype(jnp.bfloat16)
    text = lax.all_gather(scaled, ("xh", "xl", "core"), axis=0)

    live_slot = jnp.arange(2, dtype=jnp.int32) < image_counts[0]
    span_bounds = jnp.where(live_slot[None, :], image_spans, 0)
    small = jnp.concatenate([power, span_bounds.reshape(4).astype(jnp.float32), jnp.zeros((124,), jnp.float32)])
    small = lax.all_gather(small, ("xh", "xl", "core"), axis=0).reshape(2, 4, TOK + 128)
    power_all = jnp.sum(small[:, :, :TOK], axis=1).reshape(2 * TOK, 1)
    scale = lax.rsqrt(power_all / D + EPS_TEXT)
    own_bounds = small[:, 0, TOK : TOK + 4].reshape(2, 2, 2).transpose(1, 0, 2).reshape(2, NX)
    near = jnp.stack([next_pair(own_bounds), own_bounds], axis=1)
    near = relative(near, 2, x, NX).transpose(0, 2, 1).reshape(2, 8).astype(jnp.int32)
    bounds = jnp.repeat(near, LAT, axis=1)

    mix = resample(
        images, patch_counts, latents, latent_gain, context_gain, res_query, res_key, res_value, res_output
    ).reshape(2, 2, LAT // 2, VW)
    first = lax.dynamic_index_in_dim(mix, core, 1, keepdims=False)
    first = first + turned(lax.dynamic_index_in_dim(mix, 1 - core, 1, keepdims=False), "core", 1, 2)
    total = lax.dynamic_index_in_dim(first, xl, 0, keepdims=False)
    total = total + turned(lax.dynamic_index_in_dim(first, 1 - xl, 0, keepdims=False), "xl", 1, 2)
    base = lax.dynamic_slice_in_dim(latents, core * (LAT // 2), LAT // 2, 0).astype(jnp.float32)
    piece = layer_norm(base + total, final_gain.astype(jnp.float32)).astype(jnp.bfloat16)
    both = jnp.stack([next_pair(piece), piece])
    ring = ("xh", "xl")
    around = jnp.stack(
        [both, turned(both, ring, -1, NX), turned(both, ring, 2, NX), turned(both, ring, 1, NX)]
    )
    resampled = jnp.stack([around, turned(around, "core", 1, 2)], axis=2).reshape(KEYS, VW)

    heads_weight = absolute(absolute(late_all[:, :, ROWS:], 1, z, NZ), 0, y, NY)
    heads_weight = heads_weight.reshape(NY * NZ, 2, 2 * part, COLS)
    keys = jnp.dot(
        resampled, heads_weight[:, 0].reshape(VW, COLS), preferred_element_type=jnp.float32
    ).astype(jnp.bfloat16)
    values = jnp.dot(
        resampled, heads_weight[:, 1].reshape(VW, COLS), preferred_element_type=jnp.float32
    ).astype(jnp.bfloat16)

    weight = jnp.concatenate([early_all, late_all[:, :, :ROWS]], axis=2)
    weight = absolute(absolute(weight, 1, z, NZ), 0, y, NY).reshape(D, COLS)

    theirs = attend(1 - xh, pair, text, weight, scale, keys, values, bounds)
    received = turned(theirs, "xh", 1, 2)
    ours = attend(xh, pair, text, weight, scale, keys, values, bounds)
    return jnp.where(
        xh == 0,
        jnp.concatenate([ours, received], axis=1),
        jnp.concatenate([received, ours], axis=1),
    )


def solution(mesh):
    fine = Mesh(mesh.devices.reshape(NY, NZ, 2, 2, 2), ("y", "z", "xh", "xl", "core"))
    seq = ("y", "z", "xh")
    head = ("xl", "core")
    return jax.shard_map(
        local,
        mesh=fine,
        in_specs=(
            P(seq, head),
            P(head),
            P(seq, head),
            P(seq, head),
            P(seq, head),
            P(seq, None, None),
            P(seq),
            P(seq),
            P(None, seq),
            P(),
            P(),
            P(),
            P(),
            P(None, head),
            P(None, head),
            P(None, head),
            P(head, None),
        ),
        out_specs=P(seq, head),
        check_vma=False,
    )
```

time: 603 us -> 281 us (0.47)
  the two profiles are of different devices: /device:TPU:24 before, /device:TPU:102 now
where the time goes in v1:
time: 281 us; the launch traced here: 277 us
  waiting for transfers between devices  111 us (40%)
  starting transfers between devices  62.1 us (22%)
  other arithmetic  33 us (12%)
  Pallas kernels  21.7 us (8%)
  between operations  15.1 us (5%)
  local copies, waits for them, and re-layouts  12.7 us (5%)
  blocking collectives  12.5 us (4%)
  matrix products  9.04 us (3%)
    ppermute x30, waiting for transfers between devices, turned(): return lax.ppermute(x, axis, [(i, (i + by) % count) for i in range(count)])  108 us
    ppermute x30, starting transfers between devices, turned(): return lax.ppermute(x, axis, [(i, (i + by) % count) for i in range(count)])  53.2 us
    concatenate x4, other arithmetic, absolute(): twice = jnp.concatenate([blocks, blocks], axis=axis)  21.7 us
    pallas_call x2, Pallas kernels, attend(): pl.pallas_call(attend_kernel, out_shape=jax.ShapeDtypeStruct((TOK, COLS),...  21.7 us
    all_gather x1, blocking collectives, local(): lax.all_gather(small, ('xh', 'xl', 'core'), axis=0).reshape(2, 4, TOK + 128)  12.5 us
    ppermute x2, starting transfers between devices, next_pair(): return lax.ppermute(x, ('y', 'z'), [(i, i + 1) for i in range(NY * NZ - 1)])  8.88 us
    unnamed x56, local copies, waits for them, and re-layouts  6.78 us
  transfers between devices with their start and end apart: 33, of which 15 were waited for; matrix products, arithmetic and copies ran while one was open for 15% of the time, Pallas kernels for 4%

profile of v1, /device:TPU:102, one launch (start us, length us, event | category | flops | bytes accessed | tf_op | source)
XLA Modules:
  0.0 277.3 jit_solution(12668543523332459521)
XLA Ops:
  7.3 3.6 %fusion.6 = (f32[512]{0:T(512)S(1)}, bf16[512,2048]{1,0:T(8,128)(2,1)}) fusion(bf16[512,2048]{1,0:T(8,128)(2,1)} %param.17, f32[2048]{0:T(1024)S(1)} %convert_element_type.82), kind=kLoop, calls=%fused_computation.19 | loop fusion | flops 5242368 | bytes 4204544 | tf_op jit(solution)/shard_map/reduce_sum | solution.py:249
  11.7 1.4 collective-permute-start
  14.6 0.9 convolution_convert_fusion.2
  16.0 1.5 convolution_convert_fusion.5
  17.6 1.5 convolution_convert_fusion.7
  19.2 2.1 convolution_convert_fusion.3
  21.4 1.1 copy.77
  26.2 12.5 %all-gather.2 = f32[8,1,640]{2,1,0:T(1,128)S(1)} all-gather(f32[1,1,640]{2,1,0:T(1,128)S(1)} %reshape.189), channel_id=3, replica_groups=mesh['y'=4,'z'=8,'xh'=2,'xl'=2,'core'=2] {'xh','xl','core'}, dimensions={0}, use_global_device_ids=true | all-gather | bytes 23040 | tf_op jit(solution)/shard_map/all_gather | solution.py:256
  39.0 5.1 %collective-permute-start.30 = (f32[2,4]{1,0:T(2,128)S(1)}, f32[2,4]{1,0:T(2,128)S(1)}, u32[]{:S(2)}, u32[]{:S(2)}) collective-permute-start(f32[2,4]{1,0:T(2,128)S(1)} %reshape.184), channel_id=1, source_target_pairs={{0,8},{8,16},{16,24},{24,32},{32,40},{40,48},{48,56},{56,64},{64,7... | collective-permute-start | bytes 104 | tf_op jit(solution)/shard_map/ppermute | solution.py:48
  46.0 3.1 %collective-permute-start.1 = (bf16[128,512]{1,0:T(8,128)(2,1)S(1)}, bf16[128,512]{1,0:T(8,128)(2,1)S(1)}, u32[]{:S(2)}, u32[]{:S(2)}) collective-permute-start(bf16[128,512]{1,0:T(8,128)(2,1)S(1)} %get-tuple-element.20), channel_id=1, source_target_pairs={{0,192},{64,0},{128,64},{192,128},{1,193},{65,1},{129,65},{193,129... | collective-permute-start | bytes 393224 | tf_op jit(solution)/shard_map/ppermute | solution.py:44
  49.7 1.0 collective-permute-start.3
  51.1 3.1 %collective-permute-done.1 = bf16[128,512]{1,0:T(8,128)(2,1)S(1)} collective-permute-done((bf16[128,512]{1,0:T(8,128)(2,1)S(1)}, bf16[128,512]{1,0:T(8,128)(2,1)S(1)}, u32[]{:S(2)}, u32[]{:S(2)}) %collective-permute-start.1) | collective-permute-done | bytes 131104 | tf_op jit(solution)/shard_map/ppermute | solution.py:44
  54.2 3.8 %collective-permute-start.16 = (bf16[208,512]{1,0:T(8,128)(2,1)S(1)}, bf16[208,512]{1,0:T(8,128)(2,1)S(1)}, u32[]{:S(2)}, u32[]{:S(2)}) collective-permute-start(bf16[208,512]{1,0:T(8,128)(2,1)S(1)} %concatenate.47), channel_id=1, source_target_pairs={{0,8},{8,16},{16,24},{24,32},{32,40},{40,48},{48,56},{56,0},{1,9},... | collective-permute-start | bytes 638984 | tf_op jit(solution)/shard_map/ppermute | solution.py:44
  58.2 3.5 %collective-permute-start.8 = (bf16[4,128,512]{2,1,0:T(8,128)(2,1)S(1)}, bf16[4,128,512]{2,1,0:T(8,128)(2,1)S(1)}, u32[]{:S(2)}, u32[]{:S(2)}) collective-permute-start(bf16[4,128,512]{2,1,0:T(8,128)(2,1)S(1)} %pad_maximum_fusion.4), channel_id=1, source_target_pairs={{0,8},{8,16},{16,24},{24,32},{32,40},{40,48},{48,56},{56,0},{1,9},... | collective-permute-start | bytes 1572872 | tf_op jit(solution)/shard_map/ppermute | solution.py:44
  61.8 1.0 bitcast_add_fusion
  63.5 3.2 %collective-permute-start.17 = (bf16[208,512]{1,0:T(8,128)(2,1)S(1)}, bf16[208,512]{1,0:T(8,128)(2,1)S(1)}, u32[]{:S(2)}, u32[]{:S(2)}) collective-permute-start(bf16[208,512]{1,0:T(8,128)(2,1)S(1)} %collective-permute-done.16), channel_id=1, source_target_pairs={{0,8},{8,16},{16,24},{24,32},{32,40},{40,48},{48,56},{56,0},{1,9},... | collective-permute-start | bytes 638984 | tf_op jit(solution)/shard_map/ppermute | solution.py:44
  66.7 6.2 %collective-permute-done.24 = f32[32,1280]{1,0:T(8,128)S(1)} collective-permute-done((f32[32,1280]{1,0:T(8,128)S(1)}, f32[32,1280]{1,0:T(8,128)S(1)}, u32[]{:S(2)}, u32[]{:S(2)}) %collective-permute-start.24) | collective-permute-done | bytes 163872 | tf_op jit(solution)/shard_map/ppermute | solution.py:44
  73.4 3.8 %collective-permute-start.25 = (bf16[32,1280]{1,0:T(8,128)(2,1)S(1)}, bf16[32,1280]{1,0:T(8,128)(2,1)S(1)}, u32[]{:S(2)}, u32[]{:S(2)}) collective-permute-start(bf16[32,1280]{1,0:T(8,128)(2,1)S(1)} %multiply_convert_fusion), channel_id=1, source_target_pairs={{0,8},{8,16},{16,24},{24,32},{32,40},{40,48},{48,56},{56,64},{64,7... | collective-permute-start | bytes 245768 | tf_op jit(solution)/shard_map/ppermute | solution.py:48
  77.3 2.5 collective-permute-done.25
  80.3 3.3 %collective-permute-start.27 = (bf16[2,32,1280]{2,1,0:T(8,128)(2,1)S(1)}, bf16[2,32,1280]{2,1,0:T(8,128)(2,1)S(1)}, u32[]{:S(2)}, u32[]{:S(2)}) collective-permute-start(bf16[2,32,1280]{2,1,0:T(8,128)(2,1)S(1)} %get-tuple-element.22), channel_id=1, source_target_pairs={{0,4},{2,6},{4,0},{6,2},{1,5},{3,7},{5,1},{7,3},{8,12},{10,14},{12... | collective-permute-start | bytes 491528 | tf_op jit(solution)/shard_map/ppermute | solution.py:44
  84.3 7.1 %collective-permute-done.26 = bf16[2,32,1280]{2,1,0:T(8,128)(2,1)S(1)} collective-permute-done((bf16[2,32,1280]{2,1,0:T(8,128)(2,1)S(1)}, bf16[2,32,1280]{2,1,0:T(8,128)(2,1)S(1)}, u32[]{:S(2)}, u32[]{:S(2)}) %collective-permute-start.26) | collective-permute-done | bytes 163872 | tf_op jit(solution)/shard_map/ppermute | solution.py:44
  91.4 6.8 %collective-permute-done.27 = bf16[2,32,1280]{2,1,0:T(8,128)(2,1)S(1)} collective-permute-done((bf16[2,32,1280]{2,1,0:T(8,128)(2,1)S(1)}, bf16[2,32,1280]{2,1,0:T(8,128)(2,1)S(1)}, u32[]{:S(2)}, u32[]{:S(2)}) %collective-permute-start.27) | collective-permute-done | bytes 163872 | tf_op jit(solution)/shard_map/ppermute | solution.py:44
  98.2 3.3 %collective-permute-start.18 = (bf16[208,512]{1,0:T(8,128)(2,1)S(1)}, bf16[208,512]{1,0:T(8,128)(2,1)S(1)}, u32[]{:S(2)}, u32[]{:S(2)}) collective-permute-start(bf16[208,512]{1,0:T(8,128)(2,1)S(1)} %collective-permute-done.17), channel_id=1, source_target_pairs={{0,8},{8,16},{16,24},{24,32},{32,40},{40,48},{48,56},{56,0},{1,9},... | collective-permute-start | bytes 638984 | tf_op jit(solution)/shard_map/ppermute | solution.py:44
  102.0 1.8 collective-permute-start.15
  103.8 3.4 %collective-permute-done.18 = bf16[208,512]{1,0:T(8,128)(2,1)S(1)} collective-permute-done((bf16[208,512]{1,0:T(8,128)(2,1)S(1)}, bf16[208,512]{1,0:T(8,128)(2,1)S(1)}, u32[]{:S(2)}, u32[]{:S(2)}) %collective-permute-start.18) | collective-permute-done | bytes 213024 | tf_op jit(solution)/shard_map/ppermute | solution.py:44
  107.2 3.8 %collective-permute-start.19 = (bf16[104,512]{1,0:T(8,128)(2,1)S(1)}, bf16[104,512]{1,0:T(8,128)(2,1)S(1)}, u32[]{:S(2)}, u32[]{:S(2)}) collective-permute-start(bf16[104,512]{1,0:T(8,128)(2,1)S(1)} %slice.73), channel_id=1, source_target_pairs={{0,8},{8,16},{16,24},{24,32},{32,40},{40,48},{48,56},{56,0},{1,9},... | collective-permute-start | bytes 319496 | tf_op jit(solution)/shard_map/ppermute | solution.py:44
  111.1 6.6 %collective-permute-done.19 = bf16[104,512]{1,0:T(8,128)(2,1)S(1)} collective-permute-done((bf16[104,512]{1,0:T(8,128)(2,1)S(1)}, bf16[104,512]{1,0:T(8,128)(2,1)S(1)}, u32[]{:S(2)}, u32[]{:S(2)}) %collective-permute-start.19) | collective-permute-done | bytes 106528 | tf_op jit(solution)/shard_map/ppermute | solution.py:44
  117.8 15.5 %collective-permute-start.10 = (bf16[4,128,512]{2,1,0:T(8,128)(2,1)S(1)}, bf16[4,128,512]{2,1,0:T(8,128)(2,1)S(1)}, u32[]{:S(2)}, u32[]{:S(2)}) collective-permute-start(bf16[4,128,512]{2,1,0:T(8,128)(2,1)S(1)} %collective-permute-done.9), channel_id=1, source_target_pairs={{0,8},{8,16},{16,24},{24,32},{32,40},{40,48},{48,56},{56,0},{1,9},... | collective-permute-start | bytes 1572872 | tf_op jit(solution)/shard_map/ppermute | solution.py:44
  133.4 3.4 %collective-permute-start.20 = (bf16[8,208,512]{2,1,0:T(8,128)(2,1)S(1)}, bf16[8,208,512]{2,1,0:T(8,128)(2,1)S(1)}, u32[]{:S(2)}, u32[]{:S(2)}) collective-permute-start(bf16[8,208,512]{2,1,0:T(8,128)(2,1)S(1)} %bitcast_dynamic-update-slice_fusion.7), channel_id=1, source_target_pairs={{0,192},{64,0},{128,64},{192,128},{1,193},{65,1},{129,65},{193,129... | collective-permute-start | bytes 5111816 | tf_op jit(solution)/shard_map/ppermute | solution.py:44
  136.8 4.9 %collective-permute-done.10 = bf16[4,128,512]{2,1,0:T(8,128)(2,1)S(1)} collective-permute-done((bf16[4,128,512]{2,1,0:T(8,128)(2,1)S(1)}, bf16[4,128,512]{2,1,0:T(8,128)(2,1)S(1)}, u32[]{:S(2)}, u32[]{:S(2)}) %collective-permute-start.10) | collective-permute-done | bytes 524320 | tf_op jit(solution)/shard_map/ppermute | solution.py:44
  141.8 3.4 %collective-permute-done.6 = bf16[4,128,512]{2,1,0:T(8,128)(2,1)S(1)} collective-permute-done((bf16[4,128,512]{2,1,0:T(8,128)(2,1)S(1)}, bf16[4,128,512]{2,1,0:T(8,128)(2,1)S(1)}, u32[]{:S(2)}, u32[]{:S(2)}) %collective-permute-start.6) | collective-permute-done | bytes 524320 | tf_op jit(solution)/shard_map/ppermute | solution.py:44
  145.6 1.8 collective-permute-start.7
  147.5 4.1 %collective-permute-done.11 = bf16[2,128,512]{2,1,0:T(8,128)(2,1)S(1)} collective-permute-done((bf16[2,128,512]{2,1,0:T(8,128)(2,1)S(1)}, bf16[2,128,512]{2,1,0:T(8,128)(2,1)S(1)}, u32[]{:S(2)}, u32[]{:S(2)}) %collective-permute-start.11) | collective-permute-done | bytes 262176 | tf_op jit(solution)/shard_map/ppermute | solution.py:44
  151.6 1.7 collective-permute-done.7
  153.4 52.9 %collective-permute-done.20 = bf16[8,208,512]{2,1,0:T(8,128)(2,1)S(1)} collective-permute-done((bf16[8,208,512]{2,1,0:T(8,128)(2,1)S(1)}, bf16[8,208,512]{2,1,0:T(8,128)(2,1)S(1)}, u32[]{:S(2)}, u32[]{:S(2)}) %collective-permute-start.20) | collective-permute-done | bytes 1703968 | tf_op jit(solution)/shard_map/ppermute | solution.py:44
  206.4 3.7 %collective-permute-done.22 = bf16[8,208,512]{2,1,0:T(8,128)(2,1)S(1)} collective-permute-done((bf16[8,208,512]{2,1,0:T(8,128)(2,1)S(1)}, bf16[8,208,512]{2,1,0:T(8,128)(2,1)S(1)}, u32[]{:S(2)}, u32[]{:S(2)}) %collective-permute-start.22) | collective-permute-done | bytes 1703968 | tf_op jit(solution)/shard_map/ppermute | solution.py:44
  210.1 0.9 pad_maximum_fusion
  211.0 2.8 %copy-done.4 = bf16[4,8,208,512]{3,2,1,0:T(8,128)(2,1)} copy-done((bf16[4,8,208,512]{3,2,1,0:T(8,128)(2,1)}, bf16[4,8,208,512]{3,2,1,0:T(8,128)(2,1)S(1)}, u32[]{:S(2)}) %copy-start.4) | copy-done | bytes 6815768
  214.0 0.9 fusion.13
  215.0 0.9 fusion.12
  217.8 1.3 slice-done
  219.2 14.8 %fusion.3 = bf16[4,8,256,512]{3,2,1,0:T(8,128)(2,1)S(1)} fusion(s32[]{:T(128)S(6)} %select_n.96, bf16[4,8,128,512]{3,2,1,0:T(8,128)(2,1)S(1)} %bitcast_dynamic-update-slice_fusion.6, bf16[4,8,128,512]{3,2,1,0:T(8,128)(2,1)S(1)} %slice-done), kind=kLoop, calls=%fused_computation.9 | loop fusion | flops 33554432 | bytes 16777220 | tf_op jit(solution)/shard_map/concatenate | solution.py:52
  233.9 5.0 %fusion.1 = bf16[4,8,256,512]{3,2,1,0:T(8,128)(2,1)} fusion(s32[]{:T(128)S(6)} %select_n.98, bf16[4,8,256,512]{3,2,1,0:T(8,128)(2,1)S(1)} %fusion.3), kind=kLoop, calls=%fused_computation.7 | loop fusion | flops 4194304 | bytes 16777220 | tf_op jit(solution)/shard_map/concatenate | solution.py:52
  239.0 3.4 %copy-done.2 = bf16[4,8,256,512]{3,2,1,0:T(8,128)(2,1)S(1)} copy-done((bf16[4,8,256,512]{3,2,1,0:T(8,128)(2,1)S(1)}, bf16[4,8,256,512]{3,2,1,0:T(8,128)(2,1)}, u32[]{:S(2)}) %copy-start.2) | copy-done | bytes 8388632
  242.4 11.0 %shard_map.164 = bf16[512,512]{1,0:T(8,128)(2,1)S(1)} custom-call(s32[2]{0:T(128)S(1)} %pad_add_fusion.1.where_ref, bf16[8,512,2048]{2,1,0:T(8,128)(2,1)} %bitcast.135, bf16[8192,512]{1,0:T(8,128)(2,1)S(1)} %bitcast.131, f32[1024,1]{1,0:T(8,128)S(1)} %bitcast.133, bf16[512,512]{1,0:T(8,128)(2,1)S(1)} %convolution_convert_fusion.1.key_ref, ...), custom_call_target="tpu_custom_call" | custom-call | flops 4831838208 | bytes 18874368 | tf_op jit(solution)/shard_map/pallas_call | solution.py:131
  254.2 10.7 %shard_map.163 = bf16[512,512]{1,0:T(8,128)(2,1)S(1)} custom-call(s32[2]{0:T(128)S(1)} %pad_add_fusion.where_ref, bf16[8,512,2048]{2,1,0:T(8,128)(2,1)} %bitcast.136, bf16[8192,512]{1,0:T(8,128)(2,1)S(1)} %bitcast.132, f32[1024,1]{1,0:T(8,128)S(1)} %bitcast.134, bf16[512,512]{1,0:T(8,128)(2,1)S(1)} %convolution_convert_fusion.1.key_ref, ...), custom_call_target="tpu_custom_call" | custom-call | flops 4831838208 | bytes 18874368 | tf_op jit(solution)/shard_map/pallas_call | solution.py:131
  264.9 4.1 %collective-permute-done.31 = bf16[512,512]{1,0:T(8,128)(2,1)S(1)} collective-permute-done((bf16[512,512]{1,0:T(8,128)(2,1)S(1)}, bf16[512,512]{1,0:T(8,128)(2,1)S(1)}, u32[]{:S(2)}, u32[]{:S(2)}) %collective-permute-start.31) | collective-permute-done | bytes 524320 | tf_op jit(solution)/shard_map/ppermute | solution.py:44
  269.0 1.3 maximum_select_fusion
  (175 shorter events, 16.8 us)
Async XLA Ops:
  6.5 7.8 %copy-start = (bf16[1280,384]{1,0:T(8,128)(2,1)S(1)}, bf16[1280,384]{1,0:T(8,128)(2,1)}, u32[]{:S(2)}) copy-start(bf16[1280,384]{1,0:T(8,128)(2,1)} %param.31) | copy-start | bytes 2949124
  6.5 232.4 %all-gather.5.cloned.1.call-start = ((), (), s32[]{:S(2)}) async-start(), calls=%async_computation | async-start | bytes 18874368 | tf_op jit(solution)/shard_map/all_gather | solution.py:251
  7.3 3.7 %copy-start.9 = (bf16[128,1024]{1,0:T(8,128)(2,1)S(1)}, bf16[128,1024]{1,0:T(8,128)(2,1)}, u32[]{:S(2)}) copy-start(bf16[128,1024]{1,0:T(8,128)(2,1)} %param.19) | copy-start | bytes 786436
  7.3 3.7 %copy-start.10 = (bf16[20,1024]{1,0:T(8,128)(2,1)S(1)}, bf16[20,1024]{1,0:T(8,128)(2,1)}, u32[]{:S(2)}) copy-start(bf16[20,1024]{1,0:T(8,128)(2,1)} %param.21) | copy-start | bytes 122884
  7.3 3.7 %copy-start.11 = (bf16[20,1024]{1,0:T(8,128)(2,1)S(1)}, bf16[20,1024]{1,0:T(8,128)(2,1)}, u32[]{:S(2)}) copy-start(bf16[20,1024]{1,0:T(8,128)(2,1)} %param.20) | copy-start | bytes 122884
  11.0 2.6 copy-start.5
  11.7 34.1 %collective-permute-start = (bf16[168,512]{1,0:T(8,128)(2,1)}, bf16[168,512]{1,0:T(8,128)(2,1)S(1)}, u32[]{:S(2)}, u32[]{:S(2)}) collective-permute-start(bf16[168,512]{1,0:T(8,128)(2,1)} %constant_dynamic-slice_fusion.4), channel_id=1, source_target_pairs={{0,4},{4,0},{1,5},{5,1},{2,6},{6,2},{3,7},{7,3},{8,12},{12,8},{9,1... | collective-permute-start | bytes 516104 | tf_op jit(solution)/shard_map/ppermute | solution.py:44
  13.2 2.4 copy-start.12
  15.6 3.6 %copy-start.13 = (f32[1280]{0:T(1024)S(1)}, f32[1280]{0:T(1024)}, u32[]{:S(2)}) copy-start(f32[1280]{0:T(1024)} %copy-done.12) | copy-start | bytes 15364
  15.6 3.6 %copy-start.18 = (f32[2,256]{1,0:T(2,128)S(1)}, f32[2,256]{1,0:T(2,128)}, u32[]{:S(2)}) copy-start(f32[2,256]{1,0:T(2,128)} %copy-done.17) | copy-start | bytes 6148
  19.2 3.3 %copy-start.20 = (s32[2]{0:T(128)S(1)}, s32[2]{0:T(128)}, u32[]{:S(2)}) copy-start(s32[2]{0:T(128)} %param.23) | copy-start | bytes 28
  23.6 2.5 copy-start.19
  23.6 20.7 %copy-start.16 = (bf16[1280]{0:T(1024)(128)(2,1)S(1)}, bf16[1280]{0:T(1024)(128)(2,1)}, u32[]{:S(2)}) copy-start(bf16[1280]{0:T(1024)(128)(2,1)} %param.29) | copy-start | bytes 7684
  25.3 36.5 %collective-permute-start.23 = (f32[2,32,1280]{2,1,0:T(8,128)}, f32[2,32,1280]{2,1,0:T(8,128)}, u32[]{:S(2)}, u32[]{:S(2)}) collective-permute-start(f32[2,32,1280]{2,1,0:T(8,128)} %dynamic-slice_bitcast_fusion), channel_id=1, source_target_pairs={{0,1},{1,0},{2,3},{3,2},{4,5},{5,4},{6,7},{7,6},{8,9},{9,8},{10,11... | collective-permute-start | bytes 983048 | tf_op jit(solution)/shard_map/ppermute | solution.py:44
  39.0 6.4 %collective-permute-start.30 = (f32[2,4]{1,0:T(2,128)S(1)}, f32[2,4]{1,0:T(2,128)S(1)}, u32[]{:S(2)}, u32[]{:S(2)}) collective-permute-start(f32[2,4]{1,0:T(2,128)S(1)} %reshape.184), channel_id=1, source_target_pairs={{0,8},{8,16},{16,24},{24,32},{32,40},{40,48},{48,56},{56,64},{64,7... | collective-permute-start | bytes 104 | tf_op jit(solution)/shard_map/ppermute | solution.py:48
  46.0 8.3 %collective-permute-start.1 = (bf16[128,512]{1,0:T(8,128)(2,1)S(1)}, bf16[128,512]{1,0:T(8,128)(2,1)S(1)}, u32[]{:S(2)}, u32[]{:S(2)}) collective-permute-start(bf16[128,512]{1,0:T(8,128)(2,1)S(1)} %get-tuple-element.20), channel_id=1, source_target_pairs={{0,192},{64,0},{128,64},{192,128},{1,193},{65,1},{129,65},{193,129... | collective-permute-start | bytes 393224 | tf_op jit(solution)/shard_map/ppermute | solution.py:44
  49.0 9.0 %collective-permute-start.2 = (bf16[128,512]{1,0:T(8,128)(2,1)S(1)}, bf16[128,512]{1,0:T(8,128)(2,1)S(1)}, u32[]{:S(2)}, u32[]{:S(2)}) collective-permute-start(bf16[128,512]{1,0:T(8,128)(2,1)S(1)} %get-tuple-element.20), channel_id=1, source_target_pairs={{0,128},{64,192},{128,0},{192,64},{1,129},{65,193},{129,1},{193,65... | collective-permute-start | bytes 393224 | tf_op jit(solution)/shard_map/ppermute | solution.py:44
  49.7 8.4 %collective-permute-start.3 = (bf16[128,512]{1,0:T(8,128)(2,1)S(1)}, bf16[128,512]{1,0:T(8,128)(2,1)S(1)}, u32[]{:S(2)}, u32[]{:S(2)}) collective-permute-start(bf16[128,512]{1,0:T(8,128)(2,1)S(1)} %get-tuple-element.20), channel_id=1, source_target_pairs={{0,64},{64,128},{128,192},{192,0},{1,65},{65,129},{129,193},{193,1... | collective-permute-start | bytes 393224 | tf_op jit(solution)/shard_map/ppermute | solution.py:44
  51.0 12.4 %collective-permute-start.12 = (bf16[208,512]{1,0:T(8,128)(2,1)S(1)}, bf16[208,512]{1,0:T(8,128)(2,1)S(1)}, u32[]{:S(2)}, u32[]{:S(2)}) collective-permute-start(bf16[208,512]{1,0:T(8,128)(2,1)S(1)} %concatenate.47), channel_id=1, source_target_pairs={{0,56},{8,0},{16,8},{24,16},{32,24},{40,32},{48,40},{56,48},{1,57}... | collective-permute-start | bytes 638984 | tf_op jit(solution)/shard_map/ppermute | solution.py:44
  54.2 9.3 %collective-permute-start.16 = (bf16[208,512]{1,0:T(8,128)(2,1)S(1)}, bf16[208,512]{1,0:T(8,128)(2,1)S(1)}, u32[]{:S(2)}, u32[]{:S(2)}) collective-permute-start(bf16[208,512]{1,0:T(8,128)(2,1)S(1)} %concatenate.47), channel_id=1, source_target_pairs={{0,8},{8,16},{16,24},{24,32},{32,40},{40,48},{48,56},{56,0},{1,9},... | collective-permute-start | bytes 638984 | tf_op jit(solution)/shard_map/ppermute | solution.py:44
  58.1 52.9 %collective-permute-start.4 = (bf16[4,128,512]{2,1,0:T(8,128)(2,1)S(1)}, bf16[4,128,512]{2,1,0:T(8,128)(2,1)S(1)}, u32[]{:S(2)}, u32[]{:S(2)}) collective-permute-start(bf16[4,128,512]{2,1,0:T(8,128)(2,1)S(1)} %pad_maximum_fusion.4), channel_id=1, source_target_pairs={{0,56},{8,0},{16,8},{24,16},{32,24},{40,32},{48,40},{56,48},{1,57}... | collective-permute-start | bytes 1572872 | tf_op jit(solution)/shard_map/ppermute | solution.py:44
  58.2 43.3 %collective-permute-start.8 = (bf16[4,128,512]{2,1,0:T(8,128)(2,1)S(1)}, bf16[4,128,512]{2,1,0:T(8,128)(2,1)S(1)}, u32[]{:S(2)}, u32[]{:S(2)}) collective-permute-start(bf16[4,128,512]{2,1,0:T(8,128)(2,1)S(1)} %pad_maximum_fusion.4), channel_id=1, source_target_pairs={{0,8},{8,16},{16,24},{24,32},{32,40},{40,48},{48,56},{56,0},{1,9},... | collective-permute-start | bytes 1572872 | tf_op jit(solution)/shard_map/ppermute | solution.py:44
  62.8 10.1 %collective-permute-start.24 = (f32[32,1280]{1,0:T(8,128)S(1)}, f32[32,1280]{1,0:T(8,128)S(1)}, u32[]{:S(2)}, u32[]{:S(2)}) collective-permute-start(f32[32,1280]{1,0:T(8,128)S(1)} %dynamic-slice_bitcast_fusion.1), channel_id=1, source_target_pairs={{0,2},{2,0},{1,3},{3,1},{4,6},{6,4},{5,7},{7,5},{8,10},{10,8},{9,1... | collective-permute-start | bytes 491528 | tf_op jit(solution)/shard_map/ppermute | solution.py:44
  63.5 16.8 %collective-permute-start.13 = (bf16[208,512]{1,0:T(8,128)(2,1)S(1)}, bf16[208,512]{1,0:T(8,128)(2,1)S(1)}, u32[]{:S(2)}, u32[]{:S(2)}) collective-permute-start(bf16[208,512]{1,0:T(8,128)(2,1)S(1)} %collective-permute-done.12), channel_id=1, source_target_pairs={{0,56},{8,0},{16,8},{24,16},{32,24},{40,32},{48,40},{56,48},{1,57}... | collective-permute-start | bytes 638984 | tf_op jit(solution)/shard_map/ppermute | solution.py:44
  63.5 20.1 %collective-permute-start.17 = (bf16[208,512]{1,0:T(8,128)(2,1)S(1)}, bf16[208,512]{1,0:T(8,128)(2,1)S(1)}, u32[]{:S(2)}, u32[]{:S(2)}) collective-permute-start(bf16[208,512]{1,0:T(8,128)(2,1)S(1)} %collective-permute-done.16), channel_id=1, source_target_pairs={{0,8},{8,16},{16,24},{24,32},{32,40},{40,48},{48,56},{56,0},{1,9},... | collective-permute-start | bytes 638984 | tf_op jit(solution)/shard_map/ppermute | solution.py:44
  73.4 6.3 %collective-permute-start.25 = (bf16[32,1280]{1,0:T(8,128)(2,1)S(1)}, bf16[32,1280]{1,0:T(8,128)(2,1)S(1)}, u32[]{:S(2)}, u32[]{:S(2)}) collective-permute-start(bf16[32,1280]{1,0:T(8,128)(2,1)S(1)} %multiply_convert_fusion), channel_id=1, source_target_pairs={{0,8},{8,16},{16,24},{24,32},{32,40},{40,48},{48,56},{56,64},{64,7... | collective-permute-start | bytes 245768 | tf_op jit(solution)/shard_map/ppermute | solution.py:48
  79.8 11.6 %collective-permute-start.26 = (bf16[2,32,1280]{2,1,0:T(8,128)(2,1)S(1)}, bf16[2,32,1280]{2,1,0:T(8,128)(2,1)S(1)}, u32[]{:S(2)}, u32[]{:S(2)}) collective-permute-start(bf16[2,32,1280]{2,1,0:T(8,128)(2,1)S(1)} %get-tuple-element.22), channel_id=1, source_target_pairs={{0,6},{2,0},{4,2},{6,4},{1,7},{3,1},{5,3},{7,5},{8,14},{10,8},{12,... | collective-permute-start | bytes 491528 | tf_op jit(solution)/shard_map/ppermute | solution.py:44
  80.3 17.9 %collective-permute-start.27 = (bf16[2,32,1280]{2,1,0:T(8,128)(2,1)S(1)}, bf16[2,32,1280]{2,1,0:T(8,128)(2,1)S(1)}, u32[]{:S(2)}, u32[]{:S(2)}) collective-permute-start(bf16[2,32,1280]{2,1,0:T(8,128)(2,1)S(1)} %get-tuple-element.22), channel_id=1, source_target_pairs={{0,4},{2,6},{4,0},{6,2},{1,5},{3,7},{5,1},{7,3},{8,12},{10,14},{12... | collective-permute-start | bytes 491528 | tf_op jit(solution)/shard_map/ppermute | solution.py:44
  83.6 18.2 %collective-permute-start.28 = (bf16[2,32,1280]{2,1,0:T(8,128)(2,1)S(1)}, bf16[2,32,1280]{2,1,0:T(8,128)(2,1)S(1)}, u32[]{:S(2)}, u32[]{:S(2)}) collective-permute-start(bf16[2,32,1280]{2,1,0:T(8,128)(2,1)S(1)} %get-tuple-element.22), channel_id=1, source_target_pairs={{0,2},{2,4},{4,6},{6,0},{1,3},{3,5},{5,7},{7,1},{8,10},{10,12},{12... | collective-permute-start | bytes 491528 | tf_op jit(solution)/shard_map/ppermute | solution.py:44
  91.4 10.6 %collective-permute-start.14 = (bf16[208,512]{1,0:T(8,128)(2,1)S(1)}, bf16[208,512]{1,0:T(8,128)(2,1)S(1)}, u32[]{:S(2)}, u32[]{:S(2)}) collective-permute-start(bf16[208,512]{1,0:T(8,128)(2,1)S(1)} %collective-permute-done.13), channel_id=1, source_target_pairs={{0,56},{8,0},{16,8},{24,16},{32,24},{40,32},{48,40},{56,48},{1,57}... | collective-permute-start | bytes 638984 | tf_op jit(solution)/shard_map/ppermute | solution.py:44
  98.2 9.0 %collective-permute-start.18 = (bf16[208,512]{1,0:T(8,128)(2,1)S(1)}, bf16[208,512]{1,0:T(8,128)(2,1)S(1)}, u32[]{:S(2)}, u32[]{:S(2)}) collective-permute-start(bf16[208,512]{1,0:T(8,128)(2,1)S(1)} %collective-permute-done.17), channel_id=1, source_target_pairs={{0,8},{8,16},{16,24},{24,32},{32,40},{40,48},{48,56},{56,0},{1,9},... | collective-permute-start | bytes 638984 | tf_op jit(solution)/shard_map/ppermute | solution.py:44
  101.5 16.3 %collective-permute-start.9 = (bf16[4,128,512]{2,1,0:T(8,128)(2,1)S(1)}, bf16[4,128,512]{2,1,0:T(8,128)(2,1)S(1)}, u32[]{:S(2)}, u32[]{:S(2)}) collective-permute-start(bf16[4,128,512]{2,1,0:T(8,128)(2,1)S(1)} %collective-permute-done.8), channel_id=1, source_target_pairs={{0,8},{8,16},{16,24},{24,32},{32,40},{40,48},{48,56},{56,0},{1,9},... | collective-permute-start | bytes 1572872 | tf_op jit(solution)/shard_map/ppermute | solution.py:44
  101.9 43.7 %collective-permute-start.29 = (bf16[4,2,32,1280]{3,2,1,0:T(8,128)(2,1)S(1)}, bf16[4,2,32,1280]{3,2,1,0:T(8,128)(2,1)S(1)}, u32[]{:S(2)}, u32[]{:S(2)}) collective-permute-start(bf16[4,2,32,1280]{3,2,1,0:T(8,128)(2,1)S(1)} %get-tuple-element.12), channel_id=1, source_target_pairs={{0,1},{1,0},{2,3},{3,2},{4,5},{5,4},{6,7},{7,6},{8,9},{9,8},{10,11... | collective-permute-start | bytes 1966088 | tf_op jit(solution)/shard_map/ppermute | solution.py:44
  102.0 9.1 %collective-permute-start.15 = (bf16[104,512]{1,0:T(8,128)(2,1)S(1)}, bf16[104,512]{1,0:T(8,128)(2,1)S(1)}, u32[]{:S(2)}, u32[]{:S(2)}) collective-permute-start(bf16[104,512]{1,0:T(8,128)(2,1)S(1)} %slice.72), channel_id=1, source_target_pairs={{0,56},{8,0},{16,8},{24,16},{32,24},{40,32},{48,40},{56,48},{1,57}... | collective-permute-start | bytes 319496 | tf_op jit(solution)/shard_map/ppermute | solution.py:44
  107.2 10.5 %collective-permute-start.19 = (bf16[104,512]{1,0:T(8,128)(2,1)S(1)}, bf16[104,512]{1,0:T(8,128)(2,1)S(1)}, u32[]{:S(2)}, u32[]{:S(2)}) collective-permute-start(bf16[104,512]{1,0:T(8,128)(2,1)S(1)} %slice.73), channel_id=1, source_target_pairs={{0,8},{8,16},{16,24},{24,32},{32,40},{40,48},{48,56},{56,0},{1,9},... | collective-permute-start | bytes 319496 | tf_op jit(solution)/shard_map/ppermute | solution.py:44
  111.0 22.3 %collective-permute-start.5 = (bf16[4,128,512]{2,1,0:T(8,128)(2,1)S(1)}, bf16[4,128,512]{2,1,0:T(8,128)(2,1)S(1)}, u32[]{:S(2)}, u32[]{:S(2)}) collective-permute-start(bf16[4,128,512]{2,1,0:T(8,128)(2,1)S(1)} %collective-permute-done.4), channel_id=1, source_target_pairs={{0,56},{8,0},{16,8},{24,16},{32,24},{40,32},{48,40},{56,48},{1,57}... | collective-permute-start | bytes 1572872 | tf_op jit(solution)/shard_map/ppermute | solution.py:44
  117.8 23.9 %collective-permute-start.10 = (bf16[4,128,512]{2,1,0:T(8,128)(2,1)S(1)}, bf16[4,128,512]{2,1,0:T(8,128)(2,1)S(1)}, u32[]{:S(2)}, u32[]{:S(2)}) collective-permute-start(bf16[4,128,512]{2,1,0:T(8,128)(2,1)S(1)} %collective-permute-done.9), channel_id=1, source_target_pairs={{0,8},{8,16},{16,24},{24,32},{32,40},{40,48},{48,56},{56,0},{1,9},... | collective-permute-start | bytes 1572872 | tf_op jit(solution)/shard_map/ppermute | solution.py:44
  133.3 12.0 %collective-permute-start.6 = (bf16[4,128,512]{2,1,0:T(8,128)(2,1)S(1)}, bf16[4,128,512]{2,1,0:T(8,128)(2,1)S(1)}, u32[]{:S(2)}, u32[]{:S(2)}) collective-permute-start(bf16[4,128,512]{2,1,0:T(8,128)(2,1)S(1)} %collective-permute-done.5), channel_id=1, source_target_pairs={{0,56},{8,0},{16,8},{24,16},{32,24},{40,32},{48,40},{56,48},{1,57}... | collective-permute-start | bytes 1572872 | tf_op jit(solution)/shard_map/ppermute | solution.py:44
  133.4 73.0 %collective-permute-start.20 = (bf16[8,208,512]{2,1,0:T(8,128)(2,1)S(1)}, bf16[8,208,512]{2,1,0:T(8,128)(2,1)S(1)}, u32[]{:S(2)}, u32[]{:S(2)}) collective-permute-start(bf16[8,208,512]{2,1,0:T(8,128)(2,1)S(1)} %bitcast_dynamic-update-slice_fusion.7), channel_id=1, source_target_pairs={{0,192},{64,0},{128,64},{192,128},{1,193},{65,1},{129,65},{193,129... | collective-permute-start | bytes 5111816 | tf_op jit(solution)/shard_map/ppermute | solution.py:44
  136.8 69.6 %collective-permute-start.21 = (bf16[8,208,512]{2,1,0:T(8,128)(2,1)S(1)}, bf16[8,208,512]{2,1,0:T(8,128)(2,1)S(1)}, u32[]{:S(2)}, u32[]{:S(2)}) collective-permute-start(bf16[8,208,512]{2,1,0:T(8,128)(2,1)S(1)} %bitcast_dynamic-update-slice_fusion.7), channel_id=1, source_target_pairs={{0,128},{64,192},{128,0},{192,64},{1,129},{65,193},{129,1},{193,65... | collective-permute-start | bytes 5111816 | tf_op jit(solution)/shard_map/ppermute | solution.py:44
  141.7 68.4 %collective-permute-start.22 = (bf16[8,208,512]{2,1,0:T(8,128)(2,1)S(1)}, bf16[8,208,512]{2,1,0:T(8,128)(2,1)S(1)}, u32[]{:S(2)}, u32[]{:S(2)}) collective-permute-start(bf16[8,208,512]{2,1,0:T(8,128)(2,1)S(1)} %bitcast_dynamic-update-slice_fusion.7), channel_id=1, source_target_pairs={{0,64},{64,128},{128,192},{192,0},{1,65},{65,129},{129,193},{193,1... | collective-permute-start | bytes 5111816 | tf_op jit(solution)/shard_map/ppermute | solution.py:44
  145.2 6.4 %collective-permute-start.11 = (bf16[2,128,512]{2,1,0:T(8,128)(2,1)S(1)}, bf16[2,128,512]{2,1,0:T(8,128)(2,1)S(1)}, u32[]{:S(2)}, u32[]{:S(2)}) collective-permute-start(bf16[2,128,512]{2,1,0:T(8,128)(2,1)S(1)} %slice.66), channel_id=1, source_target_pairs={{0,8},{8,16},{16,24},{24,32},{32,40},{40,48},{48,56},{56,0},{1,9},... | collective-permute-start | bytes 786440 | tf_op jit(solution)/shard_map/ppermute | solution.py:44
  145.6 7.7 %collective-permute-start.7 = (bf16[2,128,512]{2,1,0:T(8,128)(2,1)S(1)}, bf16[2,128,512]{2,1,0:T(8,128)(2,1)S(1)}, u32[]{:S(2)}, u32[]{:S(2)}) collective-permute-start(bf16[2,128,512]{2,1,0:T(8,128)(2,1)S(1)} %slice.65), channel_id=1, source_target_pairs={{0,56},{8,0},{16,8},{24,16},{32,24},{40,32},{48,40},{56,48},{1,57}... | collective-permute-start | bytes 786440 | tf_op jit(solution)/shard_map/ppermute | solution.py:44
  211.0 2.8 %copy-start.4 = (bf16[4,8,208,512]{3,2,1,0:T(8,128)(2,1)}, bf16[4,8,208,512]{3,2,1,0:T(8,128)(2,1)S(1)}, u32[]{:S(2)}) copy-start(bf16[4,8,208,512]{3,2,1,0:T(8,128)(2,1)S(1)} %pad_maximum_fusion) | copy-start | bytes 20447236
  239.0 3.4 %copy-start.2 = (bf16[4,8,256,512]{3,2,1,0:T(8,128)(2,1)S(1)}, bf16[4,8,256,512]{3,2,1,0:T(8,128)(2,1)}, u32[]{:S(2)}) copy-start(bf16[4,8,256,512]{3,2,1,0:T(8,128)(2,1)} %fusion.1) | copy-start | bytes 25165828
  242.4 11.8 %copy-start.3 = (bf16[4,8,256,512]{3,2,1,0:T(8,128)(2,1)S(1)}, bf16[4,8,256,512]{3,2,1,0:T(8,128)(2,1)}, u32[]{:S(2)}) copy-start(bf16[4,8,256,512]{3,2,1,0:T(8,128)(2,1)} %fusion.1) | copy-start | bytes 25165828
  253.3 15.6 %collective-permute-start.31 = (bf16[512,512]{1,0:T(8,128)(2,1)S(1)}, bf16[512,512]{1,0:T(8,128)(2,1)S(1)}, u32[]{:S(2)}, u32[]{:S(2)}) collective-permute-start(bf16[512,512]{1,0:T(8,128)(2,1)S(1)} %shard_map.164), channel_id=1, source_target_pairs={{0,4},{4,0},{1,5},{5,1},{2,6},{6,2},{3,7},{7,3},{8,12},{12,8},{9,1... | collective-permute-start | bytes 1572872 | tf_op jit(solution)/shard_map/ppermute | solution.py:44
  254.2 16.1 %copy-start.1 = (bf16[1280,384]{1,0:T(8,128)(2,1)S(1)}, bf16[1280,384]{1,0:T(8,128)(2,1)}, u32[]{:S(2)}) copy-start(bf16[1280,384]{1,0:T(8,128)(2,1)} %param.31) | copy-start | bytes 2949124
  (7 other events, 12.5 us)
Sparse Core Ops, SparseCore 0:
  11.1 98.1 all-gather.4

commit v2 on v1

v2 whole, which is shorter than its diff:
```python
import functools

import jax
import jax.numpy as jnp
from jax import lax
from jax.experimental import pallas as pl
from jax.experimental.pallas import tpu as pltpu
from jax.sharding import Mesh, PartitionSpec as P

D = 8192
HD = 128
RHD = 96
LAT = 64
PATCH = 256
VW = 1280

EPS_TEXT = 1e-06
EPS_VISION = 1e-05
FILL = -1e30
LOG2E = 1.4426950408889634

NY, NZ, NX = 4, 8, 4
TOK = 512
COLS = 512
KEYS = 512
ROWS = 128


def layer_norm(values, gain):
    middle = jnp.mean(values, axis=-1, keepdims=True)
    centred = values - middle
    spread = jnp.mean(centred * centred, axis=-1, keepdims=True)
    return centred * lax.rsqrt(spread + EPS_VISION) * gain


def masked_softmax(scores, allowed):
    highest = jnp.max(jnp.where(allowed, scores, FILL), axis=-1, keepdims=True)
    weights = jnp.where(allowed, jnp.exp(scores - highest), 0.0)
    summed = jnp.sum(weights, axis=-1, keepdims=True)
    anything = jnp.any(allowed, axis=-1, keepdims=True)
    return (weights / jnp.where(anything, summed, 1.0)).astype(jnp.bfloat16)


def turned(x, axis, by, count):
    return lax.ppermute(x, axis, [(i, (i + by) % count) for i in range(count)])


def next_pair(x):
    return lax.ppermute(x, ("y", "z"), [(i, i + 1) for i in range(NY * NZ - 1)])


def after(x, *others):
    return lax.optimization_barrier((x, others))[0]


def flipped(x, axes):
    count = 2 ** len(axes)
    return lax.ppermute(x, axes, [(i, count - 1 - i) for i in range(count)])


AHEAD = 2


def attend_kernel(counts, fresh, *refs):
    refs = list(refs)
    take = lambda count: [refs.pop(0) for _ in range(count)]
    where_ref, gain_ref, scale_ref, bound_ref = take(4)
    if fresh:
        (rows_ref,) = take(1)
    else:
        key_ref, value_ref = take(2)
    (weight_ref,) = take(1)
    blocks = [take(count) for count in counts]
    (out_ref,) = take(1)
    if fresh:
        key_ref, value_ref = take(2)
        pair_sem, side_buf, pair_buf = refs.pop(), refs.pop(), refs.pop()
    text_buf, weight_buf, acc_ref, text_sem, weight_sem = refs

    def fetch(k):
        height = TOK // len(blocks[k])
        for j, ref in enumerate(blocks[k]):
            pltpu.make_async_copy(ref, text_buf.at[k, pl.ds(j * height, height), :], text_sem.at[k]).start()
        pltpu.make_async_copy(
            weight_ref.at[pl.ds(where_ref[1 + k] * NZ, NZ), pl.ds(0, 2 * ROWS), :], weight_buf.at[k], weight_sem.at[k]
        ).start()

    for k in range(AHEAD):
        fetch(k)
    if fresh:
        count = pair_buf.shape[1]
        pltpu.make_async_copy(weight_ref.at[:, pl.ds(2 * ROWS, count), :], pair_buf, pair_sem.at[0]).start()
    for k in range(NY):
        pltpu.make_async_copy(text_buf.at[k], text_buf.at[k], text_sem.at[k]).wait()
        pltpu.make_async_copy(weight_buf.at[k], weight_buf.at[k], weight_sem.at[k]).wait()
        if k + AHEAD < NY:
            fetch(k + AHEAD)
        part = jnp.dot(
            text_buf[k] * gain_ref[where_ref[1 + NY + k]],
            weight_buf[k].reshape(D // NY, COLS),
            preferred_element_type=jnp.float32,
        )
        acc_ref[...] = part if k == 0 else acc_ref[...] + part
        if fresh and k == 1:
            pltpu.make_async_copy(pair_buf, pair_buf, pair_sem.at[0]).wait()
            half = pair_buf.shape[1] // 2
            tall = NZ * half

            @pl.loop(0, NY)
            def _(group):
                rows = pair_buf[pl.ds(group * NZ, NZ)].astype(jnp.float32)
                start = pl.multiple_of(group * tall, tall)
                for i in range(2):
                    side = rows[:, i * half : (i + 1) * half].reshape(tall, COLS)
                    side_buf[i, pl.ds(start, tall), :] = side.astype(jnp.bfloat16)

            for i, ref in enumerate((key_ref, value_ref)):
                ref[...] = jnp.dot(
                    rows_ref[...], side_buf[i], preferred_element_type=jnp.float32
                ).astype(jnp.bfloat16)

    position = where_ref[0] + lax.broadcasted_iota(jnp.int32, (TOK, KEYS), 0)
    seen = (position >= bound_ref[0:1, :]) & (position < bound_ref[1:2, :])
    anything = jnp.any(seen, axis=-1, keepdims=True)
    hidden = jnp.where(seen, 0.0, FILL)
    for head in range(COLS // HD):
        cols = pl.ds(head * HD, HD)
        queries = (acc_ref[:, cols] * scale_ref[...]).astype(jnp.bfloat16)
        scores = lax.dot_general(
            queries, key_ref[:, cols], (((1,), (1,)), ((), ())), preferred_element_type=jnp.float32
        )
        scores = scores * (HD ** (-0.5) * LOG2E) + hidden
        highest = jnp.max(scores, axis=-1, keepdims=True)
        weights = jnp.exp2(scores - highest)
        summed = jnp.sum(weights, axis=-1, keepdims=True)
        probs = (weights * jnp.where(anything, 1.0 / summed, 0.0)).astype(jnp.bfloat16)
        out_ref[:, cols] = jnp.dot(
            probs, value_ref[:, cols], preferred_element_type=jnp.float32
        ).astype(jnp.bfloat16)


def attend(blocks, where, gain, scale, bounds, rows, weight):
    fresh = len(rows) == 1
    counts = tuple(len(refs) for refs in blocks)
    vmem = pl.BlockSpec(memory_space=pltpu.VMEM)
    anywhere = pl.BlockSpec(memory_space=pl.ANY)
    result = jax.ShapeDtypeStruct((TOK, COLS), jnp.bfloat16)
    pairs = weight.shape[1] - 2 * ROWS
    return pl.pallas_call(
        functools.partial(attend_kernel, counts, fresh),
        out_shape=[result] * (3 if fresh else 1),
        in_specs=[pl.BlockSpec(memory_space=pltpu.SMEM)] + [vmem] * (3 + len(rows)) + [anywhere] * (1 + sum(counts)),
        out_specs=[vmem] * (3 if fresh else 1),
        scratch_shapes=[
            pltpu.VMEM((NY, TOK, D // NY), jnp.bfloat16),
            pltpu.VMEM((NY, NZ, 2 * ROWS, COLS), jnp.bfloat16),
            pltpu.VMEM((TOK, COLS), jnp.float32),
            pltpu.SemaphoreType.DMA((NY,)),
            pltpu.SemaphoreType.DMA((NY,)),
        ]
        + (
            [
                pltpu.VMEM((NY * NZ, pairs, COLS), jnp.bfloat16),
                pltpu.VMEM((2, VW, COLS), jnp.bfloat16),
                pltpu.SemaphoreType.DMA((1,)),
            ]
            if fresh
            else []
        ),
        compiler_params=pltpu.CompilerParams(vmem_limit_bytes=56 * 1024 * 1024),
        cost_estimate=pl.CostEstimate(
            flops=2 * TOK * COLS * (D + 2 * KEYS), bytes_accessed=18 << 20, transcendentals=TOK * KEYS * 4
        ),
    )(where, gain, scale, bounds, *rows, weight, *(ref for refs in blocks for ref in refs))


def resample(images, patch_counts, latents, latent_gain, context_gain, res_query, res_key, res_value, res_output):
    slot_count = images.shape[0]
    res_local = res_query.shape[1] // RHD
    latent_base = latents.astype(jnp.float32)
    latent_normed = layer_norm(latent_base, latent_gain.astype(jnp.float32)).astype(jnp.bfloat16)
    latent_queries = (
        jnp.dot(latent_normed, res_query, preferred_element_type=jnp.float32)
        .astype(jnp.bfloat16)
        .reshape(LAT, res_local, RHD)
    )
    context_normed = layer_norm(
        images.astype(jnp.float32), context_gain.astype(jnp.float32)
    ).astype(jnp.bfloat16)
    patch_keys = jnp.einsum(
        "cpf,fe->cpe", context_normed, res_key, preferred_element_type=jnp.float32
    ).astype(jnp.bfloat16)
    patch_values = jnp.einsum(
        "cpf,fe->cpe", context_normed, res_value, preferred_element_type=jnp.float32
    ).astype(jnp.bfloat16)
    latent_keys = jnp.dot(latent_normed, res_key, preferred_element_type=jnp.float32).astype(
        jnp.bfloat16
    )
    latent_values = jnp.dot(latent_normed, res_value, preferred_element_type=jnp.float32).astype(
        jnp.bfloat16
    )
    res_keys = jnp.concatenate(
        [patch_keys, jnp.broadcast_to(latent_keys[None], (slot_count, LAT, latent_keys.shape[1]))],
        axis=1,
    ).reshape(slot_count, PATCH + LAT, res_local, RHD)
    res_values = jnp.concatenate(
        [
            patch_values,
            jnp.broadcast_to(latent_values[None], (slot_count, LAT, latent_values.shape[1])),
        ],
        axis=1,
    ).reshape(slot_count, PATCH + LAT, res_local, RHD)
    res_scores = jnp.einsum(
        "qhd,ckhd->chqk", latent_queries, res_keys, preferred_element_type=jnp.float32
    ) * RHD ** (-0.5)
    key_rows = jnp.arange(PATCH + LAT, dtype=jnp.int32)
    patch_allowed = (key_rows[None, :] < patch_counts[:, None]) | (key_rows[None, :] >= PATCH)
    res_probs = masked_softmax(res_scores, patch_allowed[:, None, None, :])
    res_heads = (
        jnp.einsum("chqk,ckhd->cqhd", res_probs, res_values, preferred_element_type=jnp.float32)
        .astype(jnp.bfloat16)
        .reshape(slot_count, LAT, res_local * RHD)
    )
    return jnp.einsum("cqe,ef->cqf", res_heads, res_output, preferred_element_type=jnp.float32)


def local(
    text_rows,
    text_gain,
    query_weight,
    key_weight,
    value_weight,
    images,
    patch_counts,
    image_counts,
    image_spans,
    latents,
    latent_gain,
    context_gain,
    final_gain,
    res_query,
    res_key,
    res_value,
    res_output,
):
    y, z = lax.axis_index("y"), lax.axis_index("z")
    xh, xl, core = lax.axis_index("xh"), lax.axis_index("xl"), lax.axis_index("core")
    x = xh * 2 + xl

    block = jnp.concatenate([query_weight, key_weight, value_weight], axis=0)
    mine = lax.dynamic_slice_in_dim(block, xh * COLS, COLS, 1)
    other = flipped(lax.dynamic_slice_in_dim(block, (1 - xh) * COLS, COLS, 1), ("xh",))
    low = jnp.where(xh == 0, mine, other)
    high = jnp.where(xh == 0, other, mine)
    part = key_weight.shape[0]
    pairs = jnp.concatenate([low[ROWS:], high[ROWS:]], axis=0)
    order = jnp.arange(4 * part, dtype=jnp.int32)
    block_of = jnp.asarray([0, 2, 1, 3], jnp.int32)[order // part] * part + order % part
    pairs = jnp.dot(
        (block_of[:, None] == order[None, :]).astype(jnp.bfloat16), pairs, preferred_element_type=jnp.float32
    ).astype(jnp.bfloat16)
    weight = lax.all_gather(jnp.concatenate([low[:ROWS], high[:ROWS], pairs], axis=0), ("y", "z"), axis=0)

    source = text_rows.astype(jnp.float32)
    power = jnp.sum(source * source, axis=-1)
    live_slot = jnp.arange(2, dtype=jnp.int32) < image_counts[0]
    span_bounds = jnp.where(live_slot[None, :], image_spans, 0)
    small = jnp.concatenate(
        [
            power,
            text_gain.astype(jnp.float32),
            span_bounds.reshape(4).astype(jnp.float32),
            next_pair(span_bounds.reshape(4).astype(jnp.float32)),
            jnp.zeros((120,), jnp.float32),
        ]
    )

    mix = resample(
        images, patch_counts, latents, latent_gain, context_gain, res_query, res_key, res_value, res_output
    ).reshape(2, 2, LAT // 2, VW)
    small = small[None]
    first = lax.dynamic_index_in_dim(mix, core, 1, keepdims=False)
    first = first + turned(lax.dynamic_index_in_dim(mix, 1 - core, 1, keepdims=False), "core", 1, 2)
    small = jnp.concatenate([small, flipped(small, ("core",))], axis=0)
    first, small = lax.optimization_barrier((first, small))
    total = lax.dynamic_index_in_dim(first, xl, 0, keepdims=False)
    total = total + turned(lax.dynamic_index_in_dim(first, 1 - xl, 0, keepdims=False), "xl", 1, 2)
    small = jnp.concatenate([small, flipped(small, ("xl",))], axis=0)
    total, small = lax.optimization_barrier((total, small))
    short = jnp.concatenate([jnp.sum(small[:, :TOK], axis=0), small[0, TOK + D // NY :]])
    short_other = flipped(short, ("xh",))

    text_out = after(text_rows, other, total)
    near_text, cross_text = flipped(text_out, ("xl",)), flipped(text_out, ("xh", "xl"))
    cut = TOK // 2
    text_top = flipped(cross_text[:cut], ("xl",))
    text_bottom = flipped(near_text[cut:], ("xh", "xl"))
    base = lax.dynamic_slice_in_dim(latents, core * (LAT // 2), LAT // 2, 0).astype(jnp.float32)
    piece = layer_norm(base + total, final_gain.astype(jnp.float32)).astype(jnp.bfloat16)
    both = jnp.stack([next_pair(piece), piece])

    swap = lambda rows: flipped(rows, ("core",))
    our_blocks = [[text_rows], [swap(text_rows)], [near_text], [swap(near_text)]]
    their_blocks = [[cross_text], [swap(cross_text)], [text_top, text_bottom], [swap(text_top), swap(text_bottom)]]
    scales = [lax.rsqrt(one[:TOK] / D + EPS_TEXT).reshape(TOK, 1) for one in (short, short_other)]
    gain = small[:, TOK : TOK + D // NY].astype(jnp.bfloat16).reshape(NY, 1, D // NY)
    spans = [one[TOK : TOK + 8].reshape(2, 2, 2) for one in (short, short_other)]
    spans = jnp.where(xh == 0, jnp.concatenate(spans, axis=2), jnp.concatenate(spans[::-1], axis=2))
    near = jnp.stack([spans[1], spans[0]], axis=1)
    near = jnp.take(near, x ^ jnp.arange(NX), axis=2).transpose(0, 2, 1).reshape(2, 8).astype(jnp.int32)
    bounds = jnp.repeat(near, LAT, axis=1)

    both = jnp.stack([both, flipped(both, ("xl",))])
    both = jnp.stack([both, flipped(both, ("xh",))])
    around = jnp.stack([both[0, 0], both[0, 1], both[1, 0], both[1, 1]])
    around = after(around, text_top, text_bottom)
    resampled = jnp.stack([around, turned(around, "core", 1, 2)], axis=2).reshape(KEYS, VW)

    def half(blocks, which, own_scale, others, rows):
        places = [2 * p + q for p, q in ((others, core), (others, 1 - core), (1 - others, core), (1 - others, 1 - core))]
        turns = [place ^ (2 * xl + core) for place in places]
        where = jnp.stack([(y * NZ + z) * (2 * TOK) + which * TOK, *places, *turns]).astype(jnp.int32)
        return attend(blocks, where, gain, own_scale, bounds, rows, weight)

    theirs, keys, values = half(their_blocks, 1 - xh, scales[1], 1 - xl, (resampled,))
    received = flipped(theirs, ("xh",))
    (ours,) = half(our_blocks, xh, scales[0], xl, (keys, values))
    return jnp.where(
        xh == 0,
        jnp.concatenate([ours, received], axis=1),
        jnp.concatenate([received, ours], axis=1),
    )


def solution(mesh):
    fine = Mesh(mesh.devices.reshape(NY, NZ, 2, 2, 2), ("y", "z", "xh", "xl", "core"))
    seq = ("y", "z", "xh")
    head = ("xl", "core")
    return jax.shard_map(
        local,
        mesh=fine,
        in_specs=(
            P(seq, head),
            P(head),
            P(seq, head),
            P(seq, head),
            P(seq, head),
            P(seq, None, None),
            P(seq),
            P(seq),
            P(None, seq),
            P(),
            P(),
            P(),
            P(),
            P(None, head),
            P(None, head),
            P(None, head),
            P(head, None),
        ),
        out_specs=P(seq, head),
        check_vma=False,
    )
```

time: 281 us -> 191 us (0.68)
  the two profiles are of different devices: /device:TPU:102 before, /device:TPU:24 now
where the time goes in v2:
time: 191 us; the launch traced here: 190 us
  waiting for transfers between devices  90.3 us (47%)
  Pallas kernels  26 us (14%)
  starting transfers between devices  23.9 us (13%)
  between operations  14.6 us (8%)
  local copies, waits for them, and re-layouts  14 us (7%)
  other arithmetic  12.5 us (7%)
  matrix products  8.92 us (5%)
    ppermute x16, waiting for transfers between devices, flipped(): return lax.ppermute(x, axes, [(i, count - 1 - i) for i in range(count)])  74.8 us
    pallas_call x2, Pallas kernels, attend(): pl.pallas_call(functools.partial(attend_kernel, counts, fresh), out_shape...  26 us
    ppermute x16, starting transfers between devices, flipped(): return lax.ppermute(x, axes, [(i, count - 1 - i) for i in range(count)])  17.5 us
    ppermute x2, waiting for transfers between devices, next_pair(): return lax.ppermute(x, ('y', 'z'), [(i, i + 1) for i in range(NY * NZ - 1)])  11.4 us
    ppermute x2, starting transfers between devices, next_pair(): return lax.ppermute(x, ('y', 'z'), [(i, i + 1) for i in range(NY * NZ - 1)])  5.73 us
    ppermute x3, waiting for transfers between devices, turned(): return lax.ppermute(x, axis, [(i, (i + by) % count) for i in range(count)])  4.06 us
  transfers between devices with their start and end apart: 22, of which 11 were waited for; matrix products, arithmetic and copies ran while one was open for 15% of the time, Pallas kernels for 14%

profile of v2, /device:TPU:24, one launch (start us, length us, event | category | flops | bytes accessed | tf_op | source)
XLA Modules:
  0.0 190.3 jit_solution(7531398498187415948)
XLA Ops:
  6.6 1.2 pad_maximum_fusion.4
  7.8 3.1 %collective-permute-start.9 = (bf16[168,512]{1,0:T(8,128)(2,1)S(1)}, bf16[168,512]{1,0:T(8,128)(2,1)S(1)}, u32[]{:S(2)}, u32[]{:S(2)}) collective-permute-start(bf16[168,512]{1,0:T(8,128)(2,1)S(1)} %constant_dynamic-slice_fusion), channel_id=1, source_target_pairs={{0,4},{4,0},{1,5},{5,1},{2,6},{6,2},{3,7},{7,3},{8,12},{12,8},{9,1... | collective-permute-start | bytes 516104 | tf_op jit(solution)/shard_map/ppermute | solution.py:58
  10.9 4.6 %collective-permute-done.9 = bf16[168,512]{1,0:T(8,128)(2,1)S(1)} collective-permute-done((bf16[168,512]{1,0:T(8,128)(2,1)S(1)}, bf16[168,512]{1,0:T(8,128)(2,1)S(1)}, u32[]{:S(2)}, u32[]{:S(2)}) %collective-permute-start.9) | collective-permute-done | bytes 172064 | tf_op jit(solution)/shard_map/ppermute | solution.py:58
  15.9 0.8 pad_maximum_fusion.5
  18.2 0.9 convolution_convert_fusion
  19.1 0.8 pad_maximum_fusion.3
  20.0 1.3 copy.40
  21.3 1.5 convolution_convert_fusion.4
  22.9 1.5 convolution_convert_fusion.6
  24.5 2.1 %convolution_convert_fusion.1 = bf16[2,256,384]{2,1,0:T(8,128)(2,1)S(1)} fusion(bf16[1280,384]{1,0:T(8,128)(2,1)} %param.33, bf16[2,256,1280]{2,1,0:T(8,128)(2,1)S(1)} %copy-done.3, f32[1280]{0:T(1024)S(1)} %convert_element_type.79, f32[2,256]{1,0:T(2,128)S(1)} %add_rsqrt_fusion.2, f32[2,256]{1,0:T(2,128)S(1)} %broadcast_multiply_fusion), kind=kOutput, calls=%fused_computation.17 | convolution fusion | flops 506789888 | bytes 2696192 | tf_op jit(solution)/shard_map/cpf,fe->cpe/dot_general | solution.py:193
  26.7 1.1 copy.39
  29.5 1.7 fusion.12
  31.2 0.8 copy-done.4
  32.1 0.8 dynamic-slice_bitcast_fusion
  33.6 3.8 %collective-permute-start.1 = (f32[4]{0:T(128)S(1)}, f32[4]{0:T(128)S(1)}, u32[]{:S(2)}, u32[]{:S(2)}) collective-permute-start(f32[4]{0:T(128)S(1)} %convert_element_type.95), channel_id=1, source_target_pairs={{0,8},{8,16},{16,24},{24,32},{32,40},{40,48},{48,56},{56,64},{64,7... | collective-permute-start | bytes 56 | tf_op jit(solution)/shard_map/ppermute | solution.py:49
  38.2 4.9 %collective-permute-done.1 = f32[4]{0:T(128)S(1)} collective-permute-done((f32[4]{0:T(128)S(1)}, f32[4]{0:T(128)S(1)}, u32[]{:S(2)}, u32[]{:S(2)}) %collective-permute-start.1) | collective-permute-done | bytes 48 | tf_op jit(solution)/shard_map/ppermute | solution.py:49
  43.4 0.7 stack.92.refs_0_
  44.1 0.7 stack.89.refs_0_
  44.8 1.1 bitcast_add_fusion
  45.9 1.6 collective-permute-start.4
  48.1 1.7 collective-permute-done.4
  49.8 4.1 %collective-permute-done.3 = f32[32,1280]{1,0:T(8,128)S(1)} collective-permute-done((f32[32,1280]{1,0:T(8,128)S(1)}, f32[32,1280]{1,0:T(8,128)S(1)}, u32[]{:S(2)}, u32[]{:S(2)}) %collective-permute-start.3) | collective-permute-done | bytes 163872 | tf_op jit(solution)/shard_map/ppermute | solution.py:45
  53.9 2.3 %collective-permute-start.10 = (bf16[512,2048]{1,0:T(8,128)(2,1)S(1)}, bf16[512,2048]{1,0:T(8,128)(2,1)}, u32[]{:S(2)}, u32[]{:S(2)}) collective-permute-start(bf16[512,2048]{1,0:T(8,128)(2,1)S(1)} %copy-done.1), channel_id=1, source_target_pairs={{0,6},{2,4},{4,2},{6,0},{1,7},{3,5},{5,3},{7,1},{8,14},{10,12},{12... | collective-permute-start | bytes 6291464 | tf_op jit(solution)/shard_map/ppermute | solution.py:58
  57.1 1.9 %collective-permute-start.6 = (bf16[32,1280]{1,0:T(8,128)(2,1)S(1)}, bf16[32,1280]{1,0:T(8,128)(2,1)S(1)}, u32[]{:S(2)}, u32[]{:S(2)}) collective-permute-start(bf16[32,1280]{1,0:T(8,128)(2,1)S(1)} %multiply_convert_fusion), channel_id=1, source_target_pairs={{0,8},{8,16},{16,24},{24,32},{32,40},{40,48},{48,56},{56,64},{64,7... | collective-permute-start | bytes 245768 | tf_op jit(solution)/shard_map/ppermute | solution.py:49
  59.1 6.5 %collective-permute-done.6 = bf16[32,1280]{1,0:T(8,128)(2,1)S(1)} collective-permute-done((bf16[32,1280]{1,0:T(8,128)(2,1)S(1)}, bf16[32,1280]{1,0:T(8,128)(2,1)S(1)}, u32[]{:S(2)}, u32[]{:S(2)}) %collective-permute-start.6) | collective-permute-done | bytes 81952 | tf_op jit(solution)/shard_map/ppermute | solution.py:49
  65.6 1.6 collective-permute-start.7
  67.2 39.3 %collective-permute-done.7 = bf16[2,32,1280]{2,1,0:T(8,128)(2,1)S(1)} collective-permute-done((bf16[2,32,1280]{2,1,0:T(8,128)(2,1)S(1)}, bf16[2,32,1280]{2,1,0:T(8,128)(2,1)S(1)}, u32[]{:S(2)}, u32[]{:S(2)}) %collective-permute-start.7) | collective-permute-done | bytes 163872 | tf_op jit(solution)/shard_map/ppermute | solution.py:58
  106.6 1.1 collective-permute-start.8
  107.7 1.3 slice.97
  109.0 1.1 collective-permute-start.11
  110.0 1.3 slice.98
  111.4 2.4 %collective-permute-start.13 = (bf16[256,2048]{1,0:T(8,128)(2,1)S(1)}, bf16[256,2048]{1,0:T(8,128)(2,1)}, u32[]{:S(2)}, u32[]{:S(2)}) collective-permute-start(bf16[256,2048]{1,0:T(8,128)(2,1)S(1)} %slice.98), channel_id=1, source_target_pairs={{0,6},{2,4},{4,2},{6,0},{1,7},{3,5},{5,3},{7,1},{8,14},{10,12},{12... | collective-permute-start | bytes 3145736 | tf_op jit(solution)/shard_map/ppermute | solution.py:58
  113.9 5.1 %collective-permute-done.8 = bf16[2,2,32,1280]{3,2,1,0:T(8,128)(2,1)S(1)} collective-permute-done((bf16[2,2,32,1280]{3,2,1,0:T(8,128)(2,1)S(1)}, bf16[2,2,32,1280]{3,2,1,0:T(8,128)(2,1)S(1)}, u32[]{:S(2)}, u32[]{:S(2)}) %collective-permute-start.8) | collective-permute-done | bytes 327712 | tf_op jit(solution)/shard_map/ppermute | solution.py:58
  119.0 0.9 pad_maximum_fusion.1
  119.9 17.2 %collective-permute-done.11.refs_8_ = bf16[256,2048]{1,0:T(8,128)(2,1)} collective-permute-done((bf16[256,2048]{1,0:T(8,128)(2,1)S(1)}, bf16[256,2048]{1,0:T(8,128)(2,1)}, u32[]{:S(2)}, u32[]{:S(2)}) %collective-permute-start.11) | collective-permute-done | bytes 1048608 | tf_op jit(solution)/shard_map/ppermute | solution.py:58
  137.2 1.8 collective-permute-done.13.refs_9_
  139.5 1.1 collective-permute-start.5
  141.3 3.4 %collective-permute-done.5 = f32[640]{0:T(1024)S(1)} collective-permute-done((f32[640]{0:T(1024)S(1)}, f32[640]{0:T(1024)S(1)}, u32[]{:S(2)}, u32[]{:S(2)}) %collective-permute-start.5) | collective-permute-done | bytes 2592 | tf_op jit(solution)/shard_map/ppermute | solution.py:58
  146.5 0.7 reshape.260.refs_3_
  147.2 0.9 copy.50.refs_2_
  148.1 1.4 pad_maximum_fusion
  149.5 1.2 copy.48
  150.7 13.8 %shard_map.172 = (bf16[512,512]{1,0:T(8,128)(2,1)}, bf16[512,512]{1,0:T(8,128)(2,1)}, bf16[512,512]{1,0:T(8,128)(2,1)}) custom-call(s32[9]{0:T(128)} %stack.92.refs_0_, bf16[4,1,2048]{2,1,0:T(2,128)(2,1)} %copy.51.refs_1_, f32[512,1]{1,0:T(8,128)} %copy.50.refs_2_, s32[2,512]{1,0:T(2,128)} %reshape.260.refs_3_, bf16[512,1280]{1,0:T(8,128)(2,1)} %bitcast.82, ...), custom_call_target="tpu_custom_call" | custom-call | flops 4831838208 | bytes 18874368 | tf_op jit(solution)/shard_map/pallas_call | solution.py:149
  164.6 1.3 collective-permute-start.20
  165.9 0.9 copy.52.refs_2_
  166.7 12.2 %shard_map.173 = bf16[512,512]{1,0:T(8,128)(2,1)} custom-call(s32[9]{0:T(128)} %stack.89.refs_0_, bf16[4,1,2048]{2,1,0:T(2,128)(2,1)} %copy.51.refs_1_, f32[512,1]{1,0:T(8,128)} %copy.52.refs_2_, s32[2,512]{1,0:T(2,128)} %reshape.260.refs_3_, bf16[512,512]{1,0:T(8,128)(2,1)} %get-tuple-element.20.refs_4_, bf16[512,512]{1,0:T(8,128)(2,1)} %get-tuple-element.21.refs_5_, ...), custom_call_target="tpu_custom_call" | custom-call | flops 4831838208 | bytes 18874368 | tf_op jit(solution)/shard_map/pallas_call | solution.py:149
  178.9 1.7 collective-permute-done.20
  180.6 2.9 %maximum_select_fusion = bf16[512,1024]{1,0:T(8,128)(2,1)} fusion(bf16[512,512]{1,0:T(8,128)(2,1)} %collective-permute-done.20, bf16[512,512]{1,0:T(8,128)(2,1)} %shard_map.173, pred[]{:T(512)S(6)} %eq.10), kind=kLoop, calls=%fused_computation.26 | loop fusion | flops 4718592 | bytes 2097153 | tf_op jit(solution)/shard_map/jit(_where)/select_n | solution.py:328
  (123 shorter events, 9.8 us)
Async XLA Ops:
  6.5 11.3 %copy-start = (bf16[1280,384]{1,0:T(8,128)(2,1)S(1)}, bf16[1280,384]{1,0:T(8,128)(2,1)}, u32[]{:S(2)}) copy-start(bf16[1280,384]{1,0:T(8,128)(2,1)} %param.32) | copy-start | bytes 2949124
  6.5 10.2 %copy-start.6 = (bf16[1280]{0:T(1024)(128)(2,1)S(1)}, bf16[1280]{0:T(1024)(128)(2,1)}, u32[]{:S(2)}) copy-start(bf16[1280]{0:T(1024)(128)(2,1)} %param.28) | copy-start | bytes 7684
  6.5 10.2 %copy-start.7 = (bf16[1280]{0:T(1024)(128)(2,1)S(1)}, bf16[1280]{0:T(1024)(128)(2,1)}, u32[]{:S(2)}) copy-start(bf16[1280]{0:T(1024)(128)(2,1)} %param.29) | copy-start | bytes 7684
  6.5 10.2 %copy-start.2 = (bf16[64,1280]{1,0:T(8,128)(2,1)S(1)}, bf16[64,1280]{1,0:T(8,128)(2,1)}, u32[]{:S(2)}) copy-start(bf16[64,1280]{1,0:T(8,128)(2,1)} %param.27) | copy-start | bytes 491524
  6.5 10.5 %copy-start.3 = (bf16[2,256,1280]{2,1,0:T(8,128)(2,1)S(1)}, bf16[2,256,1280]{2,1,0:T(8,128)(2,1)}, u32[]{:S(2)}) copy-start(bf16[2,256,1280]{2,1,0:T(8,128)(2,1)} %param.23) | copy-start | bytes 3932164
  6.5 144.2 %all-gather.3.cloned.1.call-start = ((), (), s32[]{:S(2)}) async-start(), calls=%async_computation | async-start | bytes 11354112 | tf_op jit(solution)/shard_map/all_gather | solution.py:262
  7.8 7.7 %collective-permute-start.9 = (bf16[168,512]{1,0:T(8,128)(2,1)S(1)}, bf16[168,512]{1,0:T(8,128)(2,1)S(1)}, u32[]{:S(2)}, u32[]{:S(2)}) collective-permute-start(bf16[168,512]{1,0:T(8,128)(2,1)S(1)} %constant_dynamic-slice_fusion), channel_id=1, source_target_pairs={{0,4},{4,0},{1,5},{5,1},{2,6},{6,2},{3,7},{7,3},{8,12},{12,8},{9,1... | collective-permute-start | bytes 516104 | tf_op jit(solution)/shard_map/ppermute | solution.py:58
  26.6 1.2 copy-start.11
  27.7 1.1 copy-start.5
  29.2 4.3 %copy-start.10 = (s32[2,2]{1,0:T(2,128)S(1)}, s32[2,2]{1,0:T(2,128)}, u32[]{:S(2)}) copy-start(s32[2,2]{1,0:T(2,128)} %param.26) | copy-start | bytes 52
  29.3 8.2 %copy-start.1 = (bf16[512,2048]{1,0:T(8,128)(2,1)S(1)}, bf16[512,2048]{1,0:T(8,128)(2,1)}, u32[]{:S(2)}) copy-start(bf16[512,2048]{1,0:T(8,128)(2,1)} %refs_7_.1) | copy-start | bytes 6291460
  29.5 13.6 %copy-start.8 = (bf16[2048]{0:T(1024)(128)(2,1)S(1)}, bf16[2048]{0:T(1024)(128)(2,1)}, u32[]{:S(2)}) copy-start(bf16[2048]{0:T(1024)(128)(2,1)} %param.19) | copy-start | bytes 12292
  29.5 13.9 %copy-start.9 = (bf16[1280]{0:T(1024)(128)(2,1)S(1)}, bf16[1280]{0:T(1024)(128)(2,1)}, u32[]{:S(2)}) copy-start(bf16[1280]{0:T(1024)(128)(2,1)} %param.30) | copy-start | bytes 7684
  31.2 0.8 copy-start.4
  32.8 12.0 %collective-permute-start = (f32[2,32,1280]{2,1,0:T(8,128)}, f32[2,32,1280]{2,1,0:T(8,128)}, u32[]{:S(2)}, u32[]{:S(2)}) collective-permute-start(f32[2,32,1280]{2,1,0:T(8,128)} %dynamic-slice_bitcast_fusion), channel_id=1, source_target_pairs={{0,1},{1,0},{2,3},{3,2},{4,5},{5,4},{6,7},{7,6},{8,9},{9,8},{10,11... | collective-permute-start | bytes 983048 | tf_op jit(solution)/shard_map/ppermute | solution.py:45
  33.6 9.5 %collective-permute-start.1 = (f32[4]{0:T(128)S(1)}, f32[4]{0:T(128)S(1)}, u32[]{:S(2)}, u32[]{:S(2)}) collective-permute-start(f32[4]{0:T(128)S(1)} %convert_element_type.95), channel_id=1, source_target_pairs={{0,8},{8,16},{16,24},{24,32},{32,40},{40,48},{48,56},{56,64},{64,7... | collective-permute-start | bytes 56 | tf_op jit(solution)/shard_map/ppermute | solution.py:49
  37.4 129.3 %collective-permute-start.18 = (bf16[512,2048]{1,0:T(8,128)(2,1)S(1)}, bf16[512,2048]{1,0:T(8,128)(2,1)}, u32[]{:S(2)}, u32[]{:S(2)}) collective-permute-start(bf16[512,2048]{1,0:T(8,128)(2,1)S(1)} %copy-done.1), channel_id=1, source_target_pairs={{0,1},{1,0},{2,3},{3,2},{4,5},{5,4},{6,7},{7,6},{8,9},{9,8},{10,11... | collective-permute-start | bytes 6291464 | tf_op jit(solution)/shard_map/ppermute | solution.py:58
  43.2 1.5 collective-permute-start.2
  45.9 3.9 %collective-permute-start.4 = (f32[2,2688]{1,0:T(2,128)S(1)}, f32[2,2688]{1,0:T(2,128)S(1)}, u32[]{:S(2)}, u32[]{:S(2)}) collective-permute-start(f32[2,2688]{1,0:T(2,128)S(1)} %pad_maximum_fusion.9), channel_id=1, source_target_pairs={{0,2},{2,0},{1,3},{3,1},{4,6},{6,4},{5,7},{7,5},{8,10},{10,8},{9,1... | collective-permute-start | bytes 64520 | tf_op jit(solution)/shard_map/ppermute | solution.py:58
  47.5 6.4 %collective-permute-start.3 = (f32[32,1280]{1,0:T(8,128)S(1)}, f32[32,1280]{1,0:T(8,128)S(1)}, u32[]{:S(2)}, u32[]{:S(2)}) collective-permute-start(f32[32,1280]{1,0:T(8,128)S(1)} %dynamic-slice_bitcast_fusion.1), channel_id=1, source_target_pairs={{0,2},{2,0},{1,3},{3,1},{4,6},{6,4},{5,7},{7,5},{8,10},{10,8},{9,1... | collective-permute-start | bytes 491528 | tf_op jit(solution)/shard_map/ppermute | solution.py:45
  53.9 53.7 %collective-permute-start.10 = (bf16[512,2048]{1,0:T(8,128)(2,1)S(1)}, bf16[512,2048]{1,0:T(8,128)(2,1)}, u32[]{:S(2)}, u32[]{:S(2)}) collective-permute-start(bf16[512,2048]{1,0:T(8,128)(2,1)S(1)} %copy-done.1), channel_id=1, source_target_pairs={{0,6},{2,4},{4,2},{6,0},{1,7},{3,5},{5,3},{7,1},{8,14},{10,12},{12... | collective-permute-start | bytes 6291464 | tf_op jit(solution)/shard_map/ppermute | solution.py:58
  56.2 53.9 %collective-permute-start.12 = (bf16[512,2048]{1,0:T(8,128)(2,1)S(1)}, bf16[512,2048]{1,0:T(8,128)(2,1)}, u32[]{:S(2)}, u32[]{:S(2)}) collective-permute-start(bf16[512,2048]{1,0:T(8,128)(2,1)S(1)} %copy-done.1), channel_id=1, source_target_pairs={{0,2},{2,0},{1,3},{3,1},{4,6},{6,4},{5,7},{7,5},{8,10},{10,8},{9,1... | collective-permute-start | bytes 6291464 | tf_op jit(solution)/shard_map/ppermute | solution.py:58
  57.1 8.4 %collective-permute-start.6 = (bf16[32,1280]{1,0:T(8,128)(2,1)S(1)}, bf16[32,1280]{1,0:T(8,128)(2,1)S(1)}, u32[]{:S(2)}, u32[]{:S(2)}) collective-permute-start(bf16[32,1280]{1,0:T(8,128)(2,1)S(1)} %multiply_convert_fusion), channel_id=1, source_target_pairs={{0,8},{8,16},{16,24},{24,32},{32,40},{40,48},{48,56},{56,64},{64,7... | collective-permute-start | bytes 245768 | tf_op jit(solution)/shard_map/ppermute | solution.py:49
  65.6 40.9 %collective-permute-start.7 = (bf16[2,32,1280]{2,1,0:T(8,128)(2,1)S(1)}, bf16[2,32,1280]{2,1,0:T(8,128)(2,1)S(1)}, u32[]{:S(2)}, u32[]{:S(2)}) collective-permute-start(bf16[2,32,1280]{2,1,0:T(8,128)(2,1)S(1)} %get-tuple-element.32), channel_id=1, source_target_pairs={{0,2},{2,0},{1,3},{3,1},{4,6},{6,4},{5,7},{7,5},{8,10},{10,8},{9,1... | collective-permute-start | bytes 491528 | tf_op jit(solution)/shard_map/ppermute | solution.py:58
  106.6 12.4 %collective-permute-start.8 = (bf16[2,2,32,1280]{3,2,1,0:T(8,128)(2,1)S(1)}, bf16[2,2,32,1280]{3,2,1,0:T(8,128)(2,1)S(1)}, u32[]{:S(2)}, u32[]{:S(2)}) collective-permute-start(bf16[2,2,32,1280]{3,2,1,0:T(8,128)(2,1)S(1)} %get-tuple-element.28), channel_id=1, source_target_pairs={{0,4},{4,0},{1,5},{5,1},{2,6},{6,2},{3,7},{7,3},{8,12},{12,8},{9,1... | collective-permute-start | bytes 983048 | tf_op jit(solution)/shard_map/ppermute | solution.py:58
  109.0 28.2 %collective-permute-start.11 = (bf16[256,2048]{1,0:T(8,128)(2,1)S(1)}, bf16[256,2048]{1,0:T(8,128)(2,1)}, u32[]{:S(2)}, u32[]{:S(2)}) collective-permute-start(bf16[256,2048]{1,0:T(8,128)(2,1)S(1)} %slice.97), channel_id=1, source_target_pairs={{0,2},{2,0},{1,3},{3,1},{4,6},{6,4},{5,7},{7,5},{8,10},{10,8},{9,1... | collective-permute-start | bytes 3145736 | tf_op jit(solution)/shard_map/ppermute | solution.py:58
  111.4 27.6 %collective-permute-start.13 = (bf16[256,2048]{1,0:T(8,128)(2,1)S(1)}, bf16[256,2048]{1,0:T(8,128)(2,1)}, u32[]{:S(2)}, u32[]{:S(2)}) collective-permute-start(bf16[256,2048]{1,0:T(8,128)(2,1)S(1)} %slice.98), channel_id=1, source_target_pairs={{0,6},{2,4},{4,2},{6,0},{1,7},{3,5},{5,3},{7,1},{8,14},{10,12},{12... | collective-permute-start | bytes 3145736 | tf_op jit(solution)/shard_map/ppermute | solution.py:58
  113.8 36.9 %collective-permute-start.15 = (bf16[512,2048]{1,0:T(8,128)(2,1)}, bf16[512,2048]{1,0:T(8,128)(2,1)}, u32[]{:S(2)}, u32[]{:S(2)}) collective-permute-start(bf16[512,2048]{1,0:T(8,128)(2,1)} %collective-permute-done.10.refs_6_), channel_id=1, source_target_pairs={{0,1},{1,0},{2,3},{3,2},{4,5},{5,4},{6,7},{7,6},{8,9},{9,8},{10,11... | collective-permute-start | bytes 6291464 | tf_op jit(solution)/shard_map/ppermute | solution.py:58
  139.0 5.9 %collective-permute-start.14 = (bf16[4,2,32,1280]{3,2,1,0:T(8,128)(2,1)}, bf16[4,2,32,1280]{3,2,1,0:T(8,128)(2,1)}, u32[]{:S(2)}, u32[]{:S(2)}) collective-permute-start(bf16[4,2,32,1280]{3,2,1,0:T(8,128)(2,1)} %pad_maximum_fusion.1), channel_id=1, source_target_pairs={{0,1},{1,0},{2,3},{3,2},{4,5},{5,4},{6,7},{7,6},{8,9},{9,8},{10,11... | collective-permute-start | bytes 1966088 | tf_op jit(solution)/shard_map/ppermute | solution.py:45
  139.0 27.8 %collective-permute-start.19 = (bf16[512,2048]{1,0:T(8,128)(2,1)}, bf16[512,2048]{1,0:T(8,128)(2,1)}, u32[]{:S(2)}, u32[]{:S(2)}) collective-permute-start(bf16[512,2048]{1,0:T(8,128)(2,1)} %collective-permute-done.12.refs_9_), channel_id=1, source_target_pairs={{0,1},{1,0},{2,3},{3,2},{4,5},{5,4},{6,7},{7,6},{8,9},{9,8},{10,11... | collective-permute-start | bytes 6291464 | tf_op jit(solution)/shard_map/ppermute | solution.py:58
  139.5 5.2 %collective-permute-start.5 = (f32[640]{0:T(1024)S(1)}, f32[640]{0:T(1024)S(1)}, u32[]{:S(2)}, u32[]{:S(2)}) collective-permute-start(f32[640]{0:T(1024)S(1)} %pad_maximum_fusion.10), channel_id=1, source_target_pairs={{0,4},{4,0},{1,5},{5,1},{2,6},{6,2},{3,7},{7,3},{8,12},{12,8},{9,1... | collective-permute-start | bytes 7688 | tf_op jit(solution)/shard_map/ppermute | solution.py:58
  144.9 5.8 %collective-permute-start.16 = (bf16[256,2048]{1,0:T(8,128)(2,1)}, bf16[256,2048]{1,0:T(8,128)(2,1)}, u32[]{:S(2)}, u32[]{:S(2)}) collective-permute-start(bf16[256,2048]{1,0:T(8,128)(2,1)} %collective-permute-done.11.refs_8_), channel_id=1, source_target_pairs={{0,1},{1,0},{2,3},{3,2},{4,5},{5,4},{6,7},{7,6},{8,9},{9,8},{10,11... | collective-permute-start | bytes 3145736 | tf_op jit(solution)/shard_map/ppermute | solution.py:58
  144.9 5.7 %collective-permute-start.17 = (bf16[256,2048]{1,0:T(8,128)(2,1)}, bf16[256,2048]{1,0:T(8,128)(2,1)}, u32[]{:S(2)}, u32[]{:S(2)}) collective-permute-start(bf16[256,2048]{1,0:T(8,128)(2,1)} %collective-permute-done.13.refs_9_), channel_id=1, source_target_pairs={{0,1},{1,0},{2,3},{3,2},{4,5},{5,4},{6,7},{7,6},{8,9},{9,8},{10,11... | collective-permute-start | bytes 3145736 | tf_op jit(solution)/shard_map/ppermute | solution.py:58
  164.6 16.1 %collective-permute-start.20 = (bf16[512,512]{1,0:T(8,128)(2,1)}, bf16[512,512]{1,0:T(8,128)(2,1)}, u32[]{:S(2)}, u32[]{:S(2)}) collective-permute-start(bf16[512,512]{1,0:T(8,128)(2,1)} %get-tuple-element.22), channel_id=1, source_target_pairs={{0,4},{4,0},{1,5},{5,1},{2,6},{6,2},{3,7},{7,3},{8,12},{12,8},{9,1... | collective-permute-start | bytes 1572872 | tf_op jit(solution)/shard_map/ppermute | solution.py:58
Sparse Core Ops, SparseCore 0:
  16.8 112.5 all-gather.2

commit v3 on v2

--- a/solution.py
+++ b/solution.py
@@ -31,14 +31,6 @@
     centred = values - middle
     spread = jnp.mean(centred * centred, axis=-1, keepdims=True)
     return centred * lax.rsqrt(spread + EPS_VISION) * gain
-
-
-def masked_softmax(scores, allowed):
-    highest = jnp.max(jnp.where(allowed, scores, FILL), axis=-1, keepdims=True)
-    weights = jnp.where(allowed, jnp.exp(scores - highest), 0.0)
-    summed = jnp.sum(weights, axis=-1, keepdims=True)
-    anything = jnp.any(allowed, axis=-1, keepdims=True)
-    return (weights / jnp.where(anything, summed, 1.0)).astype(jnp.bfloat16)
 
 
 def turned(x, axis, by, count):
@@ -174,54 +166,55 @@
     )(where, gain, scale, bounds, *rows, weight, *(ref for refs in blocks for ref in refs))
 
 
+def resample_kernel(
+    count_ref, image_ref, latent_ref, latent_gain_ref, context_gain_ref, query_ref, key_ref, value_ref, output_ref, out_ref
+):
+    latent_normed = layer_norm(
+        latent_ref[...].astype(jnp.float32), latent_gain_ref[...].astype(jnp.float32)
+    ).astype(jnp.bfloat16)
+
+    def project(rows, weight_ref):
+        return jnp.dot(rows, weight_ref[...], preferred_element_type=jnp.float32).astype(jnp.bfloat16)
+
+    width = query_ref.shape[1]
+    heads = width // RHD
+    column = lax.broadcasted_iota(jnp.int32, (LAT, width), 1)
+    masks = [(column >= h * RHD) & (column < (h + 1) * RHD) for h in range(heads)]
+    latent_queries = project(latent_normed, query_ref).astype(jnp.float32)
+    queries = jnp.concatenate([jnp.where(mask, latent_queries, 0.0) for mask in masks], axis=0).astype(jnp.bfloat16)
+    for slot in range(image_ref.shape[0]):
+        context = layer_norm(
+            image_ref[slot].astype(jnp.float32), context_gain_ref[...].astype(jnp.float32)
+        ).astype(jnp.bfloat16)
+        joined = jnp.concatenate([context, latent_normed], axis=0)
+        keys, values = project(joined, key_ref), project(joined, value_ref)
+        scores = lax.dot_general(
+            queries, keys, (((1,), (1,)), ((), ())), preferred_element_type=jnp.float32
+        ) * RHD ** (-0.5)
+        row = lax.broadcasted_iota(jnp.int32, scores.shape, 1)
+        allowed = (row < count_ref[slot]) | (row >= PATCH)
+        scores = jnp.where(allowed, scores, FILL)
+        weights = jnp.exp(scores - jnp.max(scores, axis=-1, keepdims=True))
+        probs = (weights / jnp.sum(weights, axis=-1, keepdims=True)).astype(jnp.bfloat16)
+        mixed = jnp.dot(probs, values, preferred_element_type=jnp.float32)
+        res_heads = sum(
+            jnp.where(mask, mixed[h * LAT : (h + 1) * LAT], 0.0) for h, mask in enumerate(masks)
+        ).astype(jnp.bfloat16)
+        out_ref[slot] = jnp.dot(res_heads, output_ref[...], preferred_element_type=jnp.float32)
+
+
 def resample(images, patch_counts, latents, latent_gain, context_gain, res_query, res_key, res_value, res_output):
-    slot_count = images.shape[0]
-    res_local = res_query.shape[1] // RHD
-    latent_base = latents.astype(jnp.float32)
-    latent_normed = layer_norm(latent_base, latent_gain.astype(jnp.float32)).astype(jnp.bfloat16)
-    latent_queries = (
-        jnp.dot(latent_normed, res_query, preferred_element_type=jnp.float32)
-        .astype(jnp.bfloat16)
-        .reshape(LAT, res_local, RHD)
+    vmem = pl.BlockSpec(memory_space=pltpu.VMEM)
+    return pl.pallas_call(
+        resample_kernel,
+        out_shape=jax.ShapeDtypeStruct((images.shape[0], LAT, VW), jnp.float32),
+        in_specs=[pl.BlockSpec(memory_space=pltpu.SMEM)] + [vmem] * 8,
+        out_specs=vmem,
+        compiler_params=pltpu.CompilerParams(vmem_limit_bytes=40 * 1024 * 1024),
+        cost_estimate=pl.CostEstimate(flops=30 << 30, bytes_accessed=8 << 20, transcendentals=1 << 18),
+    )(
+        patch_counts, images, latents, latent_gain[None], context_gain[None], res_query, res_key, res_value, res_output
     )
-    context_normed = layer_norm(
-        images.astype(jnp.float32), context_gain.astype(jnp.float32)
-    ).astype(jnp.bfloat16)
-    patch_keys = jnp.einsum(
-        "cpf,fe->cpe", context_normed, res_key, preferred_element_type=jnp.float32
-    ).astype(jnp.bfloat16)
-    patch_values = jnp.einsum(
-        "cpf,fe->cpe", context_normed, res_value, preferred_element_type=jnp.float32
-    ).astype(jnp.bfloat16)
-    latent_keys = jnp.dot(latent_normed, res_key, preferred_element_type=jnp.float32).astype(
-        jnp.bfloat16
-    )
-    latent_values = jnp.dot(latent_normed, res_value, preferred_element_type=jnp.float32).astype(
-        jnp.bfloat16
-    )
-    res_keys = jnp.concatenate(
-        [patch_keys, jnp.broadcast_to(latent_keys[None], (slot_count, LAT, latent_keys.shape[1]))],
-        axis=1,
-    ).reshape(slot_count, PATCH + LAT, res_local, RHD)
-    res_values = jnp.concatenate(
-        [
-            patch_values,
-            jnp.broadcast_to(latent_values[None], (slot_count, LAT, latent_values.shape[1])),
-        ],
-        axis=1,
-    ).reshape(slot_count, PATCH + LAT, res_local, RHD)
-    res_scores = jnp.einsum(
-        "qhd,ckhd->chqk", latent_queries, res_keys, preferred_element_type=jnp.float32
-    ) * RHD ** (-0.5)
-    key_rows = jnp.arange(PATCH + LAT, dtype=jnp.int32)
-    patch_allowed = (key_rows[None, :] < patch_counts[:, None]) | (key_rows[None, :] >= PATCH)
-    res_probs = masked_softmax(res_scores, patch_allowed[:, None, None, :])
-    res_heads = (
-        jnp.einsum("chqk,ckhd->cqhd", res_probs, res_values, preferred_element_type=jnp.float32)
-        .astype(jnp.bfloat16)
-        .reshape(slot_count, LAT, res_local * RHD)
-    )
-    return jnp.einsum("cqe,ef->cqf", res_heads, res_output, preferred_element_type=jnp.float32)
 
 
 def local(
@@ -282,19 +275,19 @@
     first = lax.dynamic_index_in_dim(mix, core, 1, keepdims=False)
     first = first + turned(lax.dynamic_index_in_dim(mix, 1 - core, 1, keepdims=False), "core", 1, 2)
     small = jnp.concatenate([small, flipped(small, ("core",))], axis=0)
-    first, small = lax.optimization_barrier((first, small))
+    text_out = after(text_rows, other)
+    near_text, cross_text = flipped(text_out, ("xl",)), flipped(text_out, ("xh", "xl"))
+    near_text, cross_text, first, small = lax.optimization_barrier((near_text, cross_text, first, small))
+    cut = TOK // 2
+    text_top = flipped(cross_text[:cut], ("xl",))
+    text_bottom = flipped(near_text[cut:], ("xh", "xl"))
     total = lax.dynamic_index_in_dim(first, xl, 0, keepdims=False)
     total = total + turned(lax.dynamic_index_in_dim(first, 1 - xl, 0, keepdims=False), "xl", 1, 2)
     small = jnp.concatenate([small, flipped(small, ("xl",))], axis=0)
-    total, small = lax.optimization_barrier((total, small))
+    text_top, text_bottom, total, small = lax.optimization_barrier((text_top, text_bottom, total, small))
     short = jnp.concatenate([jnp.sum(small[:, :TOK], axis=0), small[0, TOK + D // NY :]])
     short_other = flipped(short, ("xh",))
 
-    text_out = after(text_rows, other, total)
-    near_text, cross_text = flipped(text_out, ("xl",)), flipped(text_out, ("xh", "xl"))
-    cut = TOK // 2
-    text_top = flipped(cross_text[:cut], ("xl",))
-    text_bottom = flipped(near_text[cut:], ("xh", "xl"))
     base = lax.dynamic_slice_in_dim(latents, core * (LAT // 2), LAT // 2, 0).astype(jnp.float32)
     piece = layer_norm(base + total, final_gain.astype(jnp.float32)).astype(jnp.bfloat16)
     both = jnp.stack([next_pair(piece), piece])
@@ -313,7 +306,6 @@
     both = jnp.stack([both, flipped(both, ("xl",))])
     both = jnp.stack([both, flipped(both, ("xh",))])
     around = jnp.stack([both[0, 0], both[0, 1], both[1, 0], both[1, 1]])
-    around = after(around, text_top, text_bottom)
     resampled = jnp.stack([around, turned(around, "core", 1, 2)], axis=2).reshape(KEYS, VW)
 
     def half(blocks, which, own_scale, others, rows):

time: 191 us -> 178 us (0.932)
  waiting for transfers between devices: 90.3 us -> 78.3 us
  matrix products: 8.92 us -> 0.21 us
  Pallas kernels: 26 us -> 30.7 us
  starting transfers between devices: 23.9 us -> 27.4 us
  other arithmetic: 12.5 us -> 9.7 us
  local copies, waits for them, and re-layouts: 14 us -> 16.6 us
    ppermute x16, waiting for transfers between devices: 74.8 us -> 65.4 us  [flipped(): return lax.ppermute(x, axes, [(i, count - 1 - i) for i in range(count)])]
    dot_general x8 -> x0, matrix products: 8.71 us -> none  [the longest x1 2.1 us: resample(): jnp.einsum('cpf,fe->cpe', context_normed, res_value, preferred_element_ty...]
    pallas_call x0 -> x1, Pallas kernels: none -> 4.68 us  [resample(): pl.pallas_call(resample_kernel, out_shape=jax.ShapeDtypeStruct((images.sh...]
    unnamed x24 -> x30, local copies, waits for them, and re-layouts: 0.89 us -> 4.95 us
    concatenate x2 -> x0, local copies, waits for them, and re-layouts: 2.4 us -> none  [the longest x1 1.34 us: resample(): jnp.concatenate([patch_keys, jnp.broadcast_to(latent_keys[None], (slot_co...]
    ppermute x3, waiting for transfers between devices: 4.06 us -> 1.83 us  [turned(): return lax.ppermute(x, axis, [(i, (i + by) % count) for i in range(count)])]
  transfers between devices with their start and end apart: 22 -> 22, of which waited for: 11 -> 11; matrix products, arithmetic and copies ran while one was open for 15% -> 9% of each run, Pallas kernels for 14% -> 17%
where the time goes in v3:
time: 178 us; the launch traced here: 177 us
  waiting for transfers between devices  78.3 us (44%)
  Pallas kernels  30.7 us (17%)
  starting transfers between devices  27.4 us (15%)
  local copies, waits for them, and re-layouts  16.6 us (9%)
  between operations  14.5 us (8%)
  other arithmetic  9.7 us (5%)
    ppermute x16, waiting for transfers between devices, flipped(): return lax.ppermute(x, axes, [(i, count - 1 - i) for i in range(count)])  65.4 us
    pallas_call x2, Pallas kernels, attend(): pl.pallas_call(functools.partial(attend_kernel, counts, fresh), out_shape...  26 us
    ppermute x16, starting transfers between devices, flipped(): return lax.ppermute(x, axes, [(i, count - 1 - i) for i in range(count)])  19.2 us
    ppermute x2, waiting for transfers between devices, next_pair(): return lax.ppermute(x, ('y', 'z'), [(i, i + 1) for i in range(NY * NZ - 1)])  10.9 us
    ppermute x2, starting transfers between devices, next_pair(): return lax.ppermute(x, ('y', 'z'), [(i, i + 1) for i in range(NY * NZ - 1)])  7.64 us
    unnamed x30, local copies, waits for them, and re-layouts  4.95 us
    pallas_call x1, Pallas kernels, resample(): pl.pallas_call(resample_kernel, out_shape=jax.ShapeDtypeStruct((images.sh...  4.68 us
  transfers between devices with their start and end apart: 22, of which 11 were waited for; matrix products, arithmetic and copies ran while one was open for 9% of the time, Pallas kernels for 17%

profile of v3, /device:TPU:24, one launch (start us, length us, event | category | flops | bytes accessed | tf_op | source)
XLA Modules:
  0.0 177.4 jit_solution(279302657707864066)
XLA Ops:
  6.6 1.2 pad_maximum_fusion.2
  7.8 3.1 %collective-permute-start = (bf16[168,512]{1,0:T(8,128)(2,1)S(1)}, bf16[168,512]{1,0:T(8,128)(2,1)S(1)}, u32[]{:S(2)}, u32[]{:S(2)}) collective-permute-start(bf16[168,512]{1,0:T(8,128)(2,1)S(1)} %constant_dynamic-slice_fusion), channel_id=1, source_target_pairs={{0,4},{4,0},{1,5},{5,1},{2,6},{6,2},{3,7},{7,3},{8,12},{12,8},{9,1... | collective-permute-start | bytes 516104 | tf_op jit(solution)/shard_map/ppermute | solution.py:50
  11.0 4.6 %collective-permute-done = bf16[168,512]{1,0:T(8,128)(2,1)S(1)} collective-permute-done((bf16[168,512]{1,0:T(8,128)(2,1)S(1)}, bf16[168,512]{1,0:T(8,128)(2,1)S(1)}, u32[]{:S(2)}, u32[]{:S(2)}) %collective-permute-start) | collective-permute-done | bytes 172064 | tf_op jit(solution)/shard_map/ppermute | solution.py:50
  15.9 0.7 pad_maximum_fusion.3
  16.8 1.6 collective-permute-start.1
  18.4 2.1 %collective-permute-start.2 = (bf16[512,2048]{1,0:T(8,128)(2,1)}, bf16[512,2048]{1,0:T(8,128)(2,1)}, u32[]{:S(2)}, u32[]{:S(2)}) collective-permute-start(bf16[512,2048]{1,0:T(8,128)(2,1)} %refs_7_.1), channel_id=1, source_target_pairs={{0,6},{2,4},{4,2},{6,0},{1,7},{3,5},{5,3},{7,1},{8,14},{10,12},{12... | collective-permute-start | bytes 6291464 | tf_op jit(solution)/shard_map/ppermute | solution.py:50
  20.5 1.2 copy-done.3
  21.7 1.2 copy-done.4
  22.9 1.2 copy-done.5
  24.1 4.7 %shard_map.172 = f32[2,64,1280]{2,1,0:T(8,128)S(1)} custom-call(s32[2]{0:T(128)S(1)} %copy-done.6, bf16[2,256,1280]{2,1,0:T(8,128)(2,1)S(1)} %copy-done.1, bf16[64,1280]{1,0:T(8,128)(2,1)S(1)} %copy-done, bf16[1,1280]{1,0:T(2,128)(2,1)S(1)} %broadcast_in_dim.40.latent_gain_ref, bf16[1,1280]{1,0:T(2,128)(2,1)S(1)} %broadcast_in_dim.41.context_gain_ref, ...), custom_call_target="tpu_custom_call" | custom-call | flops 32212254720 | bytes 8388608 | tf_op jit(solution)/shard_map/pallas_call | solution.py:208
  29.7 3.8 %collective-permute-start.4 = (f32[4]{0:T(128)S(1)}, f32[4]{0:T(128)S(1)}, u32[]{:S(2)}, u32[]{:S(2)}) collective-permute-start(f32[4]{0:T(128)S(1)} %convert_element_type.39), channel_id=1, source_target_pairs={{0,8},{8,16},{16,24},{24,32},{32,40},{40,48},{48,56},{56,64},{64,7... | collective-permute-start | bytes 56 | tf_op jit(solution)/shard_map/ppermute | solution.py:41
  33.6 2.1 %multiply_reduce_fusion = f32[512]{0:T(512)S(1)} fusion(bf16[512,2048]{1,0:T(8,128)(2,1)} %refs_7_.1), kind=kLoop, calls=%fused_computation.1 | loop fusion | flops 3145216 | bytes 2099200 | tf_op jit(solution)/shard_map/reduce_sum | solution.py:258
  35.6 3.5 %collective-permute-done.4 = f32[4]{0:T(128)S(1)} collective-permute-done((f32[4]{0:T(128)S(1)}, f32[4]{0:T(128)S(1)}, u32[]{:S(2)}, u32[]{:S(2)}) %collective-permute-start.4) | collective-permute-done | bytes 48 | tf_op jit(solution)/shard_map/ppermute | solution.py:41
  39.4 1.1 collective-permute-done.5
  40.6 24.6 %collective-permute-done.1.refs_9_ = bf16[512,2048]{1,0:T(8,128)(2,1)} collective-permute-done((bf16[512,2048]{1,0:T(8,128)(2,1)}, bf16[512,2048]{1,0:T(8,128)(2,1)}, u32[]{:S(2)}, u32[]{:S(2)}) %collective-permute-start.1) | collective-permute-done | bytes 2097184 | tf_op jit(solution)/shard_map/ppermute | solution.py:50
  65.3 2.4 %collective-permute-done.2.refs_6_ = bf16[512,2048]{1,0:T(8,128)(2,1)} collective-permute-done((bf16[512,2048]{1,0:T(8,128)(2,1)}, bf16[512,2048]{1,0:T(8,128)(2,1)}, u32[]{:S(2)}, u32[]{:S(2)}) %collective-permute-start.2) | collective-permute-done | bytes 2097184 | tf_op jit(solution)/shard_map/ppermute | solution.py:50
  67.7 2.3 %slice.65 = bf16[256,2048]{1,0:T(8,128)(2,1)} slice(bf16[512,2048]{1,0:T(8,128)(2,1)} %collective-permute-done.2.refs_6_), slice={[0:256], [0:2048]} | slice | bytes 2097152 | tf_op jit(solution)/shard_map/slice | solution.py:282
  70.0 2.4 %slice.66 = bf16[256,2048]{1,0:T(8,128)(2,1)} slice(bf16[512,2048]{1,0:T(8,128)(2,1)} %collective-permute-done.1.refs_9_), slice={[256:512], [0:2048]} | slice | bytes 2097152 | tf_op jit(solution)/shard_map/slice | solution.py:283
  72.3 2.1 %collective-permute-start.7 = (bf16[256,2048]{1,0:T(8,128)(2,1)}, bf16[256,2048]{1,0:T(8,128)(2,1)S(1)}, u32[]{:S(2)}, u32[]{:S(2)}) collective-permute-start(bf16[256,2048]{1,0:T(8,128)(2,1)} %slice.66), channel_id=1, source_target_pairs={{0,6},{2,4},{4,2},{6,0},{1,7},{3,5},{5,3},{7,1},{8,14},{10,12},{12... | collective-permute-start | bytes 3145736 | tf_op jit(solution)/shard_map/ppermute | solution.py:50
  74.5 0.6 stack.92.refs_0_
  75.1 0.6 stack.89.refs_0_
  75.7 1.6 collective-permute-start.9
  77.4 0.5 collective-permute-start.8
  77.9 18.9 %collective-permute-done.9 = f32[2,2688]{1,0:T(2,128)S(1)} collective-permute-done((f32[2,2688]{1,0:T(2,128)S(1)}, f32[2,2688]{1,0:T(2,128)S(1)}, u32[]{:S(2)}, u32[]{:S(2)}) %collective-permute-start.9) | collective-permute-done | bytes 21536 | tf_op jit(solution)/shard_map/ppermute | solution.py:50
  96.8 1.8 %collective-permute-done.8 = f32[32,1280]{1,0:T(8,128)S(1)} collective-permute-done((f32[32,1280]{1,0:T(8,128)S(1)}, f32[32,1280]{1,0:T(8,128)S(1)}, u32[]{:S(2)}, u32[]{:S(2)}) %collective-permute-start.8) | collective-permute-done | bytes 163872 | tf_op jit(solution)/shard_map/ppermute | solution.py:37
  99.1 3.8 %collective-permute-start.11 = (bf16[32,1280]{1,0:T(8,128)(2,1)S(1)}, bf16[32,1280]{1,0:T(8,128)(2,1)S(1)}, u32[]{:S(2)}, u32[]{:S(2)}) collective-permute-start(bf16[32,1280]{1,0:T(8,128)(2,1)S(1)} %multiply_convert_fusion), channel_id=1, source_target_pairs={{0,8},{8,16},{16,24},{24,32},{32,40},{40,48},{48,56},{56,64},{64,7... | collective-permute-start | bytes 245768 | tf_op jit(solution)/shard_map/ppermute | solution.py:41
  103.1 0.5 collective-permute-start.19
  103.6 7.4 %collective-permute-done.11 = bf16[32,1280]{1,0:T(8,128)(2,1)S(1)} collective-permute-done((bf16[32,1280]{1,0:T(8,128)(2,1)S(1)}, bf16[32,1280]{1,0:T(8,128)(2,1)S(1)}, u32[]{:S(2)}, u32[]{:S(2)}) %collective-permute-start.11) | collective-permute-done | bytes 81952 | tf_op jit(solution)/shard_map/ppermute | solution.py:41
  111.0 0.7 collective-permute-start.12
  111.7 4.9 %collective-permute-done.12 = bf16[2,32,1280]{2,1,0:T(8,128)(2,1)S(1)} collective-permute-done((bf16[2,32,1280]{2,1,0:T(8,128)(2,1)S(1)}, bf16[2,32,1280]{2,1,0:T(8,128)(2,1)S(1)}, u32[]{:S(2)}, u32[]{:S(2)}) %collective-permute-start.12) | collective-permute-done | bytes 163872 | tf_op jit(solution)/shard_map/ppermute | solution.py:50
  116.7 2.1 %collective-permute-start.13 = (bf16[2,2,32,1280]{3,2,1,0:T(8,128)(2,1)S(1)}, bf16[2,2,32,1280]{3,2,1,0:T(8,128)(2,1)S(1)}, u32[]{:S(2)}, u32[]{:S(2)}) collective-permute-start(bf16[2,2,32,1280]{3,2,1,0:T(8,128)(2,1)S(1)} %get-tuple-element.36), channel_id=1, source_target_pairs={{0,4},{4,0},{1,5},{5,1},{2,6},{6,2},{3,7},{7,3},{8,12},{12,8},{9,1... | collective-permute-start | bytes 983048 | tf_op jit(solution)/shard_map/ppermute | solution.py:50
  118.7 6.6 %collective-permute-done.13 = bf16[2,2,32,1280]{3,2,1,0:T(8,128)(2,1)S(1)} collective-permute-done((bf16[2,2,32,1280]{3,2,1,0:T(8,128)(2,1)S(1)}, bf16[2,2,32,1280]{3,2,1,0:T(8,128)(2,1)S(1)}, u32[]{:S(2)}, u32[]{:S(2)}) %collective-permute-start.13) | collective-permute-done | bytes 327712 | tf_op jit(solution)/shard_map/ppermute | solution.py:50
  125.4 1.0 fusion.13
  126.4 2.2 %collective-permute-start.10 = (f32[640]{0:T(1024)S(1)}, f32[640]{0:T(1024)S(1)}, u32[]{:S(2)}, u32[]{:S(2)}) collective-permute-start(f32[640]{0:T(1024)S(1)} %pad_maximum_fusion.8), channel_id=1, source_target_pairs={{0,4},{4,0},{1,5},{5,1},{2,6},{6,2},{3,7},{7,3},{8,12},{12,8},{9,1... | collective-permute-start | bytes 7688 | tf_op jit(solution)/shard_map/ppermute | solution.py:50
  128.6 0.6 copy.27.refs_1_
  129.3 2.3 %collective-permute-done.10 = f32[640]{0:T(1024)S(1)} collective-permute-done((f32[640]{0:T(1024)S(1)}, f32[640]{0:T(1024)S(1)}, u32[]{:S(2)}, u32[]{:S(2)}) %collective-permute-start.10) | collective-permute-done | bytes 2592 | tf_op jit(solution)/shard_map/ppermute | solution.py:50
  131.7 0.5 collective-permute-start.17
  132.6 0.6 gather_fusion
  133.4 0.7 reshape.150.refs_3_
  134.1 0.9 copy.26.refs_2_
  134.9 1.2 pad_maximum_fusion
  136.1 1.2 copy.24
  137.4 13.8 %shard_map.173 = (bf16[512,512]{1,0:T(8,128)(2,1)}, bf16[512,512]{1,0:T(8,128)(2,1)}, bf16[512,512]{1,0:T(8,128)(2,1)}) custom-call(s32[9]{0:T(128)} %stack.92.refs_0_, bf16[4,1,2048]{2,1,0:T(2,128)(2,1)} %copy.27.refs_1_, f32[512,1]{1,0:T(8,128)} %copy.26.refs_2_, s32[2,512]{1,0:T(2,128)} %reshape.150.refs_3_, bf16[512,1280]{1,0:T(8,128)(2,1)} %bitcast.63, ...), custom_call_target="tpu_custom_call" | custom-call | flops 4831838208 | bytes 18874368 | tf_op jit(solution)/shard_map/pallas_call | solution.py:141
  151.2 2.4 %collective-permute-start.20 = (bf16[512,512]{1,0:T(8,128)(2,1)}, bf16[512,512]{1,0:T(8,128)(2,1)S(1)}, u32[]{:S(2)}, u32[]{:S(2)}) collective-permute-start(bf16[512,512]{1,0:T(8,128)(2,1)} %get-tuple-element.28), channel_id=1, source_target_pairs={{0,4},{4,0},{1,5},{5,1},{2,6},{6,2},{3,7},{7,3},{8,12},{12,8},{9,1... | collective-permute-start | bytes 1572872 | tf_op jit(solution)/shard_map/ppermute | solution.py:50
  153.6 0.9 copy.28.refs_2_
  154.5 1.3 copy-done.7
  155.8 12.2 %shard_map.174 = bf16[512,512]{1,0:T(8,128)(2,1)} custom-call(s32[9]{0:T(128)} %stack.89.refs_0_, bf16[4,1,2048]{2,1,0:T(2,128)(2,1)} %copy.27.refs_1_, f32[512,1]{1,0:T(8,128)} %copy.28.refs_2_, s32[2,512]{1,0:T(2,128)} %reshape.150.refs_3_, bf16[512,512]{1,0:T(8,128)(2,1)} %get-tuple-element.26.refs_4_, bf16[512,512]{1,0:T(8,128)(2,1)} %get-tuple-element.27.refs_5_, ...), custom_call_target="tpu_custom_call" | custom-call | flops 4831838208 | bytes 18874368 | tf_op jit(solution)/shard_map/pallas_call | solution.py:141
  168.0 2.5 %maximum_select_fusion = bf16[512,1024]{1,0:T(8,128)(2,1)} fusion(bf16[512,512]{1,0:T(8,128)(2,1)S(1)} %collective-permute-done.20, bf16[512,512]{1,0:T(8,128)(2,1)} %shard_map.174, pred[]{:T(512)S(6)} %eq.10), kind=kLoop, calls=%fused_computation.4 | loop fusion | flops 4718592 | bytes 2097153 | tf_op jit(solution)/shard_map/jit(_where)/select_n | solution.py:320
  (100 shorter events, 2.7 us)
Async XLA Ops:
  6.5 10.2 %copy-start.12 = (bf16[1280]{0:T(1024)(128)(2,1)S(1)}, bf16[1280]{0:T(1024)(128)(2,1)}, u32[]{:S(2)}) copy-start(bf16[1280]{0:T(1024)(128)(2,1)} %param.28) | copy-start | bytes 7684
  6.5 10.3 %copy-start.13 = (bf16[1280]{0:T(1024)(128)(2,1)S(1)}, bf16[1280]{0:T(1024)(128)(2,1)}, u32[]{:S(2)}) copy-start(bf16[1280]{0:T(1024)(128)(2,1)} %param.29) | copy-start | bytes 7684
  6.5 14.0 %copy-start.1 = (bf16[2,256,1280]{2,1,0:T(8,128)(2,1)S(1)}, bf16[2,256,1280]{2,1,0:T(8,128)(2,1)}, u32[]{:S(2)}) copy-start(bf16[2,256,1280]{2,1,0:T(8,128)(2,1)} %image_ref.1) | copy-start | bytes 3932164
  6.5 14.0 %copy-start.6 = (s32[2]{0:T(128)S(1)}, s32[2]{0:T(128)}, u32[]{:S(2)}) copy-start(s32[2]{0:T(128)} %count_ref.1) | copy-start | bytes 28
  6.5 14.0 %copy-start = (bf16[64,1280]{1,0:T(8,128)(2,1)S(1)}, bf16[64,1280]{1,0:T(8,128)(2,1)}, u32[]{:S(2)}) copy-start(bf16[64,1280]{1,0:T(8,128)(2,1)} %latent_ref.1) | copy-start | bytes 491524
  6.5 14.0 %copy-start.2 = (bf16[1280,384]{1,0:T(8,128)(2,1)S(1)}, bf16[1280,384]{1,0:T(8,128)(2,1)}, u32[]{:S(2)}) copy-start(bf16[1280,384]{1,0:T(8,128)(2,1)} %query_ref.1) | copy-start | bytes 2949124
  6.6 130.8 %all-gather.3.cloned.1.call-start = ((), (), s32[]{:S(2)}) async-start(), calls=%async_computation | async-start | bytes 11354112 | tf_op jit(solution)/shard_map/all_gather | solution.py:255
  7.8 7.7 %collective-permute-start = (bf16[168,512]{1,0:T(8,128)(2,1)S(1)}, bf16[168,512]{1,0:T(8,128)(2,1)S(1)}, u32[]{:S(2)}, u32[]{:S(2)}) collective-permute-start(bf16[168,512]{1,0:T(8,128)(2,1)S(1)} %constant_dynamic-slice_fusion), channel_id=1, source_target_pairs={{0,4},{4,0},{1,5},{5,1},{2,6},{6,2},{3,7},{7,3},{8,12},{12,8},{9,1... | collective-permute-start | bytes 516104 | tf_op jit(solution)/shard_map/ppermute | solution.py:50
  16.7 137.8 %collective-permute-start.18 = (bf16[512,2048]{1,0:T(8,128)(2,1)}, bf16[512,2048]{1,0:T(8,128)(2,1)}, u32[]{:S(2)}, u32[]{:S(2)}) collective-permute-start(bf16[512,2048]{1,0:T(8,128)(2,1)} %refs_7_.1), channel_id=1, source_target_pairs={{0,1},{1,0},{2,3},{3,2},{4,5},{5,4},{6,7},{7,6},{8,9},{9,8},{10,11... | collective-permute-start | bytes 6291464 | tf_op jit(solution)/shard_map/ppermute | solution.py:50
  16.8 12.8 %copy-start.14 = (s32[2,2]{1,0:T(2,128)S(1)}, s32[2,2]{1,0:T(2,128)}, u32[]{:S(2)}) copy-start(s32[2,2]{1,0:T(2,128)} %param.26) | copy-start | bytes 52
  16.8 48.4 %collective-permute-start.1 = (bf16[512,2048]{1,0:T(8,128)(2,1)}, bf16[512,2048]{1,0:T(8,128)(2,1)}, u32[]{:S(2)}, u32[]{:S(2)}) collective-permute-start(bf16[512,2048]{1,0:T(8,128)(2,1)} %refs_7_.1), channel_id=1, source_target_pairs={{0,2},{2,0},{1,3},{3,1},{4,6},{6,4},{5,7},{7,5},{8,10},{10,8},{9,1... | collective-permute-start | bytes 6291464 | tf_op jit(solution)/shard_map/ppermute | solution.py:50
  18.4 49.3 %collective-permute-start.2 = (bf16[512,2048]{1,0:T(8,128)(2,1)}, bf16[512,2048]{1,0:T(8,128)(2,1)}, u32[]{:S(2)}, u32[]{:S(2)}) collective-permute-start(bf16[512,2048]{1,0:T(8,128)(2,1)} %refs_7_.1), channel_id=1, source_target_pairs={{0,6},{2,4},{4,2},{6,0},{1,7},{3,5},{5,3},{7,1},{8,14},{10,12},{12... | collective-permute-start | bytes 6291464 | tf_op jit(solution)/shard_map/ppermute | solution.py:50
  20.5 1.2 copy-start.3
  21.7 1.2 copy-start.4
  22.9 1.2 copy-start.5
  28.8 10.4 %copy-start.10 = (bf16[2048]{0:T(1024)(128)(2,1)S(1)}, bf16[2048]{0:T(1024)(128)(2,1)}, u32[]{:S(2)}) copy-start(bf16[2048]{0:T(1024)(128)(2,1)} %param.19) | copy-start | bytes 12292
  28.9 11.7 %collective-permute-start.3 = (f32[2,32,1280]{2,1,0:T(8,128)S(1)}, f32[2,32,1280]{2,1,0:T(8,128)S(1)}, u32[]{:S(2)}, u32[]{:S(2)}) collective-permute-start(f32[2,32,1280]{2,1,0:T(8,128)S(1)} %dynamic-slice_bitcast_fusion), channel_id=1, source_target_pairs={{0,1},{1,0},{2,3},{3,2},{4,5},{5,4},{6,7},{7,6},{8,9},{9,8},{10,11... | collective-permute-start | bytes 983048 | tf_op jit(solution)/shard_map/ppermute | solution.py:37
  29.7 9.4 %collective-permute-start.4 = (f32[4]{0:T(128)S(1)}, f32[4]{0:T(128)S(1)}, u32[]{:S(2)}, u32[]{:S(2)}) collective-permute-start(f32[4]{0:T(128)S(1)} %convert_element_type.39), channel_id=1, source_target_pairs={{0,8},{8,16},{16,24},{24,32},{32,40},{40,48},{48,56},{56,64},{64,7... | collective-permute-start | bytes 56 | tf_op jit(solution)/shard_map/ppermute | solution.py:41
  39.3 1.3 collective-permute-start.5
  40.6 33.8 %copy-start.11 = (bf16[1280]{0:T(1024)(128)(2,1)S(1)}, bf16[1280]{0:T(1024)(128)(2,1)}, u32[]{:S(2)}) copy-start(bf16[1280]{0:T(1024)(128)(2,1)} %param.30) | copy-start | bytes 7684
  70.0 28.6 %collective-permute-start.6 = (bf16[256,2048]{1,0:T(8,128)(2,1)}, bf16[256,2048]{1,0:T(8,128)(2,1)S(1)}, u32[]{:S(2)}, u32[]{:S(2)}) collective-permute-start(bf16[256,2048]{1,0:T(8,128)(2,1)} %slice.65), channel_id=1, source_target_pairs={{0,2},{2,0},{1,3},{3,1},{4,6},{6,4},{5,7},{7,5},{8,10},{10,8},{9,1... | collective-permute-start | bytes 3145736 | tf_op jit(solution)/shard_map/ppermute | solution.py:50
  72.3 26.3 %collective-permute-start.7 = (bf16[256,2048]{1,0:T(8,128)(2,1)}, bf16[256,2048]{1,0:T(8,128)(2,1)S(1)}, u32[]{:S(2)}, u32[]{:S(2)}) collective-permute-start(bf16[256,2048]{1,0:T(8,128)(2,1)} %slice.66), channel_id=1, source_target_pairs={{0,6},{2,4},{4,2},{6,0},{1,7},{3,5},{5,3},{7,1},{8,14},{10,12},{12... | collective-permute-start | bytes 3145736 | tf_op jit(solution)/shard_map/ppermute | solution.py:50
  75.7 21.0 %collective-permute-start.9 = (f32[2,2688]{1,0:T(2,128)S(1)}, f32[2,2688]{1,0:T(2,128)S(1)}, u32[]{:S(2)}, u32[]{:S(2)}) collective-permute-start(f32[2,2688]{1,0:T(2,128)S(1)} %pad_maximum_fusion.7), channel_id=1, source_target_pairs={{0,2},{2,0},{1,3},{3,1},{4,6},{6,4},{5,7},{7,5},{8,10},{10,8},{9,1... | collective-permute-start | bytes 64520 | tf_op jit(solution)/shard_map/ppermute | solution.py:50
  77.4 21.2 %collective-permute-start.8 = (f32[32,1280]{1,0:T(8,128)S(1)}, f32[32,1280]{1,0:T(8,128)S(1)}, u32[]{:S(2)}, u32[]{:S(2)}) collective-permute-start(f32[32,1280]{1,0:T(8,128)S(1)} %dynamic-slice_bitcast_fusion.1), channel_id=1, source_target_pairs={{0,2},{2,0},{1,3},{3,1},{4,6},{6,4},{5,7},{7,5},{8,10},{10,8},{9,1... | collective-permute-start | bytes 491528 | tf_op jit(solution)/shard_map/ppermute | solution.py:37
  98.6 4.3 %copy-start.8 = (bf16[256,2048]{1,0:T(8,128)(2,1)}, bf16[256,2048]{1,0:T(8,128)(2,1)S(1)}, u32[]{:S(2)}) copy-start(bf16[256,2048]{1,0:T(8,128)(2,1)S(1)} %collective-permute-done.6.refs_8_) | copy-start | bytes 3145732
  98.7 4.3 %copy-start.9 = (bf16[256,2048]{1,0:T(8,128)(2,1)}, bf16[256,2048]{1,0:T(8,128)(2,1)S(1)}, u32[]{:S(2)}) copy-start(bf16[256,2048]{1,0:T(8,128)(2,1)S(1)} %collective-permute-done.7.refs_9_) | copy-start | bytes 3145732
  99.1 11.9 %collective-permute-start.11 = (bf16[32,1280]{1,0:T(8,128)(2,1)S(1)}, bf16[32,1280]{1,0:T(8,128)(2,1)S(1)}, u32[]{:S(2)}, u32[]{:S(2)}) collective-permute-start(bf16[32,1280]{1,0:T(8,128)(2,1)S(1)} %multiply_convert_fusion), channel_id=1, source_target_pairs={{0,8},{8,16},{16,24},{24,32},{32,40},{40,48},{48,56},{56,64},{64,7... | collective-permute-start | bytes 245768 | tf_op jit(solution)/shard_map/ppermute | solution.py:41
  103.0 34.4 %collective-permute-start.15 = (bf16[512,2048]{1,0:T(8,128)(2,1)}, bf16[512,2048]{1,0:T(8,128)(2,1)}, u32[]{:S(2)}, u32[]{:S(2)}) collective-permute-start(bf16[512,2048]{1,0:T(8,128)(2,1)} %collective-permute-done.2.refs_6_), channel_id=1, source_target_pairs={{0,1},{1,0},{2,3},{3,2},{4,5},{5,4},{6,7},{7,6},{8,9},{9,8},{10,11... | collective-permute-start | bytes 6291464 | tf_op jit(solution)/shard_map/ppermute | solution.py:50
  103.1 51.4 %collective-permute-start.19 = (bf16[512,2048]{1,0:T(8,128)(2,1)}, bf16[512,2048]{1,0:T(8,128)(2,1)S(1)}, u32[]{:S(2)}, u32[]{:S(2)}) collective-permute-start(bf16[512,2048]{1,0:T(8,128)(2,1)} %collective-permute-done.1.refs_9_), channel_id=1, source_target_pairs={{0,1},{1,0},{2,3},{3,2},{4,5},{5,4},{6,7},{7,6},{8,9},{9,8},{10,11... | collective-permute-start | bytes 6291464 | tf_op jit(solution)/shard_map/ppermute | solution.py:50
  111.0 5.6 %collective-permute-start.12 = (bf16[2,32,1280]{2,1,0:T(8,128)(2,1)S(1)}, bf16[2,32,1280]{2,1,0:T(8,128)(2,1)S(1)}, u32[]{:S(2)}, u32[]{:S(2)}) collective-permute-start(bf16[2,32,1280]{2,1,0:T(8,128)(2,1)S(1)} %get-tuple-element.40), channel_id=1, source_target_pairs={{0,2},{2,0},{1,3},{3,1},{4,6},{6,4},{5,7},{7,5},{8,10},{10,8},{9,1... | collective-permute-start | bytes 491528 | tf_op jit(solution)/shard_map/ppermute | solution.py:50
  116.7 8.7 %collective-permute-start.13 = (bf16[2,2,32,1280]{3,2,1,0:T(8,128)(2,1)S(1)}, bf16[2,2,32,1280]{3,2,1,0:T(8,128)(2,1)S(1)}, u32[]{:S(2)}, u32[]{:S(2)}) collective-permute-start(bf16[2,2,32,1280]{3,2,1,0:T(8,128)(2,1)S(1)} %get-tuple-element.36), channel_id=1, source_target_pairs={{0,4},{4,0},{1,5},{5,1},{2,6},{6,2},{3,7},{7,3},{8,12},{12,8},{9,1... | collective-permute-start | bytes 983048 | tf_op jit(solution)/shard_map/ppermute | solution.py:50
  126.3 5.4 %collective-permute-start.14 = (bf16[4,2,32,1280]{3,2,1,0:T(8,128)(2,1)}, bf16[4,2,32,1280]{3,2,1,0:T(8,128)(2,1)}, u32[]{:S(2)}, u32[]{:S(2)}) collective-permute-start(bf16[4,2,32,1280]{3,2,1,0:T(8,128)(2,1)} %get-tuple-element.30), channel_id=1, source_target_pairs={{0,1},{1,0},{2,3},{3,2},{4,5},{5,4},{6,7},{7,6},{8,9},{9,8},{10,11... | collective-permute-start | bytes 1966088 | tf_op jit(solution)/shard_map/ppermute | solution.py:37
  126.4 5.2 %collective-permute-start.10 = (f32[640]{0:T(1024)S(1)}, f32[640]{0:T(1024)S(1)}, u32[]{:S(2)}, u32[]{:S(2)}) collective-permute-start(f32[640]{0:T(1024)S(1)} %pad_maximum_fusion.8), channel_id=1, source_target_pairs={{0,4},{4,0},{1,5},{5,1},{2,6},{6,2},{3,7},{7,3},{8,12},{12,8},{9,1... | collective-permute-start | bytes 7688 | tf_op jit(solution)/shard_map/ppermute | solution.py:50
  131.6 5.8 %collective-permute-start.16 = (bf16[256,2048]{1,0:T(8,128)(2,1)}, bf16[256,2048]{1,0:T(8,128)(2,1)}, u32[]{:S(2)}, u32[]{:S(2)}) collective-permute-start(bf16[256,2048]{1,0:T(8,128)(2,1)} %copy-done.8), channel_id=1, source_target_pairs={{0,1},{1,0},{2,3},{3,2},{4,5},{5,4},{6,7},{7,6},{8,9},{9,8},{10,11... | collective-permute-start | bytes 3145736 | tf_op jit(solution)/shard_map/ppermute | solution.py:50
  131.7 5.6 %collective-permute-start.17 = (bf16[256,2048]{1,0:T(8,128)(2,1)}, bf16[256,2048]{1,0:T(8,128)(2,1)}, u32[]{:S(2)}, u32[]{:S(2)}) collective-permute-start(bf16[256,2048]{1,0:T(8,128)(2,1)} %copy-done.9), channel_id=1, source_target_pairs={{0,1},{1,0},{2,3},{3,2},{4,5},{5,4},{6,7},{7,6},{8,9},{9,8},{10,11... | collective-permute-start | bytes 3145736 | tf_op jit(solution)/shard_map/ppermute | solution.py:50
  151.2 16.8 %collective-permute-start.20 = (bf16[512,512]{1,0:T(8,128)(2,1)}, bf16[512,512]{1,0:T(8,128)(2,1)S(1)}, u32[]{:S(2)}, u32[]{:S(2)}) collective-permute-start(bf16[512,512]{1,0:T(8,128)(2,1)} %get-tuple-element.28), channel_id=1, source_target_pairs={{0,4},{4,0},{1,5},{5,1},{2,6},{6,2},{3,7},{7,3},{8,12},{12,8},{9,1... | collective-permute-start | bytes 1572872 | tf_op jit(solution)/shard_map/ppermute | solution.py:50
  154.5 1.3 copy-start.7
Sparse Core Ops, SparseCore 0:
  16.8 112.5 all-gather.2

commit v4 on v3

--- a/solution.py
+++ b/solution.py
@@ -50,7 +50,9 @@
     return lax.ppermute(x, axes, [(i, count - 1 - i) for i in range(count)])
 
 
-AHEAD = 2
+CHUNKS = 8
+DEEP = D // CHUNKS
+WIDE = DEEP // (2 * ROWS)
 
 
 def attend_kernel(counts, fresh, *refs):
@@ -69,38 +71,48 @@
         pair_sem, side_buf, pair_buf = refs.pop(), refs.pop(), refs.pop()
     text_buf, weight_buf, acc_ref, text_sem, weight_sem = refs
 
-    def fetch(k):
+    def fetch(chunk):
+        k, i = divmod(chunk, CHUNKS // NY)
         height = TOK // len(blocks[k])
         for j, ref in enumerate(blocks[k]):
-            pltpu.make_async_copy(ref, text_buf.at[k, pl.ds(j * height, height), :], text_sem.at[k]).start()
+            pltpu.make_async_copy(
+                ref.at[:, pl.ds(i * DEEP, DEEP)],
+                text_buf.at[chunk, pl.ds(j * height, height), :],
+                text_sem.at[chunk],
+            ).start()
         pltpu.make_async_copy(
-            weight_ref.at[pl.ds(where_ref[1 + k] * NZ, NZ), pl.ds(0, 2 * ROWS), :], weight_buf.at[k], weight_sem.at[k]
+            weight_ref.at[pl.ds(i * WIDE, WIDE), where_ref[1 + k], pl.ds(0, 2 * ROWS), :],
+            weight_buf.at[chunk],
+            weight_sem.at[chunk],
         ).start()
 
-    for k in range(AHEAD):
-        fetch(k)
+    fetch(0)
     if fresh:
-        count = pair_buf.shape[1]
-        pltpu.make_async_copy(weight_ref.at[:, pl.ds(2 * ROWS, count), :], pair_buf, pair_sem.at[0]).start()
-    for k in range(NY):
-        pltpu.make_async_copy(text_buf.at[k], text_buf.at[k], text_sem.at[k]).wait()
-        pltpu.make_async_copy(weight_buf.at[k], weight_buf.at[k], weight_sem.at[k]).wait()
-        if k + AHEAD < NY:
-            fetch(k + AHEAD)
+        count = pair_buf.shape[2]
+        pltpu.make_async_copy(weight_ref.at[:, :, pl.ds(2 * ROWS, count), :], pair_buf, pair_sem.at[0]).start()
+    ahead = 4 if fresh else CHUNKS
+    for chunk in range(1, ahead):
+        fetch(chunk)
+    for chunk in range(CHUNKS):
+        k, i = divmod(chunk, CHUNKS // NY)
+        pltpu.make_async_copy(text_buf.at[chunk], text_buf.at[chunk], text_sem.at[chunk]).wait()
+        pltpu.make_async_copy(weight_buf.at[chunk], weight_buf.at[chunk], weight_sem.at[chunk]).wait()
+        if chunk + ahead < CHUNKS:
+            fetch(chunk + ahead)
         part = jnp.dot(
-            text_buf[k] * gain_ref[where_ref[1 + NY + k]],
-            weight_buf[k].reshape(D // NY, COLS),
+            text_buf[chunk] * gain_ref[where_ref[1 + NY + k], :, pl.ds(i * DEEP, DEEP)],
+            weight_buf[chunk].reshape(DEEP, COLS),
             preferred_element_type=jnp.float32,
         )
-        acc_ref[...] = part if k == 0 else acc_ref[...] + part
-        if fresh and k == 1:
+        acc_ref[...] = part if chunk == 0 else acc_ref[...] + part
+        if fresh and chunk == 3:
             pltpu.make_async_copy(pair_buf, pair_buf, pair_sem.at[0]).wait()
-            half = pair_buf.shape[1] // 2
+            half = pair_buf.shape[2] // 2
             tall = NZ * half
 
             @pl.loop(0, NY)
             def _(group):
-                rows = pair_buf[pl.ds(group * NZ, NZ)].astype(jnp.float32)
+                rows = pair_buf[:, group].astype(jnp.float32)
                 start = pl.multiple_of(group * tall, tall)
                 for i in range(2):
                     side = rows[:, i * half : (i + 1) * half].reshape(tall, COLS)
@@ -117,7 +129,7 @@
     hidden = jnp.where(seen, 0.0, FILL)
     for head in range(COLS // HD):
         cols = pl.ds(head * HD, HD)
-        queries = (acc_ref[:, cols] * scale_ref[...]).astype(jnp.bfloat16)
+        queries = (acc_ref[:, cols] * scale_ref[pl.ds(TOK if fresh else 0, TOK), :]).astype(jnp.bfloat16)
         scores = lax.dot_general(
             queries, key_ref[:, cols], (((1,), (1,)), ((), ())), preferred_element_type=jnp.float32
         )
@@ -137,29 +149,29 @@
     vmem = pl.BlockSpec(memory_space=pltpu.VMEM)
     anywhere = pl.BlockSpec(memory_space=pl.ANY)
     result = jax.ShapeDtypeStruct((TOK, COLS), jnp.bfloat16)
-    pairs = weight.shape[1] - 2 * ROWS
+    pairs = weight.shape[2] - 2 * ROWS
     return pl.pallas_call(
         functools.partial(attend_kernel, counts, fresh),
         out_shape=[result] * (3 if fresh else 1),
         in_specs=[pl.BlockSpec(memory_space=pltpu.SMEM)] + [vmem] * (3 + len(rows)) + [anywhere] * (1 + sum(counts)),
         out_specs=[vmem] * (3 if fresh else 1),
         scratch_shapes=[
-            pltpu.VMEM((NY, TOK, D // NY), jnp.bfloat16),
-            pltpu.VMEM((NY, NZ, 2 * ROWS, COLS), jnp.bfloat16),
+            pltpu.VMEM((CHUNKS, TOK, DEEP), jnp.bfloat16),
+            pltpu.VMEM((CHUNKS, WIDE, 2 * ROWS, COLS), jnp.bfloat16),
             pltpu.VMEM((TOK, COLS), jnp.float32),
-            pltpu.SemaphoreType.DMA((NY,)),
-            pltpu.SemaphoreType.DMA((NY,)),
+            pltpu.SemaphoreType.DMA((CHUNKS,)),
+            pltpu.SemaphoreType.DMA((CHUNKS,)),
         ]
         + (
             [
-                pltpu.VMEM((NY * NZ, pairs, COLS), jnp.bfloat16),
+                pltpu.VMEM((NZ, NY, pairs, COLS), jnp.bfloat16),
                 pltpu.VMEM((2, VW, COLS), jnp.bfloat16),
                 pltpu.SemaphoreType.DMA((1,)),
             ]
             if fresh
             else []
         ),
-        compiler_params=pltpu.CompilerParams(vmem_limit_bytes=56 * 1024 * 1024),
+        compiler_params=pltpu.CompilerParams(vmem_limit_bytes=62 * 1024 * 1024),
         cost_estimate=pl.CostEstimate(
             flops=2 * TOK * COLS * (D + 2 * KEYS), bytes_accessed=18 << 20, transcendentals=TOK * KEYS * 4
         ),
@@ -240,9 +252,11 @@
     xh, xl, core = lax.axis_index("xh"), lax.axis_index("xl"), lax.axis_index("core")
     x = xh * 2 + xl
 
-    block = jnp.concatenate([query_weight, key_weight, value_weight], axis=0)
-    mine = lax.dynamic_slice_in_dim(block, xh * COLS, COLS, 1)
-    other = flipped(lax.dynamic_slice_in_dim(block, (1 - xh) * COLS, COLS, 1), ("xh",))
+    def side(which):
+        parts = (query_weight, key_weight, value_weight)
+        return jnp.concatenate([lax.dynamic_slice_in_dim(one, which * COLS, COLS, 1) for one in parts], axis=0)
+
+    mine, other = side(xh), flipped(side(1 - xh), ("xh",))
     low = jnp.where(xh == 0, mine, other)
     high = jnp.where(xh == 0, other, mine)
     part = key_weight.shape[0]
@@ -252,71 +266,82 @@
     pairs = jnp.dot(
         (block_of[:, None] == order[None, :]).astype(jnp.bfloat16), pairs, preferred_element_type=jnp.float32
     ).astype(jnp.bfloat16)
-    weight = lax.all_gather(jnp.concatenate([low[:ROWS], high[:ROWS], pairs], axis=0), ("y", "z"), axis=0)
+    weight = lax.all_gather(jnp.concatenate([low[:ROWS], high[:ROWS], pairs], axis=0), ("z", "y"), axis=0)
+    weight = weight.reshape(NZ, NY, -1, COLS)
 
     source = text_rows.astype(jnp.float32)
     power = jnp.sum(source * source, axis=-1)
     live_slot = jnp.arange(2, dtype=jnp.int32) < image_counts[0]
     span_bounds = jnp.where(live_slot[None, :], image_spans, 0)
+    mix = resample(
+        images, patch_counts, latents, latent_gain, context_gain, res_query, res_key, res_value, res_output
+    ).reshape(2, 2, LAT // 2, VW)
     small = jnp.concatenate(
         [
             power,
             text_gain.astype(jnp.float32),
             span_bounds.reshape(4).astype(jnp.float32),
-            next_pair(span_bounds.reshape(4).astype(jnp.float32)),
-            jnp.zeros((120,), jnp.float32),
+            next_pair(after(span_bounds.reshape(4).astype(jnp.float32), mix)),
+            jnp.zeros((4 * VW - TOK - D // NY - 8,), jnp.float32),
         ]
-    )
-
-    mix = resample(
-        images, patch_counts, latents, latent_gain, context_gain, res_query, res_key, res_value, res_output
-    ).reshape(2, 2, LAT // 2, VW)
-    small = small[None]
-    first = lax.dynamic_index_in_dim(mix, core, 1, keepdims=False)
-    first = first + turned(lax.dynamic_index_in_dim(mix, 1 - core, 1, keepdims=False), "core", 1, 2)
-    small = jnp.concatenate([small, flipped(small, ("core",))], axis=0)
+    ).reshape(1, 4, VW)
     text_out = after(text_rows, other)
-    near_text, cross_text = flipped(text_out, ("xl",)), flipped(text_out, ("xh", "xl"))
-    near_text, cross_text, first, small = lax.optimization_barrier((near_text, cross_text, first, small))
     cut = TOK // 2
-    text_top = flipped(cross_text[:cut], ("xl",))
-    text_bottom = flipped(near_text[cut:], ("xh", "xl"))
-    total = lax.dynamic_index_in_dim(first, xl, 0, keepdims=False)
-    total = total + turned(lax.dynamic_index_in_dim(first, 1 - xl, 0, keepdims=False), "xl", 1, 2)
-    small = jnp.concatenate([small, flipped(small, ("xl",))], axis=0)
-    text_top, text_bottom, total, small = lax.optimization_barrier((text_top, text_bottom, total, small))
-    short = jnp.concatenate([jnp.sum(small[:, :TOK], axis=0), small[0, TOK + D // NY :]])
-    short_other = flipped(short, ("xh",))
+    halves = (text_out[:cut], text_out[cut:])
+    near_bottom, cross_top = flipped(halves[1], ("xl",)), flipped(halves[0], ("xh", "xl"))
+    cross_top, near_bottom, mix = lax.optimization_barrier((cross_top, near_bottom, mix))
+    sent = jnp.concatenate(
+        [lax.dynamic_index_in_dim(mix, 1 - core, 1, keepdims=False).reshape(LAT, VW), small[0]], axis=0
+    )
+    got = flipped(sent, ("core",))
+    first = lax.dynamic_index_in_dim(mix, core, 1, keepdims=False) + got[:LAT].reshape(2, LAT // 2, VW)
+    small = jnp.stack([small[0], got[LAT:]])
+    sent = jnp.concatenate([lax.dynamic_index_in_dim(first, 1 - xl, 0, keepdims=False), small.reshape(8, VW)], axis=0)
+    got = flipped(sent, ("xl",))
+    small = small.reshape(2, 4 * VW)
+    short = jnp.concatenate([jnp.sum(small[:, :TOK], axis=0), small[0, TOK + D // NY :][:128]])
+    cross_top, near_bottom, *halves, got = lax.optimization_barrier((cross_top, near_bottom, *halves, got))
+    near_text = [flipped(halves[0], ("xl",)), near_bottom]
+    cross_text = [cross_top, flipped(halves[1], ("xh", "xl"))]
+    far_text = [flipped(cross_top, ("xl",)), flipped(near_bottom, ("xh", "xl"))]
+    total = lax.dynamic_index_in_dim(first, xl, 0, keepdims=False) + got[: LAT // 2]
+    small = jnp.concatenate([small, got[LAT // 2 :].reshape(2, 4 * VW)], axis=0)
 
     base = lax.dynamic_slice_in_dim(latents, core * (LAT // 2), LAT // 2, 0).astype(jnp.float32)
     piece = layer_norm(base + total, final_gain.astype(jnp.float32)).astype(jnp.bfloat16)
     both = jnp.stack([next_pair(piece), piece])
-
-    swap = lambda rows: flipped(rows, ("core",))
-    our_blocks = [[text_rows], [swap(text_rows)], [near_text], [swap(near_text)]]
-    their_blocks = [[cross_text], [swap(cross_text)], [text_top, text_bottom], [swap(text_top), swap(text_bottom)]]
-    scales = [lax.rsqrt(one[:TOK] / D + EPS_TEXT).reshape(TOK, 1) for one in (short, short_other)]
+    near_text[0], cross_text[1], *far_text, both = lax.optimization_barrier(
+        (near_text[0], cross_text[1], *far_text, both)
+    )
+    both, short_cross, short_far = lax.optimization_barrier(
+        (jnp.stack([both, flipped(both, ("xl",))]), flipped(short, ("xh", "xl")), flipped(short, ("xh",)))
+    )
+
+    swap = lambda rows: [flipped(one, ("core",)) for one in rows]
+    our_blocks = [[text_rows], swap([text_rows]), near_text, swap(near_text)]
+    their_blocks = [cross_text, swap(cross_text), far_text, swap(far_text)]
+    power = jnp.concatenate([jnp.sum(small[:, :TOK], axis=0), short_cross[:TOK] + short_far[:TOK]])
+    scale = lax.rsqrt(power / D + EPS_TEXT).reshape(2 * TOK, 1)
     gain = small[:, TOK : TOK + D // NY].astype(jnp.bfloat16).reshape(NY, 1, D // NY)
-    spans = [one[TOK : TOK + 8].reshape(2, 2, 2) for one in (short, short_other)]
+    spans = [one[TOK : TOK + 8].reshape(2, 2, 2) for one in (short, short_far)]
     spans = jnp.where(xh == 0, jnp.concatenate(spans, axis=2), jnp.concatenate(spans[::-1], axis=2))
     near = jnp.stack([spans[1], spans[0]], axis=1)
     near = jnp.take(near, x ^ jnp.arange(NX), axis=2).transpose(0, 2, 1).reshape(2, 8).astype(jnp.int32)
-    bounds = jnp.repeat(near, LAT, axis=1)
-
-    both = jnp.stack([both, flipped(both, ("xl",))])
+    bounds = jnp.tile(jnp.repeat(near, LAT // 2, axis=1), (1, 2))
+
     both = jnp.stack([both, flipped(both, ("xh",))])
     around = jnp.stack([both[0, 0], both[0, 1], both[1, 0], both[1, 1]])
-    resampled = jnp.stack([around, turned(around, "core", 1, 2)], axis=2).reshape(KEYS, VW)
-
-    def half(blocks, which, own_scale, others, rows):
+    resampled = jnp.concatenate([around, turned(around, "core", 1, 2)], axis=0).reshape(KEYS, VW)
+
+    def half(blocks, which, others, rows):
         places = [2 * p + q for p, q in ((others, core), (others, 1 - core), (1 - others, core), (1 - others, 1 - core))]
         turns = [place ^ (2 * xl + core) for place in places]
         where = jnp.stack([(y * NZ + z) * (2 * TOK) + which * TOK, *places, *turns]).astype(jnp.int32)
-        return attend(blocks, where, gain, own_scale, bounds, rows, weight)
-
-    theirs, keys, values = half(their_blocks, 1 - xh, scales[1], 1 - xl, (resampled,))
+        return attend(blocks, where, gain, scale, bounds, rows, weight)
+
+    theirs, keys, values = half(their_blocks, 1 - xh, 1 - xl, (resampled,))
     received = flipped(theirs, ("xh",))
-    (ours,) = half(our_blocks, xh, scales[0], xl, (keys, values))
+    (ours,) = half(our_blocks, xh, xl, (keys, values))
     return jnp.where(
         xh == 0,
         jnp.concatenate([ours, received], axis=1),

time: 178 us -> 172 us (0.966)
  local copies, waits for them, and re-layouts: 16.6 us -> 10.5 us
  other arithmetic: 9.7 us -> 6.71 us
  waiting for transfers between devices: 78.3 us -> 81.1 us
    ppermute x16 -> x21, waiting for transfers between devices: 65.4 us -> 76.1 us  [flipped(): return lax.ppermute(x, axes, [(i, count - 1 - i) for i in range(count)])]
    ppermute x2, waiting for transfers between devices: 10.9 us -> 4.95 us  [next_pair(): return lax.ppermute(x, ('y', 'z'), [(i, i + 1) for i in range(NY * NZ - 1)])]
    unnamed x30 -> x38, local copies, waits for them, and re-layouts: 4.95 us -> 0.76 us
    another operation x4 -> x5, other arithmetic: 2.23 us -> 0.24 us  [the longest x2 0.11 us: local(): both = jnp.stack([next_pair(piece), piece])]
    ppermute x3 -> x1, waiting for transfers between devices: 1.83 us -> 0.01 us  [turned(): return lax.ppermute(x, axis, [(i, (i + by) % count) for i in range(count)])]
    dynamic_slice x1 -> x3, local copies, waits for them, and re-layouts: 0.02 us -> 1.82 us  [the longest x2 1.79 us: side(): lax.dynamic_slice_in_dim(one, which * COLS, COLS, 1)]
    slice x4 -> x6, local copies, waits for them, and re-layouts: 4.69 us -> 3.32 us  [the longest x1 3.27 us: local(): halves = (text_out[:cut], text_out[cut:])]
    ppermute x16 -> x21, starting transfers between devices: 19.2 us -> 19.5 us  [flipped(): return lax.ppermute(x, axes, [(i, count - 1 - i) for i in range(count)])]
  transfers between devices with their start and end apart: 22 -> 25, of which waited for: 11 -> 15; matrix products, arithmetic and copies ran while one was open for 9% -> 7% of each run, Pallas kernels for 17% -> 18%
where the time goes in v4:
time: 172 us; the launch traced here: 171 us
  waiting for transfers between devices  81.1 us (47%)
  Pallas kernels  30.5 us (18%)
  starting transfers between devices  27.3 us (16%)
  between operations  14.6 us (8%)
  local copies, waits for them, and re-layouts  10.5 us (6%)
  other arithmetic  6.71 us (4%)
    ppermute x21, waiting for transfers between devices, flipped(): return lax.ppermute(x, axes, [(i, count - 1 - i) for i in range(count)])  76.1 us
    pallas_call x2, Pallas kernels, attend(): pl.pallas_call(functools.partial(attend_kernel, counts, fresh), out_shape...  25.8 us
    ppermute x21, starting transfers between devices, flipped(): return lax.ppermute(x, axes, [(i, count - 1 - i) for i in range(count)])  19.5 us
    ppermute x2, starting transfers between devices, next_pair(): return lax.ppermute(x, ('y', 'z'), [(i, i + 1) for i in range(NY * NZ - 1)])  7.65 us
    ppermute x2, waiting for transfers between devices, next_pair(): return lax.ppermute(x, ('y', 'z'), [(i, i + 1) for i in range(NY * NZ - 1)])  4.95 us
    pallas_call x1, Pallas kernels, resample(): pl.pallas_call(resample_kernel, out_shape=jax.ShapeDtypeStruct((images.sh...  4.68 us
  transfers between devices with their start and end apart: 25, of which 15 were waited for; matrix products, arithmetic and copies ran while one was open for 7% of the time, Pallas kernels for 18%

profile of v4, /device:TPU:24, one launch (start us, length us, event | category | flops | bytes accessed | tf_op | source)
XLA Modules:
  0.0 170.9 jit_solution(14337860963883227806)
XLA Ops:
  6.5 1.0 constant_dynamic-slice_fusion.2
  7.5 0.8 constant_dynamic-slice_fusion
  8.4 3.1 %collective-permute-start.1 = (bf16[168,512]{1,0:T(8,128)(2,1)S(1)}, bf16[168,512]{1,0:T(8,128)(2,1)S(1)}, u32[]{:S(2)}, u32[]{:S(2)}) collective-permute-start(bf16[168,512]{1,0:T(8,128)(2,1)S(1)} %pad_maximum_fusion.5), channel_id=1, source_target_pairs={{0,4},{4,0},{1,5},{5,1},{2,6},{6,2},{3,7},{7,3},{8,12},{12,8},{9,1... | collective-permute-start | bytes 516104 | tf_op jit(solution)/shard_map/ppermute | solution.py:50
  11.5 4.6 %collective-permute-done.1 = bf16[168,512]{1,0:T(8,128)(2,1)S(1)} collective-permute-done((bf16[168,512]{1,0:T(8,128)(2,1)S(1)}, bf16[168,512]{1,0:T(8,128)(2,1)S(1)}, u32[]{:S(2)}, u32[]{:S(2)}) %collective-permute-start.1) | collective-permute-done | bytes 172064 | tf_op jit(solution)/shard_map/ppermute | solution.py:50
  16.4 0.8 pad_maximum_fusion.2
  17.3 3.3 %fusion.15 = (bf16[256,2048]{1,0:T(8,128)(2,1)}, bf16[256,2048]{1,0:T(8,128)(2,1)}) fusion(bf16[512,2048]{1,0:T(8,128)(2,1)} %refs_7_.1), kind=kLoop, calls=%fused_computation.85 | loop fusion | bytes 4194304 | tf_op jit(solution)/shard_map/slice | solution.py:290
  20.6 2.8 %collective-permute-start.2 = (bf16[256,2048]{1,0:T(8,128)(2,1)}, bf16[256,2048]{1,0:T(8,128)(2,1)}, u32[]{:S(2)}, u32[]{:S(2)}) collective-permute-start(bf16[256,2048]{1,0:T(8,128)(2,1)} %get-tuple-element.32), channel_id=1, source_target_pairs={{0,6},{2,4},{4,2},{6,0},{1,7},{3,5},{5,3},{7,1},{8,14},{10,12},{12... | collective-permute-start | bytes 3145736 | tf_op jit(solution)/shard_map/ppermute | solution.py:50
  23.4 0.2 collective-permute-start.3
  23.6 4.7 %shard_map.172 = f32[2,64,1280]{2,1,0:T(8,128)S(1)} custom-call(s32[2]{0:T(128)S(1)} %copy-done.6, bf16[2,256,1280]{2,1,0:T(8,128)(2,1)S(1)} %copy-done.1, bf16[64,1280]{1,0:T(8,128)(2,1)S(1)} %copy-done, bf16[1,1280]{1,0:T(2,128)(2,1)S(1)} %broadcast_in_dim.39.latent_gain_ref, bf16[1,1280]{1,0:T(2,128)(2,1)S(1)} %broadcast_in_dim.40.context_gain_ref, ...), custom_call_target="tpu_custom_call" | custom-call | flops 32212254720 | bytes 8388608 | tf_op jit(solution)/shard_map/pallas_call | solution.py:220
  29.1 3.8 %collective-permute-start = (f32[4]{0:T(128)S(1)}, f32[4]{0:T(128)S(1)}, u32[]{:S(2)}, u32[]{:S(2)}) collective-permute-start(f32[4]{0:T(128)S(1)} %convert_element_type.39), channel_id=1, source_target_pairs={{0,8},{8,16},{16,24},{24,32},{32,40},{40,48},{48,56},{56,64},{64,7... | collective-permute-start | bytes 56 | tf_op jit(solution)/shard_map/ppermute | solution.py:41
  33.0 2.2 %multiply_reduce_fusion = f32[512]{0:T(512)S(1)} fusion(bf16[512,2048]{1,0:T(8,128)(2,1)} %refs_7_.1), kind=kLoop, calls=%fused_computation.1 | loop fusion | flops 3145216 | bytes 2099200 | tf_op jit(solution)/shard_map/reduce_sum | solution.py:273
  35.2 3.4 %collective-permute-done = f32[4]{0:T(128)S(1)} collective-permute-done((f32[4]{0:T(128)S(1)}, f32[4]{0:T(128)S(1)}, u32[]{:S(2)}, u32[]{:S(2)}) %collective-permute-start) | collective-permute-done | bytes 48 | tf_op jit(solution)/shard_map/ppermute | solution.py:41
  38.6 7.5 %collective-permute-done.2.refs_6_ = bf16[256,2048]{1,0:T(8,128)(2,1)} collective-permute-done((bf16[256,2048]{1,0:T(8,128)(2,1)}, bf16[256,2048]{1,0:T(8,128)(2,1)}, u32[]{:S(2)}, u32[]{:S(2)}) %collective-permute-start.2) | collective-permute-done | bytes 1048608 | tf_op jit(solution)/shard_map/ppermute | solution.py:50
  46.2 1.3 collective-permute-done.3.refs_10_
  47.7 0.6 stack.106.refs_0_
  48.3 1.0 collective-permute-done.4
  49.4 0.4 collective-permute-start.5
  50.0 6.7 %collective-permute-done.5 = f32[40,1280]{1,0:T(8,128)S(1)} collective-permute-done((f32[40,1280]{1,0:T(8,128)S(1)}, f32[40,1280]{1,0:T(8,128)S(1)}, u32[]{:S(2)}, u32[]{:S(2)}) %collective-permute-start.5) | collective-permute-done | bytes 204832 | tf_op jit(solution)/shard_map/ppermute | solution.py:50
  57.1 3.8 %collective-permute-start.10 = (bf16[32,1280]{1,0:T(8,128)(2,1)S(1)}, bf16[32,1280]{1,0:T(8,128)(2,1)S(1)}, u32[]{:S(2)}, u32[]{:S(2)}) collective-permute-start(bf16[32,1280]{1,0:T(8,128)(2,1)S(1)} %multiply_convert_fusion), channel_id=1, source_target_pairs={{0,8},{8,16},{16,24},{24,32},{32,40},{40,48},{48,56},{56,64},{64,7... | collective-permute-start | bytes 245768 | tf_op jit(solution)/shard_map/ppermute | solution.py:41
  60.9 0.4 collective-permute-start.6
  61.3 1.5 collective-permute-start.7
  62.8 1.1 collective-permute-start.8
  63.9 1.7 %collective-permute-start.9 = (bf16[256,2048]{1,0:T(8,128)(2,1)}, bf16[256,2048]{1,0:T(8,128)(2,1)S(1)}, u32[]{:S(2)}, u32[]{:S(2)}) collective-permute-start(bf16[256,2048]{1,0:T(8,128)(2,1)} %collective-permute-done.3.refs_10_), channel_id=1, source_target_pairs={{0,6},{2,4},{4,2},{6,0},{1,7},{3,5},{5,3},{7,1},{8,14},{10,12},{12... | collective-permute-start | bytes 3145736 | tf_op jit(solution)/shard_map/ppermute | solution.py:50
  65.9 1.6 collective-permute-done.10
  67.5 19.8 %collective-permute-done.6.refs_9_ = bf16[256,2048]{1,0:T(8,128)(2,1)S(1)} collective-permute-done((bf16[256,2048]{1,0:T(8,128)(2,1)}, bf16[256,2048]{1,0:T(8,128)(2,1)S(1)}, u32[]{:S(2)}, u32[]{:S(2)}) %collective-permute-start.6) | collective-permute-done | bytes 1048608 | tf_op jit(solution)/shard_map/ppermute | solution.py:50
  87.3 1.5 collective-permute-start.12
  88.9 1.5 collective-permute-start.13
  90.4 17.7 %collective-permute-done.8.refs_10_ = bf16[256,2048]{1,0:T(8,128)(2,1)} collective-permute-done((bf16[256,2048]{1,0:T(8,128)(2,1)}, bf16[256,2048]{1,0:T(8,128)(2,1)}, u32[]{:S(2)}, u32[]{:S(2)}) %collective-permute-start.8) | collective-permute-done | bytes 1048608 | tf_op jit(solution)/shard_map/ppermute | solution.py:50
  108.1 1.3 collective-permute-done.9.refs_11_
  109.4 0.4 collective-permute-start.11
  109.8 0.6 copy.40.refs_1_
  110.5 4.2 %collective-permute-done.11 = bf16[2,32,1280]{2,1,0:T(8,128)(2,1)S(1)} collective-permute-done((bf16[2,32,1280]{2,1,0:T(8,128)(2,1)S(1)}, bf16[2,32,1280]{2,1,0:T(8,128)(2,1)S(1)}, u32[]{:S(2)}, u32[]{:S(2)}) %collective-permute-start.11) | collective-permute-done | bytes 163872 | tf_op jit(solution)/shard_map/ppermute | solution.py:50
  114.7 0.6 collective-permute-start.18
  115.3 1.4 collective-permute-start.14
  117.2 0.6 gather_fusion
  118.2 8.4 %collective-permute-done.14 = bf16[2,2,32,1280]{3,2,1,0:T(8,128)(2,1)S(1)} collective-permute-done((bf16[2,2,32,1280]{3,2,1,0:T(8,128)(2,1)S(1)}, bf16[2,2,32,1280]{3,2,1,0:T(8,128)(2,1)S(1)}, u32[]{:S(2)}, u32[]{:S(2)}) %collective-permute-start.14) | collective-permute-done | bytes 327712 | tf_op jit(solution)/shard_map/ppermute | solution.py:50
  126.8 0.6 copy.42
  127.4 0.2 copy.35
  127.6 0.9 rsqrt.19.refs_2_
  128.5 0.5 collective-permute-start.19
  129.1 0.5 collective-permute-start.21
  129.7 1.9 %collective-permute-done.19.refs_13_ = bf16[256,2048]{1,0:T(8,128)(2,1)} collective-permute-done((bf16[256,2048]{1,0:T(8,128)(2,1)}, bf16[256,2048]{1,0:T(8,128)(2,1)}, u32[]{:S(2)}, u32[]{:S(2)}) %collective-permute-start.19) | collective-permute-done | bytes 1048608 | tf_op jit(solution)/shard_map/ppermute | solution.py:50
  131.6 13.7 %shard_map.173 = (bf16[512,512]{1,0:T(8,128)(2,1)}, bf16[512,512]{1,0:T(8,128)(2,1)}, bf16[512,512]{1,0:T(8,128)(2,1)}) custom-call(s32[9]{0:T(128)} %stack.106.refs_0_, bf16[4,1,2048]{2,1,0:T(2,128)(2,1)} %copy.40.refs_1_, f32[1024,1]{1,0:T(8,128)} %rsqrt.19.refs_2_, s32[2,512]{1,0:T(2,128)} %bitcast.100, bf16[512,1280]{1,0:T(8,128)(2,1)} %bitcast.83, ...), custom_call_target="tpu_custom_call" | custom-call | flops 4831838208 | bytes 18874368 | tf_op jit(solution)/shard_map/pallas_call | solution.py:153
  145.4 1.7 %collective-permute-start.23 = (bf16[512,512]{1,0:T(8,128)(2,1)}, bf16[512,512]{1,0:T(8,128)(2,1)S(1)}, u32[]{:S(2)}, u32[]{:S(2)}) collective-permute-start(bf16[512,512]{1,0:T(8,128)(2,1)} %get-tuple-element.46), channel_id=1, source_target_pairs={{0,4},{4,0},{1,5},{5,1},{2,6},{6,2},{3,7},{7,3},{8,12},{12,8},{9,1... | collective-permute-start | bytes 1572872 | tf_op jit(solution)/shard_map/ppermute | solution.py:50
  147.1 0.6 stack.92.refs_0_
  147.8 12.1 %shard_map.174 = bf16[512,512]{1,0:T(8,128)(2,1)} custom-call(s32[9]{0:T(128)} %stack.92.refs_0_, bf16[4,1,2048]{2,1,0:T(2,128)(2,1)} %copy.40.refs_1_, f32[1024,1]{1,0:T(8,128)} %rsqrt.19.refs_2_, s32[2,512]{1,0:T(2,128)} %bitcast.101, bf16[512,512]{1,0:T(8,128)(2,1)} %get-tuple-element.43.refs_4_, bf16[512,512]{1,0:T(8,128)(2,1)} %get-tuple-element.44.refs_5_, ...), custom_call_target="tpu_custom_call" | custom-call | flops 4831838208 | bytes 18874368 | tf_op jit(solution)/shard_map/pallas_call | solution.py:153
  159.9 1.7 %collective-permute-done.23 = bf16[512,512]{1,0:T(8,128)(2,1)S(1)} collective-permute-done((bf16[512,512]{1,0:T(8,128)(2,1)}, bf16[512,512]{1,0:T(8,128)(2,1)S(1)}, u32[]{:S(2)}, u32[]{:S(2)}) %collective-permute-start.23) | collective-permute-done | bytes 524320 | tf_op jit(solution)/shard_map/ppermute | solution.py:50
  161.6 2.5 %maximum_select_fusion = bf16[512,1024]{1,0:T(8,128)(2,1)} fusion(bf16[512,512]{1,0:T(8,128)(2,1)S(1)} %collective-permute-done.23, bf16[512,512]{1,0:T(8,128)(2,1)} %shard_map.174, pred[]{:T(512)S(6)} %eq.10), kind=kLoop, calls=%fused_computation.3 | loop fusion | flops 4718592 | bytes 2097153 | tf_op jit(solution)/shard_map/jit(_where)/select_n | solution.py:345
  (121 shorter events, 3.2 us)
Async XLA Ops:
  6.5 125.1 %all-gather.3.cloned.1.call-start = ((), (), s32[]{:S(2)}) async-start(), calls=%async_computation | async-start | bytes 11354112 | tf_op jit(solution)/shard_map/all_gather | solution.py:269
  8.4 8.9 %copy-start.12 = (bf16[1280]{0:T(1024)(128)(2,1)S(1)}, bf16[1280]{0:T(1024)(128)(2,1)}, u32[]{:S(2)}) copy-start(bf16[1280]{0:T(1024)(128)(2,1)} %param.28) | copy-start | bytes 7684
  8.4 8.9 %copy-start.13 = (bf16[1280]{0:T(1024)(128)(2,1)S(1)}, bf16[1280]{0:T(1024)(128)(2,1)}, u32[]{:S(2)}) copy-start(bf16[1280]{0:T(1024)(128)(2,1)} %param.29) | copy-start | bytes 7684
  8.4 7.7 %collective-permute-start.1 = (bf16[168,512]{1,0:T(8,128)(2,1)S(1)}, bf16[168,512]{1,0:T(8,128)(2,1)S(1)}, u32[]{:S(2)}, u32[]{:S(2)}) collective-permute-start(bf16[168,512]{1,0:T(8,128)(2,1)S(1)} %pad_maximum_fusion.5), channel_id=1, source_target_pairs={{0,4},{4,0},{1,5},{5,1},{2,6},{6,2},{3,7},{7,3},{8,12},{12,8},{9,1... | collective-permute-start | bytes 516104 | tf_op jit(solution)/shard_map/ppermute | solution.py:50
  16.2 7.4 %copy-start.5 = (bf16[384,1280]{1,0:T(8,128)(2,1)S(1)}, bf16[384,1280]{1,0:T(8,128)(2,1)}, u32[]{:S(2)}) copy-start(bf16[384,1280]{1,0:T(8,128)(2,1)} %output_ref.1) | copy-start | bytes 2949124
  17.2 6.4 %copy-start.4 = (bf16[1280,384]{1,0:T(8,128)(2,1)S(1)}, bf16[1280,384]{1,0:T(8,128)(2,1)}, u32[]{:S(2)}) copy-start(bf16[1280,384]{1,0:T(8,128)(2,1)} %value_ref.1) | copy-start | bytes 2949124
  17.3 6.3 %copy-start = (bf16[64,1280]{1,0:T(8,128)(2,1)S(1)}, bf16[64,1280]{1,0:T(8,128)(2,1)}, u32[]{:S(2)}) copy-start(bf16[64,1280]{1,0:T(8,128)(2,1)} %latent_ref.1) | copy-start | bytes 491524
  17.3 6.3 %copy-start.1 = (bf16[2,256,1280]{2,1,0:T(8,128)(2,1)S(1)}, bf16[2,256,1280]{2,1,0:T(8,128)(2,1)}, u32[]{:S(2)}) copy-start(bf16[2,256,1280]{2,1,0:T(8,128)(2,1)} %image_ref.1) | copy-start | bytes 3932164
  17.3 6.3 %copy-start.2 = (bf16[1280,384]{1,0:T(8,128)(2,1)S(1)}, bf16[1280,384]{1,0:T(8,128)(2,1)}, u32[]{:S(2)}) copy-start(bf16[1280,384]{1,0:T(8,128)(2,1)} %query_ref.1) | copy-start | bytes 2949124
  17.3 6.3 %copy-start.3 = (bf16[1280,384]{1,0:T(8,128)(2,1)S(1)}, bf16[1280,384]{1,0:T(8,128)(2,1)}, u32[]{:S(2)}) copy-start(bf16[1280,384]{1,0:T(8,128)(2,1)} %key_ref.1) | copy-start | bytes 2949124
  17.3 6.3 %copy-start.6 = (s32[2]{0:T(128)S(1)}, s32[2]{0:T(128)}, u32[]{:S(2)}) copy-start(s32[2]{0:T(128)} %count_ref.1) | copy-start | bytes 28
  20.6 25.6 %collective-permute-start.2 = (bf16[256,2048]{1,0:T(8,128)(2,1)}, bf16[256,2048]{1,0:T(8,128)(2,1)}, u32[]{:S(2)}, u32[]{:S(2)}) collective-permute-start(bf16[256,2048]{1,0:T(8,128)(2,1)} %get-tuple-element.32), channel_id=1, source_target_pairs={{0,6},{2,4},{4,2},{6,0},{1,7},{3,5},{5,3},{7,1},{8,14},{10,12},{12... | collective-permute-start | bytes 3145736 | tf_op jit(solution)/shard_map/ppermute | solution.py:50
  23.4 5.6 %copy-start.14 = (s32[2,2]{1,0:T(2,128)S(1)}, s32[2,2]{1,0:T(2,128)}, u32[]{:S(2)}) copy-start(s32[2,2]{1,0:T(2,128)} %param.26) | copy-start | bytes 52
  23.4 24.1 %collective-permute-start.3 = (bf16[256,2048]{1,0:T(8,128)(2,1)}, bf16[256,2048]{1,0:T(8,128)(2,1)}, u32[]{:S(2)}, u32[]{:S(2)}) collective-permute-start(bf16[256,2048]{1,0:T(8,128)(2,1)} %get-tuple-element.33), channel_id=1, source_target_pairs={{0,2},{2,0},{1,3},{3,1},{4,6},{6,4},{5,7},{7,5},{8,10},{10,8},{9,1... | collective-permute-start | bytes 3145736 | tf_op jit(solution)/shard_map/ppermute | solution.py:50
  28.3 10.2 %copy-start.10 = (bf16[2048]{0:T(1024)(128)(2,1)S(1)}, bf16[2048]{0:T(1024)(128)(2,1)}, u32[]{:S(2)}) copy-start(bf16[2048]{0:T(1024)(128)(2,1)} %param.19) | copy-start | bytes 12292
  29.1 9.4 %collective-permute-start = (f32[4]{0:T(128)S(1)}, f32[4]{0:T(128)S(1)}, u32[]{:S(2)}, u32[]{:S(2)}) collective-permute-start(f32[4]{0:T(128)S(1)} %convert_element_type.39), channel_id=1, source_target_pairs={{0,8},{8,16},{16,24},{24,32},{32,40},{40,48},{48,56},{56,64},{64,7... | collective-permute-start | bytes 56 | tf_op jit(solution)/shard_map/ppermute | solution.py:41
  33.0 14.7 %copy-start.11 = (bf16[1280]{0:T(1024)(128)(2,1)S(1)}, bf16[1280]{0:T(1024)(128)(2,1)}, u32[]{:S(2)}) copy-start(bf16[1280]{0:T(1024)(128)(2,1)} %param.30) | copy-start | bytes 7684
  47.5 1.8 %collective-permute-start.4 = (f32[68,1280]{1,0:T(8,128)S(1)}, f32[68,1280]{1,0:T(8,128)S(1)}, u32[]{:S(2)}, u32[]{:S(2)}) collective-permute-start(f32[68,1280]{1,0:T(8,128)S(1)} %pad_maximum_fusion.1), channel_id=1, source_target_pairs={{0,1},{1,0},{2,3},{3,2},{4,5},{5,4},{6,7},{7,6},{8,9},{9,8},{10,11... | collective-permute-start | bytes 1044488 | tf_op jit(solution)/shard_map/ppermute | solution.py:50
  49.4 7.2 %collective-permute-start.5 = (f32[40,1280]{1,0:T(8,128)S(1)}, f32[40,1280]{1,0:T(8,128)S(1)}, u32[]{:S(2)}, u32[]{:S(2)}) collective-permute-start(f32[40,1280]{1,0:T(8,128)S(1)} %pad_maximum_fusion.4), channel_id=1, source_target_pairs={{0,2},{2,0},{1,3},{3,1},{4,6},{6,4},{5,7},{7,5},{8,10},{10,8},{9,1... | collective-permute-start | bytes 614408 | tf_op jit(solution)/shard_map/ppermute | solution.py:50
  57.1 10.4 %collective-permute-start.10 = (bf16[32,1280]{1,0:T(8,128)(2,1)S(1)}, bf16[32,1280]{1,0:T(8,128)(2,1)S(1)}, u32[]{:S(2)}, u32[]{:S(2)}) collective-permute-start(bf16[32,1280]{1,0:T(8,128)(2,1)S(1)} %multiply_convert_fusion), channel_id=1, source_target_pairs={{0,8},{8,16},{16,24},{24,32},{32,40},{40,48},{48,56},{56,64},{64,7... | collective-permute-start | bytes 245768 | tf_op jit(solution)/shard_map/ppermute | solution.py:41
  60.9 26.4 %collective-permute-start.6 = (bf16[256,2048]{1,0:T(8,128)(2,1)}, bf16[256,2048]{1,0:T(8,128)(2,1)S(1)}, u32[]{:S(2)}, u32[]{:S(2)}) collective-permute-start(bf16[256,2048]{1,0:T(8,128)(2,1)} %get-tuple-element.32), channel_id=1, source_target_pairs={{0,2},{2,0},{1,3},{3,1},{4,6},{6,4},{5,7},{7,5},{8,10},{10,8},{9,1... | collective-permute-start | bytes 3145736 | tf_op jit(solution)/shard_map/ppermute | solution.py:50
  61.3 27.6 %collective-permute-start.7 = (bf16[256,2048]{1,0:T(8,128)(2,1)}, bf16[256,2048]{1,0:T(8,128)(2,1)}, u32[]{:S(2)}, u32[]{:S(2)}) collective-permute-start(bf16[256,2048]{1,0:T(8,128)(2,1)} %get-tuple-element.33), channel_id=1, source_target_pairs={{0,6},{2,4},{4,2},{6,0},{1,7},{3,5},{5,3},{7,1},{8,14},{10,12},{12... | collective-permute-start | bytes 3145736 | tf_op jit(solution)/shard_map/ppermute | solution.py:50
  62.8 45.2 %collective-permute-start.8 = (bf16[256,2048]{1,0:T(8,128)(2,1)}, bf16[256,2048]{1,0:T(8,128)(2,1)}, u32[]{:S(2)}, u32[]{:S(2)}) collective-permute-start(bf16[256,2048]{1,0:T(8,128)(2,1)} %collective-permute-done.2.refs_6_), channel_id=1, source_target_pairs={{0,2},{2,0},{1,3},{3,1},{4,6},{6,4},{5,7},{7,5},{8,10},{10,8},{9,1... | collective-permute-start | bytes 3145736 | tf_op jit(solution)/shard_map/ppermute | solution.py:50
  63.9 45.4 %collective-permute-start.9 = (bf16[256,2048]{1,0:T(8,128)(2,1)}, bf16[256,2048]{1,0:T(8,128)(2,1)S(1)}, u32[]{:S(2)}, u32[]{:S(2)}) collective-permute-start(bf16[256,2048]{1,0:T(8,128)(2,1)} %collective-permute-done.3.refs_10_), channel_id=1, source_target_pairs={{0,6},{2,4},{4,2},{6,0},{1,7},{3,5},{5,3},{7,1},{8,14},{10,12},{12... | collective-permute-start | bytes 3145736 | tf_op jit(solution)/shard_map/ppermute | solution.py:50
  67.5 80.3 %collective-permute-start.20 = (bf16[512,2048]{1,0:T(8,128)(2,1)}, bf16[512,2048]{1,0:T(8,128)(2,1)}, u32[]{:S(2)}, u32[]{:S(2)}) collective-permute-start(bf16[512,2048]{1,0:T(8,128)(2,1)} %refs_7_.1), channel_id=1, source_target_pairs={{0,1},{1,0},{2,3},{3,2},{4,5},{5,4},{6,7},{7,6},{8,9},{9,8},{10,11... | collective-permute-start | bytes 6291464 | tf_op jit(solution)/shard_map/ppermute | solution.py:50
  87.3 27.3 %copy-start.8 = (bf16[256,2048]{1,0:T(8,128)(2,1)}, bf16[256,2048]{1,0:T(8,128)(2,1)S(1)}, u32[]{:S(2)}) copy-start(bf16[256,2048]{1,0:T(8,128)(2,1)S(1)} %collective-permute-done.6.refs_9_) | copy-start | bytes 3145732
  87.3 27.4 %collective-permute-start.12 = (f32[640]{0:T(1024)S(1)}, f32[640]{0:T(1024)S(1)}, u32[]{:S(2)}, u32[]{:S(2)}) collective-permute-start(f32[640]{0:T(1024)S(1)} %pad_maximum_fusion.11), channel_id=1, source_target_pairs={{0,6},{2,4},{4,2},{6,0},{1,7},{3,5},{5,3},{7,1},{8,14},{10,12},{12... | collective-permute-start | bytes 7688 | tf_op jit(solution)/shard_map/ppermute | solution.py:50
  88.9 26.4 %collective-permute-start.13 = (f32[640]{0:T(1024)S(1)}, f32[640]{0:T(1024)S(1)}, u32[]{:S(2)}, u32[]{:S(2)}) collective-permute-start(f32[640]{0:T(1024)S(1)} %pad_maximum_fusion.11), channel_id=1, source_target_pairs={{0,4},{4,0},{1,5},{5,1},{2,6},{6,2},{3,7},{7,3},{8,12},{12,8},{9,1... | collective-permute-start | bytes 7688 | tf_op jit(solution)/shard_map/ppermute | solution.py:50
  108.1 20.5 %collective-permute-start.16 = (bf16[256,2048]{1,0:T(8,128)(2,1)}, bf16[256,2048]{1,0:T(8,128)(2,1)}, u32[]{:S(2)}, u32[]{:S(2)}) collective-permute-start(bf16[256,2048]{1,0:T(8,128)(2,1)} %collective-permute-done.2.refs_6_), channel_id=1, source_target_pairs={{0,1},{1,0},{2,3},{3,2},{4,5},{5,4},{6,7},{7,6},{8,9},{9,8},{10,11... | collective-permute-start | bytes 3145736 | tf_op jit(solution)/shard_map/ppermute | solution.py:50
  109.4 8.4 %copy-start.9 = (bf16[256,2048]{1,0:T(8,128)(2,1)}, bf16[256,2048]{1,0:T(8,128)(2,1)S(1)}, u32[]{:S(2)}) copy-start(bf16[256,2048]{1,0:T(8,128)(2,1)S(1)} %collective-permute-done.9.refs_11_) | copy-start | bytes 3145732
  109.4 5.3 %collective-permute-start.11 = (bf16[2,32,1280]{2,1,0:T(8,128)(2,1)S(1)}, bf16[2,32,1280]{2,1,0:T(8,128)(2,1)S(1)}, u32[]{:S(2)}, u32[]{:S(2)}) collective-permute-start(bf16[2,32,1280]{2,1,0:T(8,128)(2,1)S(1)} %pad_maximum_fusion.7), channel_id=1, source_target_pairs={{0,2},{2,0},{1,3},{3,1},{4,6},{6,4},{5,7},{7,5},{8,10},{10,8},{9,1... | collective-permute-start | bytes 491528 | tf_op jit(solution)/shard_map/ppermute | solution.py:50
  114.7 14.3 %collective-permute-start.17 = (bf16[256,2048]{1,0:T(8,128)(2,1)}, bf16[256,2048]{1,0:T(8,128)(2,1)}, u32[]{:S(2)}, u32[]{:S(2)}) collective-permute-start(bf16[256,2048]{1,0:T(8,128)(2,1)} %collective-permute-done.7.refs_7_), channel_id=1, source_target_pairs={{0,1},{1,0},{2,3},{3,2},{4,5},{5,4},{6,7},{7,6},{8,9},{9,8},{10,11... | collective-permute-start | bytes 3145736 | tf_op jit(solution)/shard_map/ppermute | solution.py:50
  114.7 15.0 %collective-permute-start.18 = (bf16[256,2048]{1,0:T(8,128)(2,1)}, bf16[256,2048]{1,0:T(8,128)(2,1)}, u32[]{:S(2)}, u32[]{:S(2)}) collective-permute-start(bf16[256,2048]{1,0:T(8,128)(2,1)} %collective-permute-done.8.refs_10_), channel_id=1, source_target_pairs={{0,1},{1,0},{2,3},{3,2},{4,5},{5,4},{6,7},{7,6},{8,9},{9,8},{10,11... | collective-permute-start | bytes 3145736 | tf_op jit(solution)/shard_map/ppermute | solution.py:50
  115.3 11.2 %collective-permute-start.14 = (bf16[2,2,32,1280]{3,2,1,0:T(8,128)(2,1)S(1)}, bf16[2,2,32,1280]{3,2,1,0:T(8,128)(2,1)S(1)}, u32[]{:S(2)}, u32[]{:S(2)}) collective-permute-start(bf16[2,2,32,1280]{3,2,1,0:T(8,128)(2,1)S(1)} %pad_maximum_fusion.3), channel_id=1, source_target_pairs={{0,4},{4,0},{1,5},{5,1},{2,6},{6,2},{3,7},{7,3},{8,12},{12,8},{9,1... | collective-permute-start | bytes 983048 | tf_op jit(solution)/shard_map/ppermute | solution.py:50
  126.7 2.5 %collective-permute-start.15 = (bf16[4,2,32,1280]{3,2,1,0:T(8,128)(2,1)S(1)}, bf16[4,2,32,1280]{3,2,1,0:T(8,128)(2,1)S(1)}, u32[]{:S(2)}, u32[]{:S(2)}) collective-permute-start(bf16[4,2,32,1280]{3,2,1,0:T(8,128)(2,1)S(1)} %pad_maximum_fusion), channel_id=1, source_target_pairs={{0,1},{1,0},{2,3},{3,2},{4,5},{5,4},{6,7},{7,6},{8,9},{9,8},{10,11... | collective-permute-start | bytes 1966088 | tf_op jit(solution)/shard_map/ppermute | solution.py:37
  128.5 3.1 %collective-permute-start.19 = (bf16[256,2048]{1,0:T(8,128)(2,1)}, bf16[256,2048]{1,0:T(8,128)(2,1)}, u32[]{:S(2)}, u32[]{:S(2)}) collective-permute-start(bf16[256,2048]{1,0:T(8,128)(2,1)} %copy-done.9), channel_id=1, source_target_pairs={{0,1},{1,0},{2,3},{3,2},{4,5},{5,4},{6,7},{7,6},{8,9},{9,8},{10,11... | collective-permute-start | bytes 3145736 | tf_op jit(solution)/shard_map/ppermute | solution.py:50
  129.0 18.7 %collective-permute-start.22 = (bf16[256,2048]{1,0:T(8,128)(2,1)}, bf16[256,2048]{1,0:T(8,128)(2,1)}, u32[]{:S(2)}, u32[]{:S(2)}) collective-permute-start(bf16[256,2048]{1,0:T(8,128)(2,1)} %collective-permute-done.3.refs_10_), channel_id=1, source_target_pairs={{0,1},{1,0},{2,3},{3,2},{4,5},{5,4},{6,7},{7,6},{8,9},{9,8},{10,11... | collective-permute-start | bytes 3145736 | tf_op jit(solution)/shard_map/ppermute | solution.py:50
  129.1 18.6 %collective-permute-start.21 = (bf16[256,2048]{1,0:T(8,128)(2,1)}, bf16[256,2048]{1,0:T(8,128)(2,1)}, u32[]{:S(2)}, u32[]{:S(2)}) collective-permute-start(bf16[256,2048]{1,0:T(8,128)(2,1)} %copy-done.8), channel_id=1, source_target_pairs={{0,1},{1,0},{2,3},{3,2},{4,5},{5,4},{6,7},{7,6},{8,9},{9,8},{10,11... | collective-permute-start | bytes 3145736 | tf_op jit(solution)/shard_map/ppermute | solution.py:50
  129.7 1.9 %copy-start.7 = (bf16[8,2,32,1280]{3,2,1,0:T(8,128)(2,1)}, bf16[8,2,32,1280]{3,2,1,0:T(8,128)(2,1)S(1)}, u32[]{:S(2)}) copy-start(bf16[8,2,32,1280]{3,2,1,0:T(8,128)(2,1)S(1)} %constant_dynamic-update-slice_fusion) | copy-start | bytes 3932164
  145.4 16.2 %collective-permute-start.23 = (bf16[512,512]{1,0:T(8,128)(2,1)}, bf16[512,512]{1,0:T(8,128)(2,1)S(1)}, u32[]{:S(2)}, u32[]{:S(2)}) collective-permute-start(bf16[512,512]{1,0:T(8,128)(2,1)} %get-tuple-element.46), channel_id=1, source_target_pairs={{0,4},{4,0},{1,5},{5,1},{2,6},{6,2},{3,7},{7,3},{8,12},{12,8},{9,1... | collective-permute-start | bytes 1572872 | tf_op jit(solution)/shard_map/ppermute | solution.py:50
Sparse Core Ops, SparseCore 0:
  17.3 112.5 all-gather.2

commit v5 on v4

--- a/solution.py
+++ b/solution.py
@@ -136,10 +136,10 @@
         scores = scores * (HD ** (-0.5) * LOG2E) + hidden
         highest = jnp.max(scores, axis=-1, keepdims=True)
         weights = jnp.exp2(scores - highest)
-        summed = jnp.sum(weights, axis=-1, keepdims=True)
-        probs = (weights * jnp.where(anything, 1.0 / summed, 0.0)).astype(jnp.bfloat16)
-        out_ref[:, cols] = jnp.dot(
-            probs, value_ref[:, cols], preferred_element_type=jnp.float32
+        both = jnp.concatenate([value_ref[:, cols], jnp.ones((KEYS, HD), jnp.bfloat16)], axis=1)
+        mixed = jnp.dot(weights.astype(jnp.bfloat16), both, preferred_element_type=jnp.float32)
+        out_ref[:, cols] = (
+            mixed[:, :HD] * jnp.where(anything, 1.0 / mixed[:, HD:], 0.0)
         ).astype(jnp.bfloat16)
 
 

time: 172 us -> 172 us (level)
  transfers between devices with their start and end apart: 25 -> 25, of which waited for: 15 -> 15; matrix products, arithmetic and copies ran while one was open for 7% -> 7% of each run, Pallas kernels for 18% -> 17%
where the time goes in v5:
time: 172 us; the launch traced here: 171 us
  waiting for transfers between devices  81.5 us (47%)
  Pallas kernels  29.7 us (17%)
  starting transfers between devices  27.3 us (16%)
  between operations  14.6 us (8%)
  local copies, waits for them, and re-layouts  10.5 us (6%)
  other arithmetic  6.71 us (4%)
    ppermute x21, waiting for transfers between devices, flipped(): return lax.ppermute(x, axes, [(i, count - 1 - i) for i in range(count)])  76.5 us
    pallas_call x2, Pallas kernels, attend(): pl.pallas_call(functools.partial(attend_kernel, counts, fresh), out_shape...  25.1 us
    ppermute x21, starting transfers between devices, flipped(): return lax.ppermute(x, axes, [(i, count - 1 - i) for i in range(count)])  19.5 us
    ppermute x2, starting transfers between devices, next_pair(): return lax.ppermute(x, ('y', 'z'), [(i, i + 1) for i in range(NY * NZ - 1)])  7.65 us
    ppermute x2, waiting for transfers between devices, next_pair(): return lax.ppermute(x, ('y', 'z'), [(i, i + 1) for i in range(NY * NZ - 1)])  4.95 us
    pallas_call x1, Pallas kernels, resample(): pl.pallas_call(resample_kernel, out_shape=jax.ShapeDtypeStruct((images.sh...  4.68 us
  transfers between devices with their start and end apart: 25, of which 15 were waited for; matrix products, arithmetic and copies ran while one was open for 7% of the time, Pallas kernels for 17%

profile of v5, /device:TPU:24, one launch (start us, length us, event | category | flops | bytes accessed | tf_op | source)
XLA Modules:
  0.0 170.5 jit_solution(8357587901383248929)
XLA Ops:
  6.5 1.0 constant_dynamic-slice_fusion.2
  7.5 0.8 constant_dynamic-slice_fusion
  8.4 3.1 %collective-permute-start.1 = (bf16[168,512]{1,0:T(8,128)(2,1)S(1)}, bf16[168,512]{1,0:T(8,128)(2,1)S(1)}, u32[]{:S(2)}, u32[]{:S(2)}) collective-permute-start(bf16[168,512]{1,0:T(8,128)(2,1)S(1)} %pad_maximum_fusion.5), channel_id=1, source_target_pairs={{0,4},{4,0},{1,5},{5,1},{2,6},{6,2},{3,7},{7,3},{8,12},{12,8},{9,1... | collective-permute-start | bytes 516104 | tf_op jit(solution)/shard_map/ppermute | solution.py:50
  11.5 4.6 %collective-permute-done.1 = bf16[168,512]{1,0:T(8,128)(2,1)S(1)} collective-permute-done((bf16[168,512]{1,0:T(8,128)(2,1)S(1)}, bf16[168,512]{1,0:T(8,128)(2,1)S(1)}, u32[]{:S(2)}, u32[]{:S(2)}) %collective-permute-start.1) | collective-permute-done | bytes 172064 | tf_op jit(solution)/shard_map/ppermute | solution.py:50
  16.4 0.8 pad_maximum_fusion.2
  17.3 3.3 %fusion.15 = (bf16[256,2048]{1,0:T(8,128)(2,1)}, bf16[256,2048]{1,0:T(8,128)(2,1)}) fusion(bf16[512,2048]{1,0:T(8,128)(2,1)} %refs_7_.1), kind=kLoop, calls=%fused_computation.85 | loop fusion | bytes 4194304 | tf_op jit(solution)/shard_map/slice | solution.py:290
  20.6 2.8 %collective-permute-start.2 = (bf16[256,2048]{1,0:T(8,128)(2,1)}, bf16[256,2048]{1,0:T(8,128)(2,1)}, u32[]{:S(2)}, u32[]{:S(2)}) collective-permute-start(bf16[256,2048]{1,0:T(8,128)(2,1)} %get-tuple-element.32), channel_id=1, source_target_pairs={{0,6},{2,4},{4,2},{6,0},{1,7},{3,5},{5,3},{7,1},{8,14},{10,12},{12... | collective-permute-start | bytes 3145736 | tf_op jit(solution)/shard_map/ppermute | solution.py:50
  23.4 0.2 collective-permute-start.3
  23.6 4.7 %shard_map.172 = f32[2,64,1280]{2,1,0:T(8,128)S(1)} custom-call(s32[2]{0:T(128)S(1)} %copy-done.6, bf16[2,256,1280]{2,1,0:T(8,128)(2,1)S(1)} %copy-done.1, bf16[64,1280]{1,0:T(8,128)(2,1)S(1)} %copy-done, bf16[1,1280]{1,0:T(2,128)(2,1)S(1)} %broadcast_in_dim.39.latent_gain_ref, bf16[1,1280]{1,0:T(2,128)(2,1)S(1)} %broadcast_in_dim.40.context_gain_ref, ...), custom_call_target="tpu_custom_call" | custom-call | flops 32212254720 | bytes 8388608 | tf_op jit(solution)/shard_map/pallas_call | solution.py:220
  29.1 3.8 %collective-permute-start = (f32[4]{0:T(128)S(1)}, f32[4]{0:T(128)S(1)}, u32[]{:S(2)}, u32[]{:S(2)}) collective-permute-start(f32[4]{0:T(128)S(1)} %convert_element_type.39), channel_id=1, source_target_pairs={{0,8},{8,16},{16,24},{24,32},{32,40},{40,48},{48,56},{56,64},{64,7... | collective-permute-start | bytes 56 | tf_op jit(solution)/shard_map/ppermute | solution.py:41
  33.0 2.2 %multiply_reduce_fusion = f32[512]{0:T(512)S(1)} fusion(bf16[512,2048]{1,0:T(8,128)(2,1)} %refs_7_.1), kind=kLoop, calls=%fused_computation.1 | loop fusion | flops 3145216 | bytes 2099200 | tf_op jit(solution)/shard_map/reduce_sum | solution.py:273
  35.2 3.4 %collective-permute-done = f32[4]{0:T(128)S(1)} collective-permute-done((f32[4]{0:T(128)S(1)}, f32[4]{0:T(128)S(1)}, u32[]{:S(2)}, u32[]{:S(2)}) %collective-permute-start) | collective-permute-done | bytes 48 | tf_op jit(solution)/shard_map/ppermute | solution.py:41
  38.6 7.5 %collective-permute-done.2.refs_6_ = bf16[256,2048]{1,0:T(8,128)(2,1)} collective-permute-done((bf16[256,2048]{1,0:T(8,128)(2,1)}, bf16[256,2048]{1,0:T(8,128)(2,1)}, u32[]{:S(2)}, u32[]{:S(2)}) %collective-permute-start.2) | collective-permute-done | bytes 1048608 | tf_op jit(solution)/shard_map/ppermute | solution.py:50
  46.2 1.3 collective-permute-done.3.refs_10_
  47.7 0.6 stack.106.refs_0_
  48.3 1.0 collective-permute-done.4
  49.4 0.4 collective-permute-start.5
  50.0 6.7 %collective-permute-done.5 = f32[40,1280]{1,0:T(8,128)S(1)} collective-permute-done((f32[40,1280]{1,0:T(8,128)S(1)}, f32[40,1280]{1,0:T(8,128)S(1)}, u32[]{:S(2)}, u32[]{:S(2)}) %collective-permute-start.5) | collective-permute-done | bytes 204832 | tf_op jit(solution)/shard_map/ppermute | solution.py:50
  57.1 3.8 %collective-permute-start.10 = (bf16[32,1280]{1,0:T(8,128)(2,1)S(1)}, bf16[32,1280]{1,0:T(8,128)(2,1)S(1)}, u32[]{:S(2)}, u32[]{:S(2)}) collective-permute-start(bf16[32,1280]{1,0:T(8,128)(2,1)S(1)} %multiply_convert_fusion), channel_id=1, source_target_pairs={{0,8},{8,16},{16,24},{24,32},{32,40},{40,48},{48,56},{56,64},{64,7... | collective-permute-start | bytes 245768 | tf_op jit(solution)/shard_map/ppermute | solution.py:41
  60.9 0.4 collective-permute-start.6
  61.3 1.5 collective-permute-start.7
  62.8 1.1 collective-permute-start.8
  63.9 1.7 %collective-permute-start.9 = (bf16[256,2048]{1,0:T(8,128)(2,1)}, bf16[256,2048]{1,0:T(8,128)(2,1)S(1)}, u32[]{:S(2)}, u32[]{:S(2)}) collective-permute-start(bf16[256,2048]{1,0:T(8,128)(2,1)} %collective-permute-done.3.refs_10_), channel_id=1, source_target_pairs={{0,6},{2,4},{4,2},{6,0},{1,7},{3,5},{5,3},{7,1},{8,14},{10,12},{12... | collective-permute-start | bytes 3145736 | tf_op jit(solution)/shard_map/ppermute | solution.py:50
  65.9 1.6 collective-permute-done.10
  67.5 19.8 %collective-permute-done.6.refs_9_ = bf16[256,2048]{1,0:T(8,128)(2,1)S(1)} collective-permute-done((bf16[256,2048]{1,0:T(8,128)(2,1)}, bf16[256,2048]{1,0:T(8,128)(2,1)S(1)}, u32[]{:S(2)}, u32[]{:S(2)}) %collective-permute-start.6) | collective-permute-done | bytes 1048608 | tf_op jit(solution)/shard_map/ppermute | solution.py:50
  87.3 1.5 collective-permute-start.12
  88.9 1.5 collective-permute-start.13
  90.4 17.7 %collective-permute-done.8.refs_10_ = bf16[256,2048]{1,0:T(8,128)(2,1)} collective-permute-done((bf16[256,2048]{1,0:T(8,128)(2,1)}, bf16[256,2048]{1,0:T(8,128)(2,1)}, u32[]{:S(2)}, u32[]{:S(2)}) %collective-permute-start.8) | collective-permute-done | bytes 1048608 | tf_op jit(solution)/shard_map/ppermute | solution.py:50
  108.1 1.3 collective-permute-done.9.refs_11_
  109.4 0.4 collective-permute-start.11
  109.8 0.6 copy.40.refs_1_
  110.5 4.2 %collective-permute-done.11 = bf16[2,32,1280]{2,1,0:T(8,128)(2,1)S(1)} collective-permute-done((bf16[2,32,1280]{2,1,0:T(8,128)(2,1)S(1)}, bf16[2,32,1280]{2,1,0:T(8,128)(2,1)S(1)}, u32[]{:S(2)}, u32[]{:S(2)}) %collective-permute-start.11) | collective-permute-done | bytes 163872 | tf_op jit(solution)/shard_map/ppermute | solution.py:50
  114.7 0.6 collective-permute-start.18
  115.3 1.4 collective-permute-start.14
  117.2 0.6 gather_fusion
  118.2 8.4 %collective-permute-done.14 = bf16[2,2,32,1280]{3,2,1,0:T(8,128)(2,1)S(1)} collective-permute-done((bf16[2,2,32,1280]{3,2,1,0:T(8,128)(2,1)S(1)}, bf16[2,2,32,1280]{3,2,1,0:T(8,128)(2,1)S(1)}, u32[]{:S(2)}, u32[]{:S(2)}) %collective-permute-start.14) | collective-permute-done | bytes 327712 | tf_op jit(solution)/shard_map/ppermute | solution.py:50
  126.8 0.6 copy.42
  127.4 0.2 copy.35
  127.6 0.9 rsqrt.19.refs_2_
  128.5 0.5 collective-permute-start.19
  129.1 0.5 collective-permute-start.21
  129.7 1.9 %collective-permute-done.19.refs_13_ = bf16[256,2048]{1,0:T(8,128)(2,1)} collective-permute-done((bf16[256,2048]{1,0:T(8,128)(2,1)}, bf16[256,2048]{1,0:T(8,128)(2,1)}, u32[]{:S(2)}, u32[]{:S(2)}) %collective-permute-start.19) | collective-permute-done | bytes 1048608 | tf_op jit(solution)/shard_map/ppermute | solution.py:50
  131.6 13.3 %shard_map.173 = (bf16[512,512]{1,0:T(8,128)(2,1)}, bf16[512,512]{1,0:T(8,128)(2,1)}, bf16[512,512]{1,0:T(8,128)(2,1)}) custom-call(s32[9]{0:T(128)} %stack.106.refs_0_, bf16[4,1,2048]{2,1,0:T(2,128)(2,1)} %copy.40.refs_1_, f32[1024,1]{1,0:T(8,128)} %rsqrt.19.refs_2_, s32[2,512]{1,0:T(2,128)} %bitcast.100, bf16[512,1280]{1,0:T(8,128)(2,1)} %bitcast.83, ...), custom_call_target="tpu_custom_call" | custom-call | flops 4831838208 | bytes 18874368 | tf_op jit(solution)/shard_map/pallas_call | solution.py:153
  145.0 1.7 %collective-permute-start.23 = (bf16[512,512]{1,0:T(8,128)(2,1)}, bf16[512,512]{1,0:T(8,128)(2,1)S(1)}, u32[]{:S(2)}, u32[]{:S(2)}) collective-permute-start(bf16[512,512]{1,0:T(8,128)(2,1)} %get-tuple-element.46), channel_id=1, source_target_pairs={{0,4},{4,0},{1,5},{5,1},{2,6},{6,2},{3,7},{7,3},{8,12},{12,8},{9,1... | collective-permute-start | bytes 1572872 | tf_op jit(solution)/shard_map/ppermute | solution.py:50
  146.7 0.6 stack.92.refs_0_
  147.4 11.7 %shard_map.174 = bf16[512,512]{1,0:T(8,128)(2,1)} custom-call(s32[9]{0:T(128)} %stack.92.refs_0_, bf16[4,1,2048]{2,1,0:T(2,128)(2,1)} %copy.40.refs_1_, f32[1024,1]{1,0:T(8,128)} %rsqrt.19.refs_2_, s32[2,512]{1,0:T(2,128)} %bitcast.101, bf16[512,512]{1,0:T(8,128)(2,1)} %get-tuple-element.43.refs_4_, bf16[512,512]{1,0:T(8,128)(2,1)} %get-tuple-element.44.refs_5_, ...), custom_call_target="tpu_custom_call" | custom-call | flops 4831838208 | bytes 18874368 | tf_op jit(solution)/shard_map/pallas_call | solution.py:153
  159.1 2.1 %collective-permute-done.23 = bf16[512,512]{1,0:T(8,128)(2,1)S(1)} collective-permute-done((bf16[512,512]{1,0:T(8,128)(2,1)}, bf16[512,512]{1,0:T(8,128)(2,1)S(1)}, u32[]{:S(2)}, u32[]{:S(2)}) %collective-permute-start.23) | collective-permute-done | bytes 524320 | tf_op jit(solution)/shard_map/ppermute | solution.py:50
  161.2 2.5 %maximum_select_fusion = bf16[512,1024]{1,0:T(8,128)(2,1)} fusion(bf16[512,512]{1,0:T(8,128)(2,1)S(1)} %collective-permute-done.23, bf16[512,512]{1,0:T(8,128)(2,1)} %shard_map.174, pred[]{:T(512)S(6)} %eq.10), kind=kLoop, calls=%fused_computation.3 | loop fusion | flops 4718592 | bytes 2097153 | tf_op jit(solution)/shard_map/jit(_where)/select_n | solution.py:345
  (121 shorter events, 3.2 us)
Async XLA Ops:
  6.5 125.1 %all-gather.3.cloned.1.call-start = ((), (), s32[]{:S(2)}) async-start(), calls=%async_computation | async-start | bytes 11354112 | tf_op jit(solution)/shard_map/all_gather | solution.py:269
  8.4 8.9 %copy-start.12 = (bf16[1280]{0:T(1024)(128)(2,1)S(1)}, bf16[1280]{0:T(1024)(128)(2,1)}, u32[]{:S(2)}) copy-start(bf16[1280]{0:T(1024)(128)(2,1)} %param.28) | copy-start | bytes 7684
  8.4 8.9 %copy-start.13 = (bf16[1280]{0:T(1024)(128)(2,1)S(1)}, bf16[1280]{0:T(1024)(128)(2,1)}, u32[]{:S(2)}) copy-start(bf16[1280]{0:T(1024)(128)(2,1)} %param.29) | copy-start | bytes 7684
  8.4 7.7 %collective-permute-start.1 = (bf16[168,512]{1,0:T(8,128)(2,1)S(1)}, bf16[168,512]{1,0:T(8,128)(2,1)S(1)}, u32[]{:S(2)}, u32[]{:S(2)}) collective-permute-start(bf16[168,512]{1,0:T(8,128)(2,1)S(1)} %pad_maximum_fusion.5), channel_id=1, source_target_pairs={{0,4},{4,0},{1,5},{5,1},{2,6},{6,2},{3,7},{7,3},{8,12},{12,8},{9,1... | collective-permute-start | bytes 516104 | tf_op jit(solution)/shard_map/ppermute | solution.py:50
  16.2 7.4 %copy-start.5 = (bf16[384,1280]{1,0:T(8,128)(2,1)S(1)}, bf16[384,1280]{1,0:T(8,128)(2,1)}, u32[]{:S(2)}) copy-start(bf16[384,1280]{1,0:T(8,128)(2,1)} %output_ref.1) | copy-start | bytes 2949124
  17.2 6.4 %copy-start.4 = (bf16[1280,384]{1,0:T(8,128)(2,1)S(1)}, bf16[1280,384]{1,0:T(8,128)(2,1)}, u32[]{:S(2)}) copy-start(bf16[1280,384]{1,0:T(8,128)(2,1)} %value_ref.1) | copy-start | bytes 2949124
  17.3 6.3 %copy-start = (bf16[64,1280]{1,0:T(8,128)(2,1)S(1)}, bf16[64,1280]{1,0:T(8,128)(2,1)}, u32[]{:S(2)}) copy-start(bf16[64,1280]{1,0:T(8,128)(2,1)} %latent_ref.1) | copy-start | bytes 491524
  17.3 6.3 %copy-start.1 = (bf16[2,256,1280]{2,1,0:T(8,128)(2,1)S(1)}, bf16[2,256,1280]{2,1,0:T(8,128)(2,1)}, u32[]{:S(2)}) copy-start(bf16[2,256,1280]{2,1,0:T(8,128)(2,1)} %image_ref.1) | copy-start | bytes 3932164
  17.3 6.3 %copy-start.2 = (bf16[1280,384]{1,0:T(8,128)(2,1)S(1)}, bf16[1280,384]{1,0:T(8,128)(2,1)}, u32[]{:S(2)}) copy-start(bf16[1280,384]{1,0:T(8,128)(2,1)} %query_ref.1) | copy-start | bytes 2949124
  17.3 6.3 %copy-start.3 = (bf16[1280,384]{1,0:T(8,128)(2,1)S(1)}, bf16[1280,384]{1,0:T(8,128)(2,1)}, u32[]{:S(2)}) copy-start(bf16[1280,384]{1,0:T(8,128)(2,1)} %key_ref.1) | copy-start | bytes 2949124
  17.3 6.3 %copy-start.6 = (s32[2]{0:T(128)S(1)}, s32[2]{0:T(128)}, u32[]{:S(2)}) copy-start(s32[2]{0:T(128)} %count_ref.1) | copy-start | bytes 28
  20.6 25.6 %collective-permute-start.2 = (bf16[256,2048]{1,0:T(8,128)(2,1)}, bf16[256,2048]{1,0:T(8,128)(2,1)}, u32[]{:S(2)}, u32[]{:S(2)}) collective-permute-start(bf16[256,2048]{1,0:T(8,128)(2,1)} %get-tuple-element.32), channel_id=1, source_target_pairs={{0,6},{2,4},{4,2},{6,0},{1,7},{3,5},{5,3},{7,1},{8,14},{10,12},{12... | collective-permute-start | bytes 3145736 | tf_op jit(solution)/shard_map/ppermute | solution.py:50
  23.4 5.6 %copy-start.14 = (s32[2,2]{1,0:T(2,128)S(1)}, s32[2,2]{1,0:T(2,128)}, u32[]{:S(2)}) copy-start(s32[2,2]{1,0:T(2,128)} %param.26) | copy-start | bytes 52
  23.4 24.1 %collective-permute-start.3 = (bf16[256,2048]{1,0:T(8,128)(2,1)}, bf16[256,2048]{1,0:T(8,128)(2,1)}, u32[]{:S(2)}, u32[]{:S(2)}) collective-permute-start(bf16[256,2048]{1,0:T(8,128)(2,1)} %get-tuple-element.33), channel_id=1, source_target_pairs={{0,2},{2,0},{1,3},{3,1},{4,6},{6,4},{5,7},{7,5},{8,10},{10,8},{9,1... | collective-permute-start | bytes 3145736 | tf_op jit(solution)/shard_map/ppermute | solution.py:50
  28.3 10.2 %copy-start.10 = (bf16[2048]{0:T(1024)(128)(2,1)S(1)}, bf16[2048]{0:T(1024)(128)(2,1)}, u32[]{:S(2)}) copy-start(bf16[2048]{0:T(1024)(128)(2,1)} %param.19) | copy-start | bytes 12292
  29.1 9.4 %collective-permute-start = (f32[4]{0:T(128)S(1)}, f32[4]{0:T(128)S(1)}, u32[]{:S(2)}, u32[]{:S(2)}) collective-permute-start(f32[4]{0:T(128)S(1)} %convert_element_type.39), channel_id=1, source_target_pairs={{0,8},{8,16},{16,24},{24,32},{32,40},{40,48},{48,56},{56,64},{64,7... | collective-permute-start | bytes 56 | tf_op jit(solution)/shard_map/ppermute | solution.py:41
  33.0 14.7 %copy-start.11 = (bf16[1280]{0:T(1024)(128)(2,1)S(1)}, bf16[1280]{0:T(1024)(128)(2,1)}, u32[]{:S(2)}) copy-start(bf16[1280]{0:T(1024)(128)(2,1)} %param.30) | copy-start | bytes 7684
  47.5 1.8 %collective-permute-start.4 = (f32[68,1280]{1,0:T(8,128)S(1)}, f32[68,1280]{1,0:T(8,128)S(1)}, u32[]{:S(2)}, u32[]{:S(2)}) collective-permute-start(f32[68,1280]{1,0:T(8,128)S(1)} %pad_maximum_fusion.1), channel_id=1, source_target_pairs={{0,1},{1,0},{2,3},{3,2},{4,5},{5,4},{6,7},{7,6},{8,9},{9,8},{10,11... | collective-permute-start | bytes 1044488 | tf_op jit(solution)/shard_map/ppermute | solution.py:50
  49.4 7.2 %collective-permute-start.5 = (f32[40,1280]{1,0:T(8,128)S(1)}, f32[40,1280]{1,0:T(8,128)S(1)}, u32[]{:S(2)}, u32[]{:S(2)}) collective-permute-start(f32[40,1280]{1,0:T(8,128)S(1)} %pad_maximum_fusion.4), channel_id=1, source_target_pairs={{0,2},{2,0},{1,3},{3,1},{4,6},{6,4},{5,7},{7,5},{8,10},{10,8},{9,1... | collective-permute-start | bytes 614408 | tf_op jit(solution)/shard_map/ppermute | solution.py:50
  57.1 10.4 %collective-permute-start.10 = (bf16[32,1280]{1,0:T(8,128)(2,1)S(1)}, bf16[32,1280]{1,0:T(8,128)(2,1)S(1)}, u32[]{:S(2)}, u32[]{:S(2)}) collective-permute-start(bf16[32,1280]{1,0:T(8,128)(2,1)S(1)} %multiply_convert_fusion), channel_id=1, source_target_pairs={{0,8},{8,16},{16,24},{24,32},{32,40},{40,48},{48,56},{56,64},{64,7... | collective-permute-start | bytes 245768 | tf_op jit(solution)/shard_map/ppermute | solution.py:41
  60.9 26.4 %collective-permute-start.6 = (bf16[256,2048]{1,0:T(8,128)(2,1)}, bf16[256,2048]{1,0:T(8,128)(2,1)S(1)}, u32[]{:S(2)}, u32[]{:S(2)}) collective-permute-start(bf16[256,2048]{1,0:T(8,128)(2,1)} %get-tuple-element.32), channel_id=1, source_target_pairs={{0,2},{2,0},{1,3},{3,1},{4,6},{6,4},{5,7},{7,5},{8,10},{10,8},{9,1... | collective-permute-start | bytes 3145736 | tf_op jit(solution)/shard_map/ppermute | solution.py:50
  61.3 27.6 %collective-permute-start.7 = (bf16[256,2048]{1,0:T(8,128)(2,1)}, bf16[256,2048]{1,0:T(8,128)(2,1)}, u32[]{:S(2)}, u32[]{:S(2)}) collective-permute-start(bf16[256,2048]{1,0:T(8,128)(2,1)} %get-tuple-element.33), channel_id=1, source_target_pairs={{0,6},{2,4},{4,2},{6,0},{1,7},{3,5},{5,3},{7,1},{8,14},{10,12},{12... | collective-permute-start | bytes 3145736 | tf_op jit(solution)/shard_map/ppermute | solution.py:50
  62.8 45.2 %collective-permute-start.8 = (bf16[256,2048]{1,0:T(8,128)(2,1)}, bf16[256,2048]{1,0:T(8,128)(2,1)}, u32[]{:S(2)}, u32[]{:S(2)}) collective-permute-start(bf16[256,2048]{1,0:T(8,128)(2,1)} %collective-permute-done.2.refs_6_), channel_id=1, source_target_pairs={{0,2},{2,0},{1,3},{3,1},{4,6},{6,4},{5,7},{7,5},{8,10},{10,8},{9,1... | collective-permute-start | bytes 3145736 | tf_op jit(solution)/shard_map/ppermute | solution.py:50
  63.9 45.4 %collective-permute-start.9 = (bf16[256,2048]{1,0:T(8,128)(2,1)}, bf16[256,2048]{1,0:T(8,128)(2,1)S(1)}, u32[]{:S(2)}, u32[]{:S(2)}) collective-permute-start(bf16[256,2048]{1,0:T(8,128)(2,1)} %collective-permute-done.3.refs_10_), channel_id=1, source_target_pairs={{0,6},{2,4},{4,2},{6,0},{1,7},{3,5},{5,3},{7,1},{8,14},{10,12},{12... | collective-permute-start | bytes 3145736 | tf_op jit(solution)/shard_map/ppermute | solution.py:50
  67.5 79.9 %collective-permute-start.20 = (bf16[512,2048]{1,0:T(8,128)(2,1)}, bf16[512,2048]{1,0:T(8,128)(2,1)}, u32[]{:S(2)}, u32[]{:S(2)}) collective-permute-start(bf16[512,2048]{1,0:T(8,128)(2,1)} %refs_7_.1), channel_id=1, source_target_pairs={{0,1},{1,0},{2,3},{3,2},{4,5},{5,4},{6,7},{7,6},{8,9},{9,8},{10,11... | collective-permute-start | bytes 6291464 | tf_op jit(solution)/shard_map/ppermute | solution.py:50
  87.3 27.3 %copy-start.8 = (bf16[256,2048]{1,0:T(8,128)(2,1)}, bf16[256,2048]{1,0:T(8,128)(2,1)S(1)}, u32[]{:S(2)}) copy-start(bf16[256,2048]{1,0:T(8,128)(2,1)S(1)} %collective-permute-done.6.refs_9_) | copy-start | bytes 3145732
  87.3 27.4 %collective-permute-start.12 = (f32[640]{0:T(1024)S(1)}, f32[640]{0:T(1024)S(1)}, u32[]{:S(2)}, u32[]{:S(2)}) collective-permute-start(f32[640]{0:T(1024)S(1)} %pad_maximum_fusion.11), channel_id=1, source_target_pairs={{0,6},{2,4},{4,2},{6,0},{1,7},{3,5},{5,3},{7,1},{8,14},{10,12},{12... | collective-permute-start | bytes 7688 | tf_op jit(solution)/shard_map/ppermute | solution.py:50
  88.9 26.4 %collective-permute-start.13 = (f32[640]{0:T(1024)S(1)}, f32[640]{0:T(1024)S(1)}, u32[]{:S(2)}, u32[]{:S(2)}) collective-permute-start(f32[640]{0:T(1024)S(1)} %pad_maximum_fusion.11), channel_id=1, source_target_pairs={{0,4},{4,0},{1,5},{5,1},{2,6},{6,2},{3,7},{7,3},{8,12},{12,8},{9,1... | collective-permute-start | bytes 7688 | tf_op jit(solution)/shard_map/ppermute | solution.py:50
  108.1 20.5 %collective-permute-start.16 = (bf16[256,2048]{1,0:T(8,128)(2,1)}, bf16[256,2048]{1,0:T(8,128)(2,1)}, u32[]{:S(2)}, u32[]{:S(2)}) collective-permute-start(bf16[256,2048]{1,0:T(8,128)(2,1)} %collective-permute-done.2.refs_6_), channel_id=1, source_target_pairs={{0,1},{1,0},{2,3},{3,2},{4,5},{5,4},{6,7},{7,6},{8,9},{9,8},{10,11... | collective-permute-start | bytes 3145736 | tf_op jit(solution)/shard_map/ppermute | solution.py:50
  109.4 8.4 %copy-start.9 = (bf16[256,2048]{1,0:T(8,128)(2,1)}, bf16[256,2048]{1,0:T(8,128)(2,1)S(1)}, u32[]{:S(2)}) copy-start(bf16[256,2048]{1,0:T(8,128)(2,1)S(1)} %collective-permute-done.9.refs_11_) | copy-start | bytes 3145732
  109.4 5.3 %collective-permute-start.11 = (bf16[2,32,1280]{2,1,0:T(8,128)(2,1)S(1)}, bf16[2,32,1280]{2,1,0:T(8,128)(2,1)S(1)}, u32[]{:S(2)}, u32[]{:S(2)}) collective-permute-start(bf16[2,32,1280]{2,1,0:T(8,128)(2,1)S(1)} %pad_maximum_fusion.7), channel_id=1, source_target_pairs={{0,2},{2,0},{1,3},{3,1},{4,6},{6,4},{5,7},{7,5},{8,10},{10,8},{9,1... | collective-permute-start | bytes 491528 | tf_op jit(solution)/shard_map/ppermute | solution.py:50
  114.7 14.3 %collective-permute-start.17 = (bf16[256,2048]{1,0:T(8,128)(2,1)}, bf16[256,2048]{1,0:T(8,128)(2,1)}, u32[]{:S(2)}, u32[]{:S(2)}) collective-permute-start(bf16[256,2048]{1,0:T(8,128)(2,1)} %collective-permute-done.7.refs_7_), channel_id=1, source_target_pairs={{0,1},{1,0},{2,3},{3,2},{4,5},{5,4},{6,7},{7,6},{8,9},{9,8},{10,11... | collective-permute-start | bytes 3145736 | tf_op jit(solution)/shard_map/ppermute | solution.py:50
  114.7 15.0 %collective-permute-start.18 = (bf16[256,2048]{1,0:T(8,128)(2,1)}, bf16[256,2048]{1,0:T(8,128)(2,1)}, u32[]{:S(2)}, u32[]{:S(2)}) collective-permute-start(bf16[256,2048]{1,0:T(8,128)(2,1)} %collective-permute-done.8.refs_10_), channel_id=1, source_target_pairs={{0,1},{1,0},{2,3},{3,2},{4,5},{5,4},{6,7},{7,6},{8,9},{9,8},{10,11... | collective-permute-start | bytes 3145736 | tf_op jit(solution)/shard_map/ppermute | solution.py:50
  115.3 11.2 %collective-permute-start.14 = (bf16[2,2,32,1280]{3,2,1,0:T(8,128)(2,1)S(1)}, bf16[2,2,32,1280]{3,2,1,0:T(8,128)(2,1)S(1)}, u32[]{:S(2)}, u32[]{:S(2)}) collective-permute-start(bf16[2,2,32,1280]{3,2,1,0:T(8,128)(2,1)S(1)} %pad_maximum_fusion.3), channel_id=1, source_target_pairs={{0,4},{4,0},{1,5},{5,1},{2,6},{6,2},{3,7},{7,3},{8,12},{12,8},{9,1... | collective-permute-start | bytes 983048 | tf_op jit(solution)/shard_map/ppermute | solution.py:50
  126.7 2.5 %collective-permute-start.15 = (bf16[4,2,32,1280]{3,2,1,0:T(8,128)(2,1)S(1)}, bf16[4,2,32,1280]{3,2,1,0:T(8,128)(2,1)S(1)}, u32[]{:S(2)}, u32[]{:S(2)}) collective-permute-start(bf16[4,2,32,1280]{3,2,1,0:T(8,128)(2,1)S(1)} %pad_maximum_fusion), channel_id=1, source_target_pairs={{0,1},{1,0},{2,3},{3,2},{4,5},{5,4},{6,7},{7,6},{8,9},{9,8},{10,11... | collective-permute-start | bytes 1966088 | tf_op jit(solution)/shard_map/ppermute | solution.py:37
  128.5 3.1 %collective-permute-start.19 = (bf16[256,2048]{1,0:T(8,128)(2,1)}, bf16[256,2048]{1,0:T(8,128)(2,1)}, u32[]{:S(2)}, u32[]{:S(2)}) collective-permute-start(bf16[256,2048]{1,0:T(8,128)(2,1)} %copy-done.9), channel_id=1, source_target_pairs={{0,1},{1,0},{2,3},{3,2},{4,5},{5,4},{6,7},{7,6},{8,9},{9,8},{10,11... | collective-permute-start | bytes 3145736 | tf_op jit(solution)/shard_map/ppermute | solution.py:50
  129.0 18.3 %collective-permute-start.22 = (bf16[256,2048]{1,0:T(8,128)(2,1)}, bf16[256,2048]{1,0:T(8,128)(2,1)}, u32[]{:S(2)}, u32[]{:S(2)}) collective-permute-start(bf16[256,2048]{1,0:T(8,128)(2,1)} %collective-permute-done.3.refs_10_), channel_id=1, source_target_pairs={{0,1},{1,0},{2,3},{3,2},{4,5},{5,4},{6,7},{7,6},{8,9},{9,8},{10,11... | collective-permute-start | bytes 3145736 | tf_op jit(solution)/shard_map/ppermute | solution.py:50
  129.1 18.2 %collective-permute-start.21 = (bf16[256,2048]{1,0:T(8,128)(2,1)}, bf16[256,2048]{1,0:T(8,128)(2,1)}, u32[]{:S(2)}, u32[]{:S(2)}) collective-permute-start(bf16[256,2048]{1,0:T(8,128)(2,1)} %copy-done.8), channel_id=1, source_target_pairs={{0,1},{1,0},{2,3},{3,2},{4,5},{5,4},{6,7},{7,6},{8,9},{9,8},{10,11... | collective-permute-start | bytes 3145736 | tf_op jit(solution)/shard_map/ppermute | solution.py:50
  129.7 1.9 %copy-start.7 = (bf16[8,2,32,1280]{3,2,1,0:T(8,128)(2,1)}, bf16[8,2,32,1280]{3,2,1,0:T(8,128)(2,1)S(1)}, u32[]{:S(2)}) copy-start(bf16[8,2,32,1280]{3,2,1,0:T(8,128)(2,1)S(1)} %constant_dynamic-update-slice_fusion) | copy-start | bytes 3932164
  145.0 16.2 %collective-permute-start.23 = (bf16[512,512]{1,0:T(8,128)(2,1)}, bf16[512,512]{1,0:T(8,128)(2,1)S(1)}, u32[]{:S(2)}, u32[]{:S(2)}) collective-permute-start(bf16[512,512]{1,0:T(8,128)(2,1)} %get-tuple-element.46), channel_id=1, source_target_pairs={{0,4},{4,0},{1,5},{5,1},{2,6},{6,2},{3,7},{7,3},{8,12},{12,8},{9,1... | collective-permute-start | bytes 1572872 | tf_op jit(solution)/shard_map/ppermute | solution.py:50
Sparse Core Ops, SparseCore 0:
  17.3 112.5 all-gather.2
